TPU v7x, 32 devices: a whole 2x2x4 slice. The times are simulated.
32 devices in a mesh: dp: 32 (over z, y, x, core).
Axes of the slice: x: 2, y: 2, z: 4, core: 2. Of those that a mesh axis runs over, the one named last changes fastest.
Arguments:
- img_emb: bfloat16 [16384, 1152], P('dp'), may hold values from -6 to 6
- txt_emb: bfloat16 [16384, 1152], P('dp'), may hold values from -6 to 6
- img_proj: bfloat16 [1152, 1152], replicated, may hold values from -0.1875 to 0.1875
- txt_proj: bfloat16 [1152, 1152], replicated, may hold values from -0.1875 to 0.1875
- log_scale: float32 [1], replicated, may hold values from 1.1 to 2.1
- bias: float32 [1], replicated, may hold values from -3 to -1
Outputs:
- d_img_emb: bfloat16 [16384, 1152], P('dp')
- d_txt_emb: bfloat16 [16384, 1152], P('dp')
- d_img_proj: float32 [1152, 1152], replicated
- d_txt_proj: float32 [1152, 1152], replicated
All inputs are finite; a program needn't handle non-finite values.
Results may differ from a plain program's by a relative error of at most 0.02.
Values may be sent and summed in bfloat16 or wider, within the bound.
No kernel may reach another device: no remote copies, remote signals or barrier semaphores. Data moves between devices by JAX's collectives and lax.ppermute only.
A program may use at most 128 MiB of HBM per device.

v0:
```python
import functools

import jax
import jax.numpy as jnp
from jax import lax
from jax.experimental import pallas as pl
from jax.experimental.pallas import tpu as pltpu
from jax.sharding import PartitionSpec as P

REACH = 3
BF16, F32 = jnp.bfloat16, jnp.float32
TILE = 512
SIDE, IN_PLANE, IN_LINE, SAME, X, Y, Z_LOW, Z_HIGH = range(8)
VMEM = pl.BlockSpec(memory_space=pltpu.VMEM)
SMEM = pl.BlockSpec(memory_space=pltpu.SMEM)
HBM = pl.BlockSpec(memory_space=pltpu.HBM)
ANY = pl.BlockSpec(memory_space=pl.ANY)


def params(mib):
    return pltpu.CompilerParams(vmem_limit_bytes=mib * 1024 * 1024)


def dot_t(left, right):
    return lax.dot_general(left, right, (((1,), (1,)), ((), ())), preferred_element_type=F32)


def dot(left, right):
    return lax.dot_general(left, right, (((1,), (0,)), ((), ())), preferred_element_type=F32)


def shift(value, size, chips):
    pairs = []
    for i in range(size):
        chip, core = i // 2, i % 2
        pairs.append((i, 2 * ((chip + chips(chip, core)) % (size // 2)) + core))
    return lax.ppermute(value, "dp", pairs)


def swap(value, size, mask):
    return lax.ppermute(value, "dp", [(i, i ^ mask) for i in range(size)])


def met_kernel(own_chip, place, *refs):
    sides, projs, (z_one, z_two, emb_v, proj_v, sems) = (refs[:2], refs[2:4]), refs[4:6], refs[6:]
    cut = proj_v.shape[0] // 256 * 128 + 128
    parts = [slice(0, cut), slice(cut, proj_v.shape[0])]
    for side, (embs, proj) in enumerate(zip(sides, projs)):

        @pl.when(place[SIDE] == side)
        def _():
            first = 1 - place[SAME] if own_chip else 0
            copies = [pltpu.make_async_copy(embs[0], emb_v.at[first], sems.at[2])]
            for k, part in enumerate(parts):
                copies.append(
                    pltpu.make_async_copy(proj.at[part, :], proj_v.at[part, :], sems.at[k])
                )
            copies.append(pltpu.make_async_copy(embs[1], emb_v.at[1 - first], sems.at[3]))
            for copy in copies:
                copy.start()
            for copy in copies:
                copy.wait()

    for k, z in enumerate((z_one, z_two)):
        raw = dot(emb_v[k], proj_v[...])
        scale = lax.rsqrt(jnp.sum(raw * raw, axis=1, keepdims=True) + 1e-06)
        z[...] = (raw * scale).astype(BF16)


def met_units(place, text_side, image_side, img_proj, txt_proj, own_chip, mib, name):
    out = jax.ShapeDtypeStruct(text_side[0].shape, BF16)
    return pl.pallas_call(
        functools.partial(met_kernel, own_chip),
        out_shape=(out, out),
        in_specs=[SMEM] + [HBM] * 6,
        out_specs=(VMEM, VMEM),
        scratch_shapes=[
            pltpu.VMEM((2, *out.shape), BF16),
            pltpu.VMEM(img_proj.shape, BF16),
            pltpu.SemaphoreType.DMA((4,)),
        ],
        compiler_params=params(mib),
        name=name,
    )(place, *text_side, *image_side, txt_proj, img_proj)


def second_kernel(place, *refs):
    sides, (unit, inverse, z, weight, emb_t, emb_v, sems) = (refs[:3], refs[3:6]), refs[6:]
    rows = emb_v.shape[1]
    for side in range(2):

        @pl.when(place[SIDE] == side)
        def _():
            copies = [
                pltpu.make_async_copy(src, dst, sems.at[at])
                for at, (src, dst) in enumerate(
                    zip(sides[side], (weight, emb_v.at[1 - place[SAME]], emb_v.at[place[SAME]]))
                )
            ]
            for copy in copies:
                copy.start()
            for copy in copies:
                copy.wait()

    for half in range(2):
        here = slice(half * rows, (half + 1) * rows)
        raw = dot(emb_v[half], weight[...])
        scale = lax.rsqrt(jnp.sum(raw * raw, axis=1, keepdims=True) + 1e-06)
        inverse[here, :] = scale
        units = raw * scale
        unit[here, :] = units
        z[here, :] = units.astype(BF16)
        emb_t[:, here] = emb_v[half].T


def second_units(place, img_emb, txt_emb, img_other, txt_other, img_proj, txt_proj):
    rows, columns = img_emb.shape
    return pl.pallas_call(
        second_kernel,
        out_shape=(
            jax.ShapeDtypeStruct((2 * rows, columns), F32),
            jax.ShapeDtypeStruct((2 * rows, 1), F32),
            jax.ShapeDtypeStruct((2 * rows, columns), BF16),
            jax.ShapeDtypeStruct(img_proj.shape, BF16),
            jax.ShapeDtypeStruct((columns, 2 * rows), BF16),
        ),
        in_specs=[SMEM] + [HBM] * 6,
        out_specs=(VMEM,) * 5,
        scratch_shapes=[
            pltpu.VMEM((2, rows, columns), BF16),
            pltpu.SemaphoreType.DMA((3,)),
        ],
        compiler_params=params(18),
        name="second_units",
    )(place, img_proj, img_emb, img_other, txt_proj, txt_emb, txt_other)


def piece_at(digit, m, height, first=0):
    return pl.ds(pl.multiple_of(first + (digit ^ m) * height, 8), height)


def pick_kernel(at, place, *refs):
    sources, outs, sems = (refs[:2], refs[2:4]), refs[4:6], refs[6]
    for flag in range(2):

        @pl.when(place[at] == flag)
        def _():
            copies = [
                pltpu.make_async_copy(pair[flag], out, sems.at[k])
                for k, (pair, out) in enumerate(zip(sources, outs))
            ]
            for copy in copies:
                copy.start()
            for copy in copies:
                copy.wait()


def pick(place, at, first, second, name):
    return pl.pallas_call(
        functools.partial(pick_kernel, at),
        out_shape=tuple(jax.ShapeDtypeStruct(p[0].shape, p[0].dtype) for p in (first, second)),
        in_specs=[SMEM] + [ANY] * 4,
        out_specs=(ANY, ANY),
        scratch_shapes=[pltpu.SemaphoreType.DMA((2,))],
        compiler_params=params(1),
        name=name,
    )(place, *first, *second)


def pair_term(z, block, scale, bias, diagonal):
    half = dot_t(z, block) * (0.5 * scale) + 0.5 * bias
    coef = 0.5 * jnp.tanh(half) + 0.5
    if diagonal is not None:
        row_at = lax.broadcasted_iota(jnp.int32, coef.shape, 0) + diagonal
        col_at = lax.broadcasted_iota(jnp.int32, coef.shape, 1)
        coef = jnp.where(row_at == col_at, coef - 1.0, coef)
    return dot(coef.astype(BF16), block)


def own_chip_kernel(scale, bias, z, met, met_other, grad):
    step = pl.program_id(0)
    per_block = met.shape[0] // TILE
    here = step * TILE
    near = pair_term(z[...], met[...], scale[0], bias[0], here)
    other = pair_term(z[...], met_other[...], scale[0], bias[0], here - per_block * TILE)
    grad[...] = near + other


def first_phase_kernel(scale, bias, z, one, two, far_own, far_other, grad_in, grad):
    step = pl.program_id(0)
    per_block = one.shape[0] // TILE
    total = grad_in[...] + pair_term(z[...], one[...], scale[0], bias[0], None)
    total = total + pair_term(z[...], two[...], scale[0], bias[0], None)

    @pl.when(step < per_block)
    def _():
        grad[...] = total + pair_term(z[...], far_own[...], scale[0], bias[0], None)

    @pl.when(step >= per_block)
    def _():
        grad[...] = total + pair_term(z[...], far_other[...], scale[0], bias[0], None)


def row_tiles(columns):
    return pl.BlockSpec((TILE, columns), lambda i: (i, 0))


def whole(array):
    return pl.BlockSpec(
        array.shape, lambda i: (0,) * len(array.shape), pipeline_mode=pl.Buffered(1)
    )


def call_tiles(kernel, scale, bias, z, blocks, grads, name, mib):
    rows, columns = z.shape
    return pl.pallas_call(
        kernel,
        grid=(rows // TILE,),
        out_shape=jax.ShapeDtypeStruct((rows, columns), F32),
        in_specs=[SMEM, SMEM, row_tiles(columns)]
        + [whole(b) for b in blocks]
        + [row_tiles(columns)] * len(grads),
        out_specs=row_tiles(columns),
        compiler_params=params(mib),
        name=name,
    )(scale, bias, z, *blocks, *grads)


def last_phase_kernel(
    place, scale, bias, z, one, two, grad_in, unit, inverse, emb_t, du, *rest
):
    half, (du_all, emb_v, sem) = rest[0], rest[1:]
    step = pl.program_id(0)
    fetch = pltpu.make_async_copy(emb_t, emb_v, sem)

    @pl.when(step == 0)
    def _():
        fetch.start()

    grad = grad_in[...] + pair_term(z[...], one[...], scale[0], bias[0], None)
    grad = scale[0] * (grad + pair_term(z[...], two[...], scale[0], bias[0], None))
    units = unit[...]
    inner = jnp.sum(units * grad, axis=1, keepdims=True)
    rounded = ((grad - units * inner) * inverse[...]).astype(BF16)
    du[...] = rounded
    du_all[pl.ds(pl.multiple_of(step * TILE, TILE), TILE), :] = rounded

    @pl.when(step == pl.num_programs(0) - 1)
    def _():
        fetch.wait()
        height = half.shape[0]
        first = emb_v.shape[0] - 2 * height
        rows = piece_at(place[Z_LOW], 1, height, first)
        half[...] = dot(emb_v[rows, :], du_all[...]).astype(BF16)


def last_phase(place, scale, bias, z, one, two, grad, unit, inverse, emb_t):
    rows, columns = z.shape
    half = jax.ShapeDtypeStruct((columns // 6, columns), BF16)
    return pl.pallas_call(
        last_phase_kernel,
        grid=(rows // TILE,),
        out_shape=(jax.ShapeDtypeStruct((rows, columns), BF16), half),
        in_specs=[
            SMEM,
            SMEM,
            SMEM,
            row_tiles(columns),
            whole(one),
            whole(two),
            row_tiles(columns),
            row_tiles(columns),
            row_tiles(1),
            HBM,
        ],
        out_specs=(row_tiles(columns), whole(half)),
        scratch_shapes=[
            pltpu.VMEM((rows, columns), BF16),
            pltpu.VMEM(emb_t.shape, BF16),
            pltpu.SemaphoreType.DMA,
        ],
        compiler_params=params(28),
        name="last_phase",
    )(place, scale, bias, z, one, two, grad, unit, inverse, emb_t)


def other_parts_kernel(place, emb_t, du, keep_b, *pieces):
    height = keep_b.shape[0]
    for m, out in enumerate(pieces):
        rows = piece_at(place[IN_PLANE], m, height)
        out[...] = dot(emb_t[rows, :], du[...]).astype(out.dtype)
    rows = piece_at(place[Z_LOW], 0, height, emb_t.shape[0] - 2 * height)
    keep_b[...] = dot(emb_t[rows, :], du[...])


def other_parts(place, emb_t, du):
    shape = (emb_t.shape[0] // 6, emb_t.shape[0])
    kinds = [F32, F32, BF16, BF16, BF16]
    return pl.pallas_call(
        other_parts_kernel,
        out_shape=tuple(jax.ShapeDtypeStruct(shape, kind) for kind in kinds),
        in_specs=[SMEM] + [VMEM] * 2,
        out_specs=(VMEM,) * 5,
        compiler_params=params(8),
        name="other_parts",
    )(place, emb_t, du)


def rows_back_kernel(place, du, weight, own, other):
    back = dot_t(du[...], weight[...]).astype(BF16)
    mine = pl.program_id(0) == 1 - place[SAME]

    @pl.when(mine)
    def _():
        own[...] = back

    @pl.when(jnp.logical_not(mine))
    def _():
        other[...] = back


def rows_back(place, du, weight):
    rows, columns = du.shape
    out = jax.ShapeDtypeStruct((TILE, columns), BF16)
    return pl.pallas_call(
        rows_back_kernel,
        grid=(rows // TILE,),
        out_shape=(out, out),
        in_specs=[SMEM, row_tiles(columns), whole(weight)],
        out_specs=(whole(out), whole(out)),
        compiler_params=params(8),
        name="rows_back",
    )(place, du, weight)


def summed(refs):
    one, two, three, four = (ref[...].astype(F32) for ref in refs)
    return (one + two) + (three + four)


def small_call(kernel, place, arrays, outs, scratch, mib, name):
    return pl.pallas_call(
        kernel,
        out_shape=tuple(jax.ShapeDtypeStruct(shape, kind) for shape, kind in outs),
        in_specs=[SMEM] + [VMEM] * len(arrays),
        out_specs=(VMEM,) * len(outs),
        scratch_shapes=[pltpu.VMEM(shape, F32) for shape in scratch],
        compiler_params=params(mib),
        name=name,
    )(place, *arrays)


def add_split_kernel(place, *refs):
    total = refs[8]
    total[...] = summed(refs[:4])
    for m, out in enumerate(refs[4:8]):
        out[...] = total[piece_at(place[IN_LINE], m, out.shape[0]), :].astype(out.dtype)


def add_split(place, parts, name):
    rows, columns = parts[0].shape
    outs = [((rows // 4, columns), F32 if m == 0 else BF16) for m in range(4)]
    return small_call(add_split_kernel, place, parts, outs, [(rows, columns)], 4, name)


def add_all_kernel(place, *refs):
    refs[4][...] = summed(refs[:4]).astype(BF16)


def add_all(place, parts, name):
    return small_call(add_all_kernel, place, parts, [(parts[0].shape, BF16)], [], 2, name)[0]


def join_four_kernel(digit, place, *refs):
    out, total = refs[4:]
    for m, piece in enumerate(refs[:4]):
        total[piece_at(place[digit], m, piece.shape[0]), :] = piece[...].astype(F32)
    out[...] = total[...].astype(BF16)


def join_four(place, digit, parts, name):
    shape = (4 * parts[0].shape[0], parts[0].shape[1])
    kernel = functools.partial(join_four_kernel, digit)
    return small_call(kernel, place, parts, [(shape, BF16)], [shape], 7, name)[0]


def add_halve_kernel(bit, place, keep, got, mine, give, total):
    total[...] = keep[...] + got[...].astype(F32)
    for m, out in enumerate((mine, give)):
        out[...] = total[piece_at(place[bit], m, out.shape[0]), :].astype(out.dtype)


def add_halve(place, bit, keep, got, name):
    rows, columns = keep.shape
    outs = [((rows // 2, columns), kind) for kind in (F32, BF16)]
    kernel = functools.partial(add_halve_kernel, bit)
    return small_call(kernel, place, [keep, got], outs, [keep.shape], 3, name)


def add_two_kernel(place, keep, got, out):
    out[...] = (keep[...] + got[...].astype(F32)).astype(BF16)


def add_two(place, keep, got, name):
    return small_call(add_two_kernel, place, [keep, got], [(keep.shape, BF16)], [], 2, name)[0]


def join_two_kernel(bit, place, mine, got, out, total):
    for m, piece in enumerate((mine, got)):
        total[piece_at(place[bit], m, piece.shape[0]), :] = piece[...].astype(F32)
    out[...] = total[...].astype(BF16)


def join_two(place, bit, mine, got, name):
    shape = (2 * mine.shape[0], mine.shape[1])
    kernel = functools.partial(join_two_kernel, bit)
    return small_call(kernel, place, [mine, got], [(shape, BF16)], [shape], 5, name)[0]


def join_all_kernel(place, *refs):
    out = refs[6]
    for m, piece in enumerate(refs[:4]):
        out[piece_at(place[IN_PLANE], m, piece.shape[0]), :] = piece[...]
    height = refs[4].shape[0]
    for m, piece in enumerate(refs[4:6]):
        out[piece_at(place[Z_LOW], m, height, out.shape[0] - 2 * height), :] = piece[...]


def join_all(place, parts_a, parts_b):
    columns = parts_b[0].shape[1]
    arrays = [*parts_a, *parts_b]
    outs = [((columns, columns), BF16)]
    return small_call(join_all_kernel, place, arrays, outs, [], 3, "join_all")[0]


def widen_kernel(own, place, weight, *refs):
    img_out, txt_out, wide, sems = refs[-4:]
    count = sems.shape[0]
    height = weight.shape[0] // count
    for side, out in enumerate((img_out, txt_out)):

        @pl.when((place[SIDE] == side) == own)
        def _():
            copies = []
            for k in range(count):
                part = slice(k * height, (k + 1) * height)
                wide[part, :] = weight[part, :].astype(F32)
                copies.append(
                    pltpu.make_async_copy(wide.at[part, :], out.at[part, :], sems.at[k])
                )
                copies[-1].start()
            for copy in copies:
                copy.wait()


def widen(place, weight, own, outs, name):
    out = jax.ShapeDtypeStruct(weight.shape, F32)
    return pl.pallas_call(
        functools.partial(widen_kernel, own),
        out_shape=(out, out),
        in_specs=[SMEM, VMEM] + [ANY] * len(outs),
        out_specs=(ANY, ANY),
        scratch_shapes=[pltpu.VMEM(weight.shape, F32), pltpu.SemaphoreType.DMA((9,))],
        input_output_aliases={2: 0, 3: 1} if outs else {},
        compiler_params=params(9),
        name=name,
    )(place, weight, *outs)


def body(img_emb, txt_emb, img_proj, txt_proj, log_scale, bias):
    size = lax.axis_size("dp")
    columns = img_emb.shape[1]
    scale = jnp.exp(log_scale)
    here = lax.axis_index("dp").astype(jnp.int32)
    side, chip = here % 2, here // 2
    bits = [(chip // n) % 2 for n in (1, 2, 4, 8)]
    place = jnp.stack([side, chip % 4, (chip // 4) % 4, (chip + side + 1) % 2, *bits])
    place, scale = lax.optimization_barrier((place, scale))

    pair = lambda value: swap(value, size, 2)
    far_as_d = lambda value: shift(value, size, lambda chip, core: -2 if chip % 2 else 2)

    def raw_target(to_far, to_pair):
        pairs = []
        for i in range(size):
            chip, core = i // 2, i % 2
            if core == chip % 2:
                pairs.append((i, 2 * ((chip + 2 if core else chip - 2) % (size // 2)) + to_far))
            else:
                pairs.append((i, 2 * (chip ^ 1) + to_pair))
        return pairs

    same = place[SAME] == 1
    raw_one = jnp.where(same, txt_emb, img_emb)
    raw_two = jnp.where(same, img_emb, txt_emb)
    got_one = lax.ppermute(raw_one, "dp", raw_target(0, 1))
    got_two = lax.ppermute(raw_two, "dp", raw_target(1, 0))
    img_other, txt_other, _ = lax.optimization_barrier(
        (swap(img_emb, size, 1), swap(txt_emb, size, 1), raw_one)
    )
    met_s, met_d = met_units(
        place,
        (txt_emb, txt_other),
        (img_emb, img_other),
        img_proj,
        txt_proj,
        True,
        58,
        "own_met",
    )
    img_emb, txt_emb, img_other, txt_other, _ = lax.optimization_barrier(
        (img_emb, txt_emb, img_other, txt_other, met_s)
    )
    unit, inverse, z, weight, emb_t = second_units(
        place, img_emb, txt_emb, img_other, txt_other, img_proj, txt_proj
    )
    got_one, got_two, sent_s, sent_d, _ = lax.optimization_barrier(
        (got_one, got_two, met_s, met_d, emb_t)
    )
    pair_s, far_d = pair(sent_s), far_as_d(sent_d)
    pair_d, far_s = met_units(
        place,
        (got_two, got_one),
        (got_one, got_two),
        img_proj,
        txt_proj,
        False,
        14,
        "raw_met",
    )
    relay_far, relay_pair = pair(far_s), far_as_d(pair_d)
    z, _ = lax.optimization_barrier((z, (pair_d, far_s)))
    grad = call_tiles(own_chip_kernel, scale, bias, z, (met_s, met_d), (), "own_chip", 8)
    pair_s, far_d, _ = lax.optimization_barrier((pair_s, far_d, grad))
    grad = call_tiles(
        first_phase_kernel,
        scale,
        bias,
        z,
        (pair_s, pair_d, far_d, far_s),
        (grad,),
        "first_phase",
        12,
    )

    du, give_b = last_phase(
        place, scale, bias, z, relay_far, relay_pair, grad, unit, inverse, emb_t
    )

    def exchange(sends, masks):
        return [swap(s, size, m) for s, m in zip(sends, masks)]

    plane_masks, line_masks = (2, 4, 6), (8, 16, 24)
    x_bit, y_bit, low_bit, high_bit = (X, 2), (Y, 4), (Z_LOW, 8), (Z_HIGH, 16)

    def halve(keep, got, bit, name):
        keep, give = add_halve(place, bit[0], keep, got, name)
        return keep, swap(give, size, bit[1]), give

    def gather(mine, bit):
        return mine, swap(mine, size, bit[1])

    together = lax.optimization_barrier
    got_b = swap(give_b, size, low_bit[1])
    keep_b, *pieces = other_parts(place, emb_t, du)
    parts_a = [pieces[0], *exchange(pieces[1:], plane_masks)]
    keep_b, got_b, give_b = halve(keep_b, got_b, high_bit, "b_high")
    du, _ = together((du, give_b))
    d_emb, d_emb_send = rows_back(place, du, weight)
    parts_a, got_b, d_emb_send = together((parts_a, got_b, d_emb_send))
    d_emb_other = swap(d_emb_send, size, 1)
    pieces = add_split(place, parts_a, "a_split")
    parts_a = [pieces[0], *exchange(pieces[:0:-1], line_masks[::-1])]
    keep_b, got_b, _ = halve(keep_b, got_b, x_bit, "b_x")
    d_img_emb, d_txt_emb = pick(
        place, SIDE, (d_emb, d_emb_other), (d_emb_other, d_emb), "rows_pick"
    )
    keep_b, got_b, give_b = halve(keep_b, got_b, y_bit, "b_y")
    parts_a, d_img_emb, d_txt_emb, _ = together((parts_a, d_img_emb, d_txt_emb, give_b))

    parts_a, got_b = together((parts_a, got_b))
    shard_a = add_all(place, parts_a, "a_last")
    shard_b = add_two(place, keep_b, got_b, "b_last")
    if size > 32:
        groups = [[i for i in range(size) if i % 32 == k] for k in range(32)]
        shard_a, shard_b = lax.psum((shard_a, shard_b), "dp", axis_index_groups=groups)
    parts_a = [shard_a, *exchange([shard_a] * 3, line_masks)]
    shard_b = join_two(place, y_bit[0], *gather(shard_b, y_bit), "b_join_y")
    got_b = swap(shard_b, size, x_bit[1])
    parts_a, _ = together((parts_a, shard_b))

    parts_a, got_b = together((parts_a, got_b))
    piece_a = join_four(place, IN_LINE, parts_a, "a_join")
    parts_a = [piece_a, *exchange([piece_a] * 3, plane_masks)]
    shard_b = join_two(place, x_bit[0], shard_b, got_b, "b_join_x")
    shard_b = join_two(place, high_bit[0], *gather(shard_b, high_bit), "b_join_high")
    got_b = swap(shard_b, size, low_bit[1])
    parts_a, got_b = together((parts_a, got_b))

    d_weight = join_all(place, parts_a, (shard_b, got_b))
    d_weight_other = swap(d_weight, size, 1)
    outs = widen(place, d_weight, True, (), "widen_own")
    d_img_proj, d_txt_proj = widen(place, d_weight_other, False, outs, "widen_other")
    return (d_img_emb, d_txt_emb, d_img_proj, d_txt_proj)


def solution(mesh):
    return jax.shard_map(
        body,
        mesh=mesh,
        in_specs=(P("dp", None), P("dp", None), P(), P(), P(), P()),
        out_specs=(P("dp", None), P("dp", None), P(), P()),
        check_vma=False,
    )
```

profile of v0, /device:TPU:0, one launch (start us, length us, event | category | flops | bytes accessed | tf_op | source)
XLA Modules:
  0.0 194.0 jit_solution(4878486358513818308)
XLA Ops:
  3.3 3.2 %broadcast_select_fusion = (bf16[512,1152]{1,0:T(8,128)(2,1)}, bf16[512,1152]{1,0:T(8,128)(2,1)}) fusion(bf16[512,1152]{1,0:T(8,128)(2,1)} %refs_1_, bf16[512,1152]{1,0:T(8,128)(2,1)} %refs_4_.3, pred[]{:T(512)} %bitcast.8), kind=kLoop, calls=%fused_computation | loop fusion | flops 1179648 | bytes 4718593 | tf_op jit(solution)/shard_map/jit(_where)/select_n | solution.py:495
  6.5 6.0 %collective-permute-start.2 = (bf16[512,1152]{1,0:T(8,128)(2,1)}, bf16[512,1152]{1,0:T(8,128)(2,1)}, u32[]{:S(2)}, u32[]{:S(2)}) collective-permute-start(bf16[512,1152]{1,0:T(8,128)(2,1)} %get-tuple-element.167), channel_id=1, source_target_pairs={{0,28},{1,3},{2,1},{3,6},{4,0},{5,7},{6,5},{7,10},{8,4},{9,11},{10... | collective-permute-start | bytes 3538952 | tf_op jit(solution)/shard_map/ppermute | solution.py:496
  12.5 0.9 collective-permute-start.3
  13.4 1.0 copy-done.4
  14.4 8.3 %own_met.1 = (bf16[512,1152]{1,0:T(8,128)(2,1)}, bf16[512,1152]{1,0:T(8,128)(2,1)}) custom-call(s32[8]{0:T(128)} %copy-done.8, bf16[512,1152]{1,0:T(8,128)(2,1)} %refs_4_.3, bf16[512,1152]{1,0:T(8,128)(2,1)} %collective-permute-done.1.refs_1_.refs_5_, bf16[512,1152]{1,0:T(8,128)(2,1)} %refs_1_, bf16[512,1152]{1,0:T(8,128)(2,1)} %copy-done.4, ...), custom_call_target="tpu_custom_call" | custom-call | tf_op jit(solution)/shard_map/own_met/pallas_call | solution.py:72
  22.8 1.3 copy-done.2
  24.1 1.3 copy-done.3
  25.3 1.3 copy-done.5
  26.6 5.3 %second_units.1 = (f32[1024,1152]{1,0:T(8,128)S(1)}, f32[1024,1]{1,0:T(8,128)S(1)}, bf16[1024,1152]{1,0:T(8,128)(2,1)S(1)}, bf16[1152,1152]{1,0:T(8,128)(2,1)S(1)}, bf16[1152,1024]{1,0:T(8,128)(2,1)S(1)}) custom-call(s32[8]{0:T(128)S(1)} %copy-done.9, bf16[1152,1152]{1,0:T(8,128)(2,1)S(1)} %copy-done, bf16[512,1152]{1,0:T(8,128)(2,1)S(1)} %copy-done.2, ...), custom_call_target="tpu_custom_call" | custom-call | tf_op jit(solution)/shard_map/second_units/pallas_call | solution.py:118
  31.9 7.2 %collective-permute-done.3.refs_0_.refs_3_ = bf16[512,1152]{1,0:T(8,128)(2,1)} collective-permute-done((bf16[512,1152]{1,0:T(8,128)(2,1)}, bf16[512,1152]{1,0:T(8,128)(2,1)}, u32[]{:S(2)}, u32[]{:S(2)}) %collective-permute-start.3) | collective-permute-done | bytes 1179680 | tf_op jit(solution)/shard_map/ppermute | solution.py:497
  39.3 6.2 %raw_met.1 = (bf16[512,1152]{1,0:T(8,128)(2,1)S(1)}, bf16[512,1152]{1,0:T(8,128)(2,1)S(1)}) custom-call(s32[8]{0:T(128)S(1)} %copy-done.9, bf16[512,1152]{1,0:T(8,128)(2,1)} %collective-permute-done.3.refs_0_.refs_3_, bf16[512,1152]{1,0:T(8,128)(2,1)} %collective-permute-done.2.refs_1_.refs_2_, bf16[512,1152]{1,0:T(8,128)(2,1)} %collective-permute-done.2.refs_1_.refs_2_, ...), custom_call_target="tpu_custom_call" | custom-call | tf_op jit(solution)/shard_map/raw_met/pallas_call | solution.py:72
  45.4 4.2 %collective-permute-start.4 = (bf16[512,1152]{1,0:T(8,128)(2,1)S(1)}, bf16[512,1152]{1,0:T(8,128)(2,1)S(1)}, u32[]{:S(2)}, u32[]{:S(2)}) collective-permute-start(bf16[512,1152]{1,0:T(8,128)(2,1)S(1)} %get-tuple-element.100.far_other), channel_id=1, source_target_pairs={{0,2},{1,3},{2,0},{3,1},{4,6},{5,7},{6,4},{7,5},{8,10},{9,11},{10,... | collective-permute-start | bytes 3538952 | tf_op jit(solution)/shard_map/ppermute | solution.py:41
  50.3 6.9 %own_chip.1.grad_in = f32[1024,1152]{1,0:T(8,128)S(1)} custom-call(f32[1]{0:T(128)S(6)} %exp.3.scale, f32[1]{0:T(128)S(6)} %copy.15.bias, bf16[1024,1152]{1,0:T(8,128)(2,1)S(1)} %get-tuple-element.101.z, bf16[512,1152]{1,0:T(8,128)(2,1)S(1)} %copy-done.7, bf16[512,1152]{1,0:T(8,128)(2,1)S(1)} %copy-done.6), custom_call_target="tpu_custom_call" | custom-call | tf_op jit(solution)/shard_map/own_chip/pallas_call | solution.py:216
  57.2 10.9 %collective-permute-done.6.one = bf16[512,1152]{1,0:T(8,128)(2,1)S(1)} collective-permute-done((bf16[512,1152]{1,0:T(8,128)(2,1)S(1)}, bf16[512,1152]{1,0:T(8,128)(2,1)S(1)}, u32[]{:S(2)}, u32[]{:S(2)}) %collective-permute-start.6) | collective-permute-done | bytes 1179680 | tf_op jit(solution)/shard_map/ppermute | solution.py:41
  68.1 2.6 %collective-permute-done.7.far_own = bf16[512,1152]{1,0:T(8,128)(2,1)S(1)} collective-permute-done((bf16[512,1152]{1,0:T(8,128)(2,1)S(1)}, bf16[512,1152]{1,0:T(8,128)(2,1)S(1)}, u32[]{:S(2)}, u32[]{:S(2)}) %collective-permute-start.7) | collective-permute-done | bytes 1179680 | tf_op jit(solution)/shard_map/ppermute | solution.py:37
  70.7 10.0 %first_phase.1.grad_in = f32[1024,1152]{1,0:T(8,128)S(1)} custom-call(f32[1]{0:T(128)S(6)} %exp.3.scale, f32[1]{0:T(128)S(6)} %copy.15.bias, bf16[1024,1152]{1,0:T(8,128)(2,1)S(1)} %get-tuple-element.101.z, bf16[512,1152]{1,0:T(8,128)(2,1)S(1)} %collective-permute-done.6.one, bf16[512,1152]{1,0:T(8,128)(2,1)S(1)} %get-tuple-element.99.two, ...), custom_call_target="tpu_custom_call" | custom-call | tf_op jit(solution)/shard_map/first_phase/pallas_call | solution.py:216
  80.7 11.3 %collective-permute-done.4.one = bf16[512,1152]{1,0:T(8,128)(2,1)S(1)} collective-permute-done((bf16[512,1152]{1,0:T(8,128)(2,1)S(1)}, bf16[512,1152]{1,0:T(8,128)(2,1)S(1)}, u32[]{:S(2)}, u32[]{:S(2)}) %collective-permute-start.4) | collective-permute-done | bytes 1179680 | tf_op jit(solution)/shard_map/ppermute | solution.py:41
  92.0 4.0 %collective-permute-done.5.two = bf16[512,1152]{1,0:T(8,128)(2,1)S(1)} collective-permute-done((bf16[512,1152]{1,0:T(8,128)(2,1)S(1)}, bf16[512,1152]{1,0:T(8,128)(2,1)S(1)}, u32[]{:S(2)}, u32[]{:S(2)}) %collective-permute-start.5) | collective-permute-done | bytes 1179680 | tf_op jit(solution)/shard_map/ppermute | solution.py:37
  96.0 9.5 %last_phase.1 = (bf16[1024,1152]{1,0:T(8,128)(2,1)S(1)}, bf16[192,1152]{1,0:T(8,128)(2,1)S(1)}) custom-call(s32[8]{0:T(128)S(1)} %copy-done.9, f32[1]{0:T(128)S(6)} %exp.3.scale, f32[1]{0:T(128)S(6)} %copy.15.bias, bf16[1024,1152]{1,0:T(8,128)(2,1)S(1)} %get-tuple-element.101.z, bf16[512,1152]{1,0:T(8,128)(2,1)S(1)} %collective-permute-done.4.one, ...), custom_call_target="tpu_custom_call" | custom-call | tf_op jit(solution)/shard_map/last_phase/pallas_call | solution.py:260
  105.6 3.3 %other_parts.1 = (f32[192,1152]{1,0:T(8,128)S(1)}, f32[192,1152]{1,0:T(8,128)S(1)}, bf16[192,1152]{1,0:T(8,128)(2,1)S(1)}, bf16[192,1152]{1,0:T(8,128)(2,1)S(1)}, bf16[192,1152]{1,0:T(8,128)(2,1)S(1)}) custom-call(s32[8]{0:T(128)S(1)} %copy-done.9, bf16[1152,1024]{1,0:T(8,128)(2,1)S(1)} %get-tuple-element.93.emb_t, bf16[1024,1152]{1,0:T(8,128)(2,1)S(1)} %get-tuple-element.116.du), custom_call_target="tpu_custom_call" | custom-call | tf_op jit(solution)/shard_map/other_parts/pallas_call | solution.py:299
  109.1 3.3 %collective-permute-start.9 = (bf16[192,1152]{1,0:T(8,128)(2,1)S(1)}, bf16[192,1152]{1,0:T(8,128)(2,1)S(1)}, u32[]{:S(2)}, u32[]{:S(2)}) collective-permute-start(bf16[192,1152]{1,0:T(8,128)(2,1)S(1)} %get-tuple-element.111), channel_id=1, source_target_pairs={{0,4},{1,5},{2,6},{3,7},{4,0},{5,1},{6,2},{7,3},{8,12},{9,13},{10,... | collective-permute-start | bytes 1327112 | tf_op jit(solution)/shard_map/ppermute | solution.py:41
  112.4 5.3 %collective-permute-done.11.got = bf16[192,1152]{1,0:T(8,128)(2,1)S(1)} collective-permute-done((bf16[192,1152]{1,0:T(8,128)(2,1)S(1)}, bf16[192,1152]{1,0:T(8,128)(2,1)S(1)}, u32[]{:S(2)}, u32[]{:S(2)}) %collective-permute-start.11) | collective-permute-done | bytes 442400 | tf_op jit(solution)/shard_map/ppermute | solution.py:41
  117.8 0.7 b_high.1
  118.5 4.6 %rows_back.1 = (bf16[512,1152]{1,0:T(8,128)(2,1)S(1)}, bf16[512,1152]{1,0:T(8,128)(2,1)S(1)}) custom-call(s32[8]{0:T(128)S(1)} %copy-done.9, bf16[1024,1152]{1,0:T(8,128)(2,1)S(1)} %get-tuple-element.116.du, bf16[1152,1152]{1,0:T(8,128)(2,1)S(1)} %get-tuple-element.117.weight), custom_call_target="tpu_custom_call" | custom-call | tf_op jit(solution)/shard_map/rows_back/pallas_call | solution.py:325
  123.1 5.3 %collective-permute-done.8.refs_1_ = bf16[192,1152]{1,0:T(8,128)(2,1)S(1)} collective-permute-done((bf16[192,1152]{1,0:T(8,128)(2,1)S(1)}, bf16[192,1152]{1,0:T(8,128)(2,1)S(1)}, u32[]{:S(2)}, u32[]{:S(2)}) %collective-permute-start.8) | collective-permute-done | bytes 442400 | tf_op jit(solution)/shard_map/ppermute | solution.py:41
  128.4 3.1 %collective-permute-done.9.refs_2_ = bf16[192,1152]{1,0:T(8,128)(2,1)S(1)} collective-permute-done((bf16[192,1152]{1,0:T(8,128)(2,1)S(1)}, bf16[192,1152]{1,0:T(8,128)(2,1)S(1)}, u32[]{:S(2)}, u32[]{:S(2)}) %collective-permute-start.9) | collective-permute-done | bytes 442400 | tf_op jit(solution)/shard_map/ppermute | solution.py:41
  132.2 1.0 a_split.1
  133.2 2.5 %collective-permute-start.13 = (bf16[48,1152]{1,0:T(8,128)(2,1)S(1)}, bf16[48,1152]{1,0:T(8,128)(2,1)S(1)}, u32[]{:S(2)}, u32[]{:S(2)}) collective-permute-start(bf16[48,1152]{1,0:T(8,128)(2,1)S(1)} %get-tuple-element.124), channel_id=1, source_target_pairs={{0,24},{1,25},{2,26},{3,27},{4,28},{5,29},{6,30},{7,31},{8,16},{9,... | collective-permute-start | bytes 331784 | tf_op jit(solution)/shard_map/ppermute | solution.py:41
  135.7 0.8 collective-permute-start.14
  136.4 1.2 collective-permute-start.15
  138.2 0.9 collective-permute-start.18
  139.1 2.0 %rows_pick.1 = (bf16[512,1152]{1,0:T(8,128)(2,1)}, bf16[512,1152]{1,0:T(8,128)(2,1)}) custom-call(s32[8]{0:T(128)S(1)} %copy-done.9, bf16[512,1152]{1,0:T(8,128)(2,1)S(1)} %get-tuple-element.127.refs_0_.refs_3_, bf16[512,1152]{1,0:T(8,128)(2,1)S(1)} %collective-permute-done.16.refs_1_.refs_2_, bf16[512,1152]{1,0:T(8,128)(2,1)S(1)} %collective-permute-done.16.refs_1_.refs_2_, ...), custom_call_target="tpu_custom_call" | custom-call | tf_op jit(solution)/shard_map/rows_pick/pallas_call | solution.py:159
  141.1 5.9 %collective-permute-done.14.refs_2_ = bf16[48,1152]{1,0:T(8,128)(2,1)S(1)} collective-permute-done((bf16[48,1152]{1,0:T(8,128)(2,1)S(1)}, bf16[48,1152]{1,0:T(8,128)(2,1)S(1)}, u32[]{:S(2)}, u32[]{:S(2)}) %collective-permute-start.14) | collective-permute-done | bytes 110624 | tf_op jit(solution)/shard_map/ppermute | solution.py:41
  147.6 1.3 collective-permute-start.22
  149.5 3.3 %collective-permute-start.20 = (bf16[48,1152]{1,0:T(8,128)(2,1)S(1)}, bf16[48,1152]{1,0:T(8,128)(2,1)S(1)}, u32[]{:S(2)}, u32[]{:S(2)}) collective-permute-start(bf16[48,1152]{1,0:T(8,128)(2,1)S(1)} %a_last.1.refs_0_), channel_id=1, source_target_pairs={{0,16},{1,17},{2,18},{3,19},{4,20},{5,21},{6,22},{7,23},{8,24},{9,... | collective-permute-start | bytes 331784 | tf_op jit(solution)/shard_map/ppermute | solution.py:41
  152.8 1.1 collective-permute-start.21
  154.5 1.2 collective-permute-start.23
  155.8 5.4 %collective-permute-done.20.refs_2_ = bf16[48,1152]{1,0:T(8,128)(2,1)S(1)} collective-permute-done((bf16[48,1152]{1,0:T(8,128)(2,1)S(1)}, bf16[48,1152]{1,0:T(8,128)(2,1)S(1)}, u32[]{:S(2)}, u32[]{:S(2)}) %collective-permute-start.20) | collective-permute-done | bytes 110624 | tf_op jit(solution)/shard_map/ppermute | solution.py:41
  161.8 2.6 %collective-permute-start.27 = (bf16[96,1152]{1,0:T(8,128)(2,1)S(1)}, bf16[96,1152]{1,0:T(8,128)(2,1)S(1)}, u32[]{:S(2)}, u32[]{:S(2)}) collective-permute-start(bf16[96,1152]{1,0:T(8,128)(2,1)S(1)} %b_join_x.1.mine), channel_id=1, source_target_pairs={{0,16},{1,17},{2,18},{3,19},{4,20},{5,21},{6,22},{7,23},{8,24},{9,... | collective-permute-start | bytes 663560 | tf_op jit(solution)/shard_map/ppermute | solution.py:41
  166.1 2.5 %collective-permute-start.26 = (bf16[192,1152]{1,0:T(8,128)(2,1)S(1)}, bf16[192,1152]{1,0:T(8,128)(2,1)S(1)}, u32[]{:S(2)}, u32[]{:S(2)}) collective-permute-start(bf16[192,1152]{1,0:T(8,128)(2,1)S(1)} %a_join.1.refs_0_), channel_id=1, source_target_pairs={{0,6},{1,7},{2,4},{3,5},{4,2},{5,3},{6,0},{7,1},{8,14},{9,15},{10,... | collective-permute-start | bytes 1327112 | tf_op jit(solution)/shard_map/ppermute | solution.py:41
  168.7 4.6 %collective-permute-done.27.got = bf16[96,1152]{1,0:T(8,128)(2,1)S(1)} collective-permute-done((bf16[96,1152]{1,0:T(8,128)(2,1)S(1)}, bf16[96,1152]{1,0:T(8,128)(2,1)S(1)}, u32[]{:S(2)}, u32[]{:S(2)}) %collective-permute-start.27) | collective-permute-done | bytes 221216 | tf_op jit(solution)/shard_map/ppermute | solution.py:41
  173.3 0.6 b_join_high.1.refs_4_
  174.0 4.3 %collective-permute-done.24.refs_1_ = bf16[192,1152]{1,0:T(8,128)(2,1)S(1)} collective-permute-done((bf16[192,1152]{1,0:T(8,128)(2,1)S(1)}, bf16[192,1152]{1,0:T(8,128)(2,1)S(1)}, u32[]{:S(2)}, u32[]{:S(2)}) %collective-permute-start.24) | collective-permute-done | bytes 442400 | tf_op jit(solution)/shard_map/ppermute | solution.py:41
  178.3 6.7 %collective-permute-done.25.refs_2_ = bf16[192,1152]{1,0:T(8,128)(2,1)S(1)} collective-permute-done((bf16[192,1152]{1,0:T(8,128)(2,1)S(1)}, bf16[192,1152]{1,0:T(8,128)(2,1)S(1)}, u32[]{:S(2)}, u32[]{:S(2)}) %collective-permute-start.25) | collective-permute-done | bytes 442400 | tf_op jit(solution)/shard_map/ppermute | solution.py:41
  185.0 0.7 join_all.1.weight
  185.8 3.0 %widen_own.1 = (f32[1152,1152]{1,0:T(8,128)}, f32[1152,1152]{1,0:T(8,128)}) custom-call(s32[8]{0:T(128)S(1)} %copy-done.9, bf16[1152,1152]{1,0:T(8,128)(2,1)S(1)} %join_all.1.weight), custom_call_target="tpu_custom_call" | custom-call | tf_op jit(solution)/shard_map/widen_own/pallas_call | solution.py:458
  188.9 1.9 collective-permute-done.29.weight
  190.8 3.0 %widen_other.1 = (f32[1152,1152]{1,0:T(8,128)}, f32[1152,1152]{1,0:T(8,128)}) custom-call(s32[8]{0:T(128)S(1)} %copy-done.9, bf16[1152,1152]{1,0:T(8,128)(2,1)S(1)} %collective-permute-done.29.weight, f32[1152,1152]{1,0:T(8,128)} %get-tuple-element.162.refs_0_, f32[1152,1152]{1,0:T(8,128)} %get-tuple-element.163.refs_1_), custom_call_target="tpu_custom_call", output_to_operand_aliasing={{0}: (2, {}), {1}: (3, {})} | custom-call | tf_op jit(solution)/shard_map/widen_other/pallas_call | solution.py:458
  (57 shorter events, 7.4 us)
Async XLA Ops:
  0.6 12.8 %collective-permute-start = (bf16[512,1152]{1,0:T(8,128)(2,1)}, bf16[512,1152]{1,0:T(8,128)(2,1)S(1)}, u32[]{:S(2)}, u32[]{:S(2)}) collective-permute-start(bf16[512,1152]{1,0:T(8,128)(2,1)} %refs_1_), channel_id=1, source_target_pairs={{0,1},{1,0},{2,3},{3,2},{4,5},{5,4},{6,7},{7,6},{8,9},{9,8},{10,11... | collective-permute-start | bytes 3538952 | tf_op jit(solution)/shard_map/ppermute | solution.py:41
  1.1 13.3 %collective-permute-start.1 = (bf16[512,1152]{1,0:T(8,128)(2,1)}, bf16[512,1152]{1,0:T(8,128)(2,1)}, u32[]{:S(2)}, u32[]{:S(2)}) collective-permute-start(bf16[512,1152]{1,0:T(8,128)(2,1)} %refs_4_.3), channel_id=1, source_target_pairs={{0,1},{1,0},{2,3},{3,2},{4,5},{5,4},{6,7},{7,6},{8,9},{9,8},{10,11... | collective-permute-start | bytes 3538952 | tf_op jit(solution)/shard_map/ppermute | solution.py:41
  2.0 4.5 %copy-start.8 = (s32[8]{0:T(128)}, s32[8]{0:T(128)S(1)}, u32[]{:S(2)}) copy-start(s32[8]{0:T(128)S(1)} %stack.35.place) | copy-start | bytes 100
  6.5 25.4 %collective-permute-start.2 = (bf16[512,1152]{1,0:T(8,128)(2,1)}, bf16[512,1152]{1,0:T(8,128)(2,1)}, u32[]{:S(2)}, u32[]{:S(2)}) collective-permute-start(bf16[512,1152]{1,0:T(8,128)(2,1)} %get-tuple-element.167), channel_id=1, source_target_pairs={{0,28},{1,3},{2,1},{3,6},{4,0},{5,7},{6,5},{7,10},{8,4},{9,11},{10... | collective-permute-start | bytes 3538952 | tf_op jit(solution)/shard_map/ppermute | solution.py:496
  12.5 10.3 %copy-start.9 = (s32[8]{0:T(128)S(1)}, s32[8]{0:T(128)}, u32[]{:S(2)}) copy-start(s32[8]{0:T(128)} %copy-done.8) | copy-start | bytes 100
  12.5 26.7 %collective-permute-start.3 = (bf16[512,1152]{1,0:T(8,128)(2,1)}, bf16[512,1152]{1,0:T(8,128)(2,1)}, u32[]{:S(2)}, u32[]{:S(2)}) collective-permute-start(bf16[512,1152]{1,0:T(8,128)(2,1)} %get-tuple-element.166), channel_id=1, source_target_pairs={{0,29},{1,2},{2,0},{3,7},{4,1},{5,6},{6,4},{7,11},{8,5},{9,10},{10... | collective-permute-start | bytes 3538952 | tf_op jit(solution)/shard_map/ppermute | solution.py:497
  13.4 1.0 copy-start.4
  14.4 8.4 %copy-start = (bf16[1152,1152]{1,0:T(8,128)(2,1)S(1)}, bf16[1152,1152]{1,0:T(8,128)(2,1)}, u32[]{:S(2)}) copy-start(bf16[1152,1152]{1,0:T(8,128)(2,1)} %refs_5_.3) | copy-start | bytes 7962628
  14.4 8.4 %copy-start.1 = (bf16[1152,1152]{1,0:T(8,128)(2,1)S(1)}, bf16[1152,1152]{1,0:T(8,128)(2,1)}, u32[]{:S(2)}) copy-start(bf16[1152,1152]{1,0:T(8,128)(2,1)} %refs_4_.4) | copy-start | bytes 7962628
  22.8 1.3 copy-start.2
  24.1 1.3 copy-start.3
  25.3 1.3 copy-start.5
  26.6 12.6 %copy-start.7 = (bf16[512,1152]{1,0:T(8,128)(2,1)S(1)}, bf16[512,1152]{1,0:T(8,128)(2,1)}, u32[]{:S(2)}) copy-start(bf16[512,1152]{1,0:T(8,128)(2,1)} %get-tuple-element.102.met) | copy-start | bytes 3538948
  26.6 12.6 %copy-start.6 = (bf16[512,1152]{1,0:T(8,128)(2,1)S(1)}, bf16[512,1152]{1,0:T(8,128)(2,1)}, u32[]{:S(2)}) copy-start(bf16[512,1152]{1,0:T(8,128)(2,1)} %get-tuple-element.103.met_other) | copy-start | bytes 3538948
  39.2 28.9 %collective-permute-start.6 = (bf16[512,1152]{1,0:T(8,128)(2,1)S(1)}, bf16[512,1152]{1,0:T(8,128)(2,1)S(1)}, u32[]{:S(2)}, u32[]{:S(2)}) collective-permute-start(bf16[512,1152]{1,0:T(8,128)(2,1)S(1)} %copy-done.7), channel_id=1, source_target_pairs={{0,2},{1,3},{2,0},{3,1},{4,6},{5,7},{6,4},{7,5},{8,10},{9,11},{10,... | collective-permute-start | bytes 3538952 | tf_op jit(solution)/shard_map/ppermute | solution.py:41
  39.2 31.5 %collective-permute-start.7 = (bf16[512,1152]{1,0:T(8,128)(2,1)S(1)}, bf16[512,1152]{1,0:T(8,128)(2,1)S(1)}, u32[]{:S(2)}, u32[]{:S(2)}) collective-permute-start(bf16[512,1152]{1,0:T(8,128)(2,1)S(1)} %copy-done.6), channel_id=1, source_target_pairs={{0,4},{1,5},{2,30},{3,31},{4,8},{5,9},{6,2},{7,3},{8,12},{9,13},{1... | collective-permute-start | bytes 3538952 | tf_op jit(solution)/shard_map/ppermute | solution.py:37
  45.4 46.5 %collective-permute-start.4 = (bf16[512,1152]{1,0:T(8,128)(2,1)S(1)}, bf16[512,1152]{1,0:T(8,128)(2,1)S(1)}, u32[]{:S(2)}, u32[]{:S(2)}) collective-permute-start(bf16[512,1152]{1,0:T(8,128)(2,1)S(1)} %get-tuple-element.100.far_other), channel_id=1, source_target_pairs={{0,2},{1,3},{2,0},{3,1},{4,6},{5,7},{6,4},{7,5},{8,10},{9,11},{10,... | collective-permute-start | bytes 3538952 | tf_op jit(solution)/shard_map/ppermute | solution.py:41
  49.6 46.4 %collective-permute-start.5 = (bf16[512,1152]{1,0:T(8,128)(2,1)S(1)}, bf16[512,1152]{1,0:T(8,128)(2,1)S(1)}, u32[]{:S(2)}, u32[]{:S(2)}) collective-permute-start(bf16[512,1152]{1,0:T(8,128)(2,1)S(1)} %get-tuple-element.99.two), channel_id=1, source_target_pairs={{0,4},{1,5},{2,30},{3,31},{4,8},{5,9},{6,2},{7,3},{8,12},{9,13},{1... | collective-permute-start | bytes 3538952 | tf_op jit(solution)/shard_map/ppermute | solution.py:37
  105.5 12.3 %collective-permute-start.11 = (bf16[192,1152]{1,0:T(8,128)(2,1)S(1)}, bf16[192,1152]{1,0:T(8,128)(2,1)S(1)}, u32[]{:S(2)}, u32[]{:S(2)}) collective-permute-start(bf16[192,1152]{1,0:T(8,128)(2,1)S(1)} %get-tuple-element.114), channel_id=1, source_target_pairs={{0,8},{1,9},{2,10},{3,11},{4,12},{5,13},{6,14},{7,15},{8,0},{9,1},... | collective-permute-start | bytes 1327112 | tf_op jit(solution)/shard_map/ppermute | solution.py:41
  108.9 14.2 %collective-permute-start.10 = (bf16[192,1152]{1,0:T(8,128)(2,1)S(1)}, bf16[192,1152]{1,0:T(8,128)(2,1)S(1)}, u32[]{:S(2)}, u32[]{:S(2)}) collective-permute-start(bf16[192,1152]{1,0:T(8,128)(2,1)S(1)} %get-tuple-element.112), channel_id=1, source_target_pairs={{0,6},{1,7},{2,4},{3,5},{4,2},{5,3},{6,0},{7,1},{8,14},{9,15},{10,... | collective-permute-start | bytes 1327112 | tf_op jit(solution)/shard_map/ppermute | solution.py:41
  109.1 19.4 %collective-permute-start.8 = (bf16[192,1152]{1,0:T(8,128)(2,1)S(1)}, bf16[192,1152]{1,0:T(8,128)(2,1)S(1)}, u32[]{:S(2)}, u32[]{:S(2)}) collective-permute-start(bf16[192,1152]{1,0:T(8,128)(2,1)S(1)} %get-tuple-element.110), channel_id=1, source_target_pairs={{0,2},{1,3},{2,0},{3,1},{4,6},{5,7},{6,4},{7,5},{8,10},{9,11},{10,... | collective-permute-start | bytes 1327112 | tf_op jit(solution)/shard_map/ppermute | solution.py:41
  109.1 22.4 %collective-permute-start.9 = (bf16[192,1152]{1,0:T(8,128)(2,1)S(1)}, bf16[192,1152]{1,0:T(8,128)(2,1)S(1)}, u32[]{:S(2)}, u32[]{:S(2)}) collective-permute-start(bf16[192,1152]{1,0:T(8,128)(2,1)S(1)} %get-tuple-element.111), channel_id=1, source_target_pairs={{0,4},{1,5},{2,6},{3,7},{4,0},{5,1},{6,2},{7,3},{8,12},{9,13},{10,... | collective-permute-start | bytes 1327112 | tf_op jit(solution)/shard_map/ppermute | solution.py:41
  118.5 13.0 %collective-permute-start.12 = (bf16[96,1152]{1,0:T(8,128)(2,1)S(1)}, bf16[96,1152]{1,0:T(8,128)(2,1)S(1)}, u32[]{:S(2)}, u32[]{:S(2)}) collective-permute-start(bf16[96,1152]{1,0:T(8,128)(2,1)S(1)} %get-tuple-element.115), channel_id=1, source_target_pairs={{0,16},{1,17},{2,18},{3,19},{4,20},{5,21},{6,22},{7,23},{8,24},{9,... | collective-permute-start | bytes 663560 | tf_op jit(solution)/shard_map/ppermute | solution.py:41
  131.5 7.6 %collective-permute-start.16 = (bf16[512,1152]{1,0:T(8,128)(2,1)S(1)}, bf16[512,1152]{1,0:T(8,128)(2,1)S(1)}, u32[]{:S(2)}, u32[]{:S(2)}) collective-permute-start(bf16[512,1152]{1,0:T(8,128)(2,1)S(1)} %get-tuple-element.128), channel_id=1, source_target_pairs={{0,1},{1,0},{2,3},{3,2},{4,5},{5,4},{6,7},{7,6},{8,9},{9,8},{10,11... | collective-permute-start | bytes 3538952 | tf_op jit(solution)/shard_map/ppermute | solution.py:41
  132.1 5.5 %collective-permute-start.17 = (bf16[48,1152]{1,0:T(8,128)(2,1)S(1)}, bf16[48,1152]{1,0:T(8,128)(2,1)S(1)}, u32[]{:S(2)}, u32[]{:S(2)}) collective-permute-start(bf16[48,1152]{1,0:T(8,128)(2,1)S(1)} %get-tuple-element.134), channel_id=1, source_target_pairs={{0,2},{1,3},{2,0},{3,1},{4,6},{5,7},{6,4},{7,5},{8,10},{9,11},{10,... | collective-permute-start | bytes 331784 | tf_op jit(solution)/shard_map/ppermute | solution.py:41
  133.2 7.9 %collective-permute-start.13 = (bf16[48,1152]{1,0:T(8,128)(2,1)S(1)}, bf16[48,1152]{1,0:T(8,128)(2,1)S(1)}, u32[]{:S(2)}, u32[]{:S(2)}) collective-permute-start(bf16[48,1152]{1,0:T(8,128)(2,1)S(1)} %get-tuple-element.124), channel_id=1, source_target_pairs={{0,24},{1,25},{2,26},{3,27},{4,28},{5,29},{6,30},{7,31},{8,16},{9,... | collective-permute-start | bytes 331784 | tf_op jit(solution)/shard_map/ppermute | solution.py:41
  135.7 11.3 %collective-permute-start.14 = (bf16[48,1152]{1,0:T(8,128)(2,1)S(1)}, bf16[48,1152]{1,0:T(8,128)(2,1)S(1)}, u32[]{:S(2)}, u32[]{:S(2)}) collective-permute-start(bf16[48,1152]{1,0:T(8,128)(2,1)S(1)} %get-tuple-element.125), channel_id=1, source_target_pairs={{0,16},{1,17},{2,18},{3,19},{4,20},{5,21},{6,22},{7,23},{8,24},{9,... | collective-permute-start | bytes 331784 | tf_op jit(solution)/shard_map/ppermute | solution.py:41
  136.4 10.5 %collective-permute-start.15 = (bf16[48,1152]{1,0:T(8,128)(2,1)S(1)}, bf16[48,1152]{1,0:T(8,128)(2,1)S(1)}, u32[]{:S(2)}, u32[]{:S(2)}) collective-permute-start(bf16[48,1152]{1,0:T(8,128)(2,1)S(1)} %get-tuple-element.126), channel_id=1, source_target_pairs={{0,8},{1,9},{2,10},{3,11},{4,12},{5,13},{6,14},{7,15},{8,0},{9,1},... | collective-permute-start | bytes 331784 | tf_op jit(solution)/shard_map/ppermute | solution.py:41
  138.2 8.7 %collective-permute-start.18 = (bf16[24,1152]{1,0:T(8,128)(2,1)S(1)}, bf16[24,1152]{1,0:T(8,128)(2,1)S(1)}, u32[]{:S(2)}, u32[]{:S(2)}) collective-permute-start(bf16[24,1152]{1,0:T(8,128)(2,1)S(1)} %get-tuple-element.135), channel_id=1, source_target_pairs={{0,4},{1,5},{2,6},{3,7},{4,0},{5,1},{6,2},{7,3},{8,12},{9,13},{10,... | collective-permute-start | bytes 165896 | tf_op jit(solution)/shard_map/ppermute | solution.py:41
  147.6 6.4 %collective-permute-start.22 = (bf16[24,1152]{1,0:T(8,128)(2,1)S(1)}, bf16[24,1152]{1,0:T(8,128)(2,1)S(1)}, u32[]{:S(2)}, u32[]{:S(2)}) collective-permute-start(bf16[24,1152]{1,0:T(8,128)(2,1)S(1)} %b_last.1.mine), channel_id=1, source_target_pairs={{0,4},{1,5},{2,6},{3,7},{4,0},{5,1},{6,2},{7,3},{8,12},{9,13},{10,... | collective-permute-start | bytes 165896 | tf_op jit(solution)/shard_map/ppermute | solution.py:41
  149.5 6.3 %collective-permute-start.19 = (bf16[48,1152]{1,0:T(8,128)(2,1)S(1)}, bf16[48,1152]{1,0:T(8,128)(2,1)S(1)}, u32[]{:S(2)}, u32[]{:S(2)}) collective-permute-start(bf16[48,1152]{1,0:T(8,128)(2,1)S(1)} %a_last.1.refs_0_), channel_id=1, source_target_pairs={{0,8},{1,9},{2,10},{3,11},{4,12},{5,13},{6,14},{7,15},{8,0},{9,1},... | collective-permute-start | bytes 331784 | tf_op jit(solution)/shard_map/ppermute | solution.py:41
  149.5 11.7 %collective-permute-start.20 = (bf16[48,1152]{1,0:T(8,128)(2,1)S(1)}, bf16[48,1152]{1,0:T(8,128)(2,1)S(1)}, u32[]{:S(2)}, u32[]{:S(2)}) collective-permute-start(bf16[48,1152]{1,0:T(8,128)(2,1)S(1)} %a_last.1.refs_0_), channel_id=1, source_target_pairs={{0,16},{1,17},{2,18},{3,19},{4,20},{5,21},{6,22},{7,23},{8,24},{9,... | collective-permute-start | bytes 331784 | tf_op jit(solution)/shard_map/ppermute | solution.py:41
  152.8 8.4 %collective-permute-start.21 = (bf16[48,1152]{1,0:T(8,128)(2,1)S(1)}, bf16[48,1152]{1,0:T(8,128)(2,1)S(1)}, u32[]{:S(2)}, u32[]{:S(2)}) collective-permute-start(bf16[48,1152]{1,0:T(8,128)(2,1)S(1)} %a_last.1.refs_0_), channel_id=1, source_target_pairs={{0,24},{1,25},{2,26},{3,27},{4,28},{5,29},{6,30},{7,31},{8,16},{9,... | collective-permute-start | bytes 331784 | tf_op jit(solution)/shard_map/ppermute | solution.py:41
  154.5 6.7 %collective-permute-start.23 = (bf16[48,1152]{1,0:T(8,128)(2,1)S(1)}, bf16[48,1152]{1,0:T(8,128)(2,1)S(1)}, u32[]{:S(2)}, u32[]{:S(2)}) collective-permute-start(bf16[48,1152]{1,0:T(8,128)(2,1)S(1)} %b_join_y.1.mine), channel_id=1, source_target_pairs={{0,2},{1,3},{2,0},{3,1},{4,6},{5,7},{6,4},{7,5},{8,10},{9,11},{10,... | collective-permute-start | bytes 331784 | tf_op jit(solution)/shard_map/ppermute | solution.py:41
  161.8 11.4 %collective-permute-start.27 = (bf16[96,1152]{1,0:T(8,128)(2,1)S(1)}, bf16[96,1152]{1,0:T(8,128)(2,1)S(1)}, u32[]{:S(2)}, u32[]{:S(2)}) collective-permute-start(bf16[96,1152]{1,0:T(8,128)(2,1)S(1)} %b_join_x.1.mine), channel_id=1, source_target_pairs={{0,16},{1,17},{2,18},{3,19},{4,20},{5,21},{6,22},{7,23},{8,24},{9,... | collective-permute-start | bytes 663560 | tf_op jit(solution)/shard_map/ppermute | solution.py:41
  165.1 13.2 %collective-permute-start.24 = (bf16[192,1152]{1,0:T(8,128)(2,1)S(1)}, bf16[192,1152]{1,0:T(8,128)(2,1)S(1)}, u32[]{:S(2)}, u32[]{:S(2)}) collective-permute-start(bf16[192,1152]{1,0:T(8,128)(2,1)S(1)} %a_join.1.refs_0_), channel_id=1, source_target_pairs={{0,2},{1,3},{2,0},{3,1},{4,6},{5,7},{6,4},{7,5},{8,10},{9,11},{10,... | collective-permute-start | bytes 1327112 | tf_op jit(solution)/shard_map/ppermute | solution.py:41
  165.5 19.5 %collective-permute-start.25 = (bf16[192,1152]{1,0:T(8,128)(2,1)S(1)}, bf16[192,1152]{1,0:T(8,128)(2,1)S(1)}, u32[]{:S(2)}, u32[]{:S(2)}) collective-permute-start(bf16[192,1152]{1,0:T(8,128)(2,1)S(1)} %a_join.1.refs_0_), channel_id=1, source_target_pairs={{0,4},{1,5},{2,6},{3,7},{4,0},{5,1},{6,2},{7,3},{8,12},{9,13},{10,... | collective-permute-start | bytes 1327112 | tf_op jit(solution)/shard_map/ppermute | solution.py:41
  166.1 18.9 %collective-permute-start.26 = (bf16[192,1152]{1,0:T(8,128)(2,1)S(1)}, bf16[192,1152]{1,0:T(8,128)(2,1)S(1)}, u32[]{:S(2)}, u32[]{:S(2)}) collective-permute-start(bf16[192,1152]{1,0:T(8,128)(2,1)S(1)} %a_join.1.refs_0_), channel_id=1, source_target_pairs={{0,6},{1,7},{2,4},{3,5},{4,2},{5,3},{6,0},{7,1},{8,14},{9,15},{10,... | collective-permute-start | bytes 1327112 | tf_op jit(solution)/shard_map/ppermute | solution.py:41
  173.9 11.1 %collective-permute-start.28 = (bf16[192,1152]{1,0:T(8,128)(2,1)S(1)}, bf16[192,1152]{1,0:T(8,128)(2,1)S(1)}, u32[]{:S(2)}, u32[]{:S(2)}) collective-permute-start(bf16[192,1152]{1,0:T(8,128)(2,1)S(1)} %b_join_high.1.refs_4_), channel_id=1, source_target_pairs={{0,8},{1,9},{2,10},{3,11},{4,12},{5,13},{6,14},{7,15},{8,0},{9,1},... | collective-permute-start | bytes 1327112 | tf_op jit(solution)/shard_map/ppermute | solution.py:41
  185.8 5.0 %collective-permute-start.29 = (bf16[1152,1152]{1,0:T(8,128)(2,1)S(1)}, bf16[1152,1152]{1,0:T(8,128)(2,1)S(1)}, u32[]{:S(2)}, u32[]{:S(2)}) collective-permute-start(bf16[1152,1152]{1,0:T(8,128)(2,1)S(1)} %join_all.1.weight), channel_id=1, source_target_pairs={{0,1},{1,0},{2,3},{3,2},{4,5},{5,4},{6,7},{7,6},{8,9},{9,8},{10,11... | collective-permute-start | bytes 7962632 | tf_op jit(solution)/shard_map/ppermute | solution.py:41
where the time goes:
time: 194 us
  waiting for transfers between devices  78.8 us (41%)
  Pallas kernels  69.2 us (36%)
  starting transfers between devices  34.1 us (18%)
  local copies, waits for them, and re-layouts  5.51 us (3%)
  other arithmetic  3.25 us (2%)
  between operations  3.12 us (2%)
    ppermute x26, waiting for transfers between devices, swap(): return lax.ppermute(value, 'dp', [(i, i ^ mask) for i in range(size)])  64.9 us
    ppermute x26, starting transfers between devices, swap(): return lax.ppermute(value, 'dp', [(i, i ^ mask) for i in range(size)])  27.1 us
    pallas_call x2, Pallas kernels, call_tiles(): pl.pallas_call(kernel, grid=(rows // TILE,), out_shape=jax.ShapeDtypeStru...  16.9 us
    pallas_call x2, Pallas kernels, met_units(): pl.pallas_call(functools.partial(met_kernel, own_chip), out_shape=(out, o...  14.5 us
    pallas_call x1, Pallas kernels, last_phase(): pl.pallas_call(last_phase_kernel, grid=(rows // TILE,), out_shape=(jax.Sh...  9.5 us
    ppermute x1, waiting for transfers between devices, body(): got_two = lax.ppermute(raw_two, 'dp', raw_target(1, 0))  7.24 us
    pallas_call x11, Pallas kernels, small_call(): pl.pallas_call(kernel, out_shape=tuple((jax.ShapeDtypeStruct(shape, kind)...  7.22 us
    ppermute x2, waiting for transfers between devices, shift(): return lax.ppermute(value, 'dp', pairs)  6.69 us
  transfers between devices with their start and end apart: 30, of which 15 were waited for; matrix products, arithmetic and copies ran while one was open for 2% of the time, Pallas kernels for 28%

commit v1 on v0

--- a/solution.py
+++ b/solution.py
@@ -201,6 +201,10 @@
         grad[...] = total + pair_term(z[...], far_other[...], scale[0], bias[0], None)
 
 
+def relayed_kernel(scale, bias, z, block, grad_in, grad):
+    grad[...] = grad_in[...] + pair_term(z[...], block[...], scale[0], bias[0], None)
+
+
 def row_tiles(columns):
     return pl.BlockSpec((TILE, columns), lambda i: (i, 0))
 
@@ -227,7 +231,7 @@
 
 
 def last_phase_kernel(
-    place, scale, bias, z, one, two, grad_in, unit, inverse, emb_t, du, *rest
+    place, scale, bias, z, block, grad_in, unit, inverse, emb_t, du, *rest
 ):
     half, (du_all, emb_v, sem) = rest[0], rest[1:]
     step = pl.program_id(0)
@@ -237,8 +241,8 @@
     def _():
         fetch.start()
 
-    grad = grad_in[...] + pair_term(z[...], one[...], scale[0], bias[0], None)
-    grad = scale[0] * (grad + pair_term(z[...], two[...], scale[0], bias[0], None))
+    grad = grad_in[...] + pair_term(z[...], block[...], scale[0], bias[0], None)
+    grad = scale[0] * grad
     units = unit[...]
     inner = jnp.sum(units * grad, axis=1, keepdims=True)
     rounded = ((grad - units * inner) * inverse[...]).astype(BF16)
@@ -254,7 +258,7 @@
         half[...] = dot(emb_v[rows, :], du_all[...]).astype(BF16)
 
 
-def last_phase(place, scale, bias, z, one, two, grad, unit, inverse, emb_t):
+def last_phase(place, scale, bias, z, block, grad, unit, inverse, emb_t):
     rows, columns = z.shape
     half = jax.ShapeDtypeStruct((columns // 6, columns), BF16)
     return pl.pallas_call(
@@ -266,8 +270,7 @@
             SMEM,
             SMEM,
             row_tiles(columns),
-            whole(one),
-            whole(two),
+            whole(block),
             row_tiles(columns),
             row_tiles(columns),
             row_tiles(1),
@@ -281,28 +284,34 @@
         ],
         compiler_params=params(28),
         name="last_phase",
-    )(place, scale, bias, z, one, two, grad, unit, inverse, emb_t)
-
-
-def other_parts_kernel(place, emb_t, du, keep_b, *pieces):
+    )(place, scale, bias, z, block, grad, unit, inverse, emb_t)
+
+
+def sent_parts_kernel(place, emb_t, du, *pieces):
+    for m, out in enumerate(pieces):
+        rows = piece_at(place[IN_PLANE], m + 1, out.shape[0])
+        out[...] = dot(emb_t[rows, :], du[...]).astype(out.dtype)
+
+
+def kept_parts_kernel(place, emb_t, du, keep_a, keep_b):
     height = keep_b.shape[0]
-    for m, out in enumerate(pieces):
-        rows = piece_at(place[IN_PLANE], m, height)
-        out[...] = dot(emb_t[rows, :], du[...]).astype(out.dtype)
-    rows = piece_at(place[Z_LOW], 0, height, emb_t.shape[0] - 2 * height)
-    keep_b[...] = dot(emb_t[rows, :], du[...])
-
-
-def other_parts(place, emb_t, du):
+    at_b = emb_t.shape[0] - 2 * height
+    for out, rows in (
+        (keep_a, piece_at(place[IN_PLANE], 0, height)),
+        (keep_b, piece_at(place[Z_LOW], 0, height, at_b)),
+    ):
+        out[...] = dot(emb_t[rows, :], du[...])
+
+
+def parts(kernel, place, emb_t, du, kinds, name):
     shape = (emb_t.shape[0] // 6, emb_t.shape[0])
-    kinds = [F32, F32, BF16, BF16, BF16]
-    return pl.pallas_call(
-        other_parts_kernel,
+    return pl.pallas_call(
+        kernel,
         out_shape=tuple(jax.ShapeDtypeStruct(shape, kind) for kind in kinds),
         in_specs=[SMEM] + [VMEM] * 2,
-        out_specs=(VMEM,) * 5,
-        compiler_params=params(8),
-        name="other_parts",
+        out_specs=(VMEM,) * len(kinds),
+        compiler_params=params(6),
+        name=name,
     )(place, emb_t, du)
 
 
@@ -543,8 +552,9 @@
         12,
     )
 
+    grad = call_tiles(relayed_kernel, scale, bias, z, (relay_far,), (grad,), "relayed", 10)
     du, give_b = last_phase(
-        place, scale, bias, z, relay_far, relay_pair, grad, unit, inverse, emb_t
+        place, scale, bias, z, relay_pair, grad, unit, inverse, emb_t
     )
 
     def exchange(sends, masks):
@@ -562,8 +572,11 @@
 
     together = lax.optimization_barrier
     got_b = swap(give_b, size, low_bit[1])
-    keep_b, *pieces = other_parts(place, emb_t, du)
-    parts_a = [pieces[0], *exchange(pieces[1:], plane_masks)]
+    sends = parts(sent_parts_kernel, place, emb_t, du, (BF16,) * 3, "sent_parts")
+    got_a = exchange(sends, plane_masks)
+    du, got_b = together((du, got_b))
+    keep_a, keep_b = parts(kept_parts_kernel, place, emb_t, du, (F32, F32), "kept_parts")
+    parts_a = [keep_a, *got_a]
     keep_b, got_b, give_b = halve(keep_b, got_b, high_bit, "b_high")
     du, _ = together((du, give_b))
     d_emb, d_emb_send = rows_back(place, du, weight)
@@ -571,6 +584,7 @@
     d_emb_other = swap(d_emb_send, size, 1)
     pieces = add_split(place, parts_a, "a_split")
     parts_a = [pieces[0], *exchange(pieces[:0:-1], line_masks[::-1])]
+    got_b, _ = together((got_b, pieces))
     keep_b, got_b, _ = halve(keep_b, got_b, x_bit, "b_x")
     d_img_emb, d_txt_emb = pick(
         place, SIDE, (d_emb, d_emb_other), (d_emb_other, d_emb), "rows_pick"
@@ -580,6 +594,7 @@
 
     parts_a, got_b = together((parts_a, got_b))
     shard_a = add_all(place, parts_a, "a_last")
+    got_b, _ = together((got_b, shard_a))
     shard_b = add_two(place, keep_b, got_b, "b_last")
     if size > 32:
         groups = [[i for i in range(size) if i % 32 == k] for k in range(32)]
@@ -592,6 +607,7 @@
     parts_a, got_b = together((parts_a, got_b))
     piece_a = join_four(place, IN_LINE, parts_a, "a_join")
     parts_a = [piece_a, *exchange([piece_a] * 3, plane_masks)]
+    got_b, _ = together((got_b, piece_a))
     shard_b = join_two(place, x_bit[0], shard_b, got_b, "b_join_x")
     shard_b = join_two(place, high_bit[0], *gather(shard_b, high_bit), "b_join_high")
     got_b = swap(shard_b, size, low_bit[1])

time: 194 us -> 191 us (0.985)
  waiting for transfers between devices: 78.8 us -> 75.8 us
    pallas_call x1, Pallas kernels: 9.5 us -> 6.13 us  [last_phase(): pl.pallas_call(last_phase_kernel, grid=(rows // TILE,), out_shape=(jax.Sh...]
    ppermute x2, waiting for transfers between devices: 6.69 us -> 3.44 us  [shift(): return lax.ppermute(value, 'dp', pairs)]
    pallas_call x2 -> x3, Pallas kernels: 16.9 us -> 20.1 us  [call_tiles(): pl.pallas_call(kernel, grid=(rows // TILE,), out_shape=jax.ShapeDtypeStru...]
    pallas_call x1 -> x2, Pallas kernels: 3.28 us -> 4.01 us  [parts(): pl.pallas_call(kernel, out_shape=tuple((jax.ShapeDtypeStruct(shape, kind)...]
  transfers between devices with their start and end apart: 30 -> 30, of which waited for: 15 -> 18; matrix products, arithmetic and copies ran while one was open for 2% -> 2% of each run, Pallas kernels for 28% -> 30%
where the time goes in v1:
time: 191 us
  waiting for transfers between devices  75.8 us (40%)
  Pallas kernels  69.9 us (37%)
  starting transfers between devices  33.1 us (17%)
  local copies, waits for them, and re-layouts  5.51 us (3%)
  other arithmetic  3.25 us (2%)
  between operations  3.1 us (2%)
    ppermute x26, waiting for transfers between devices, swap(): return lax.ppermute(value, 'dp', [(i, i ^ mask) for i in range(size)])  65.2 us
    ppermute x26, starting transfers between devices, swap(): return lax.ppermute(value, 'dp', [(i, i ^ mask) for i in range(size)])  26.1 us
    pallas_call x3, Pallas kernels, call_tiles(): pl.pallas_call(kernel, grid=(rows // TILE,), out_shape=jax.ShapeDtypeStru...  20.1 us
    pallas_call x2, Pallas kernels, met_units(): pl.pallas_call(functools.partial(met_kernel, own_chip), out_shape=(out, o...  14.5 us
    pallas_call x11, Pallas kernels, small_call(): pl.pallas_call(kernel, out_shape=tuple((jax.ShapeDtypeStruct(shape, kind)...  7.23 us
    ppermute x1, waiting for transfers between devices, body(): got_two = lax.ppermute(raw_two, 'dp', raw_target(1, 0))  7.23 us
    pallas_call x1, Pallas kernels, last_phase(): pl.pallas_call(last_phase_kernel, grid=(rows // TILE,), out_shape=(jax.Sh...  6.13 us
    pallas_call x2, Pallas kernels, widen(): pl.pallas_call(functools.partial(widen_kernel, own), out_shape=(out, out)...  6.06 us
  transfers between devices with their start and end apart: 30, of which 18 were waited for; matrix products, arithmetic and copies ran while one was open for 2% of the time, Pallas kernels for 30%

profile of v1, /device:TPU:0, one launch (start us, length us, event | category | flops | bytes accessed | tf_op | source)
XLA Modules:
  0.0 190.6 jit_solution(8531526068061131551)
XLA Ops:
  3.3 3.2 %broadcast_select_fusion = (bf16[512,1152]{1,0:T(8,128)(2,1)}, bf16[512,1152]{1,0:T(8,128)(2,1)}) fusion(bf16[512,1152]{1,0:T(8,128)(2,1)} %refs_1_, bf16[512,1152]{1,0:T(8,128)(2,1)} %refs_4_.3, pred[]{:T(512)} %bitcast.8), kind=kLoop, calls=%fused_computation | loop fusion | flops 1179648 | bytes 4718593 | tf_op jit(solution)/shard_map/jit(_where)/select_n | solution.py:504
  6.5 6.0 %collective-permute-start.2 = (bf16[512,1152]{1,0:T(8,128)(2,1)}, bf16[512,1152]{1,0:T(8,128)(2,1)}, u32[]{:S(2)}, u32[]{:S(2)}) collective-permute-start(bf16[512,1152]{1,0:T(8,128)(2,1)} %get-tuple-element.177), channel_id=1, source_target_pairs={{0,28},{1,3},{2,1},{3,6},{4,0},{5,7},{6,5},{7,10},{8,4},{9,11},{10... | collective-permute-start | bytes 3538952 | tf_op jit(solution)/shard_map/ppermute | solution.py:505
  12.5 0.9 collective-permute-start.3
  13.4 1.0 copy-done.4
  14.4 8.3 %own_met.1 = (bf16[512,1152]{1,0:T(8,128)(2,1)}, bf16[512,1152]{1,0:T(8,128)(2,1)}) custom-call(s32[8]{0:T(128)} %copy-done.8, bf16[512,1152]{1,0:T(8,128)(2,1)} %refs_4_.3, bf16[512,1152]{1,0:T(8,128)(2,1)} %collective-permute-done.1.refs_1_.refs_5_, bf16[512,1152]{1,0:T(8,128)(2,1)} %refs_1_, bf16[512,1152]{1,0:T(8,128)(2,1)} %copy-done.4, ...), custom_call_target="tpu_custom_call" | custom-call | tf_op jit(solution)/shard_map/own_met/pallas_call | solution.py:72
  22.8 1.3 copy-done.2
  24.1 1.3 copy-done.3
  25.4 1.3 copy-done.5
  26.6 5.3 %second_units.1 = (f32[1024,1152]{1,0:T(8,128)S(1)}, f32[1024,1]{1,0:T(8,128)S(1)}, bf16[1024,1152]{1,0:T(8,128)(2,1)S(1)}, bf16[1152,1152]{1,0:T(8,128)(2,1)S(1)}, bf16[1152,1024]{1,0:T(8,128)(2,1)S(1)}) custom-call(s32[8]{0:T(128)S(1)} %copy-done.9, bf16[1152,1152]{1,0:T(8,128)(2,1)S(1)} %copy-done, bf16[512,1152]{1,0:T(8,128)(2,1)S(1)} %copy-done.2, ...), custom_call_target="tpu_custom_call" | custom-call | tf_op jit(solution)/shard_map/second_units/pallas_call | solution.py:118
  32.0 7.2 %collective-permute-done.3.refs_0_.refs_3_ = bf16[512,1152]{1,0:T(8,128)(2,1)} collective-permute-done((bf16[512,1152]{1,0:T(8,128)(2,1)}, bf16[512,1152]{1,0:T(8,128)(2,1)}, u32[]{:S(2)}, u32[]{:S(2)}) %collective-permute-start.3) | collective-permute-done | bytes 1179680 | tf_op jit(solution)/shard_map/ppermute | solution.py:506
  39.3 6.2 %raw_met.1 = (bf16[512,1152]{1,0:T(8,128)(2,1)S(1)}, bf16[512,1152]{1,0:T(8,128)(2,1)S(1)}) custom-call(s32[8]{0:T(128)S(1)} %copy-done.9, bf16[512,1152]{1,0:T(8,128)(2,1)} %collective-permute-done.3.refs_0_.refs_3_, bf16[512,1152]{1,0:T(8,128)(2,1)} %collective-permute-done.2.refs_1_.refs_2_, bf16[512,1152]{1,0:T(8,128)(2,1)} %collective-permute-done.2.refs_1_.refs_2_, ...), custom_call_target="tpu_custom_call" | custom-call | tf_op jit(solution)/shard_map/raw_met/pallas_call | solution.py:72
  45.4 4.2 %collective-permute-start.5 = (bf16[512,1152]{1,0:T(8,128)(2,1)S(1)}, bf16[512,1152]{1,0:T(8,128)(2,1)S(1)}, u32[]{:S(2)}, u32[]{:S(2)}) collective-permute-start(bf16[512,1152]{1,0:T(8,128)(2,1)S(1)} %get-tuple-element.105.far_other), channel_id=1, source_target_pairs={{0,2},{1,3},{2,0},{3,1},{4,6},{5,7},{6,4},{7,5},{8,10},{9,11},{10,... | collective-permute-start | bytes 3538952 | tf_op jit(solution)/shard_map/ppermute | solution.py:41
  50.3 6.9 %own_chip.1.grad_in = f32[1024,1152]{1,0:T(8,128)S(1)} custom-call(f32[1]{0:T(128)S(6)} %exp.3.scale, f32[1]{0:T(128)S(6)} %copy.15.bias, bf16[1024,1152]{1,0:T(8,128)(2,1)S(1)} %get-tuple-element.106.z, bf16[512,1152]{1,0:T(8,128)(2,1)S(1)} %copy-done.7, bf16[512,1152]{1,0:T(8,128)(2,1)S(1)} %copy-done.6), custom_call_target="tpu_custom_call" | custom-call | tf_op jit(solution)/shard_map/own_chip/pallas_call | solution.py:220
  57.2 10.9 %collective-permute-done.6.one = bf16[512,1152]{1,0:T(8,128)(2,1)S(1)} collective-permute-done((bf16[512,1152]{1,0:T(8,128)(2,1)S(1)}, bf16[512,1152]{1,0:T(8,128)(2,1)S(1)}, u32[]{:S(2)}, u32[]{:S(2)}) %collective-permute-start.6) | collective-permute-done | bytes 1179680 | tf_op jit(solution)/shard_map/ppermute | solution.py:41
  68.1 2.6 %collective-permute-done.7.far_own = bf16[512,1152]{1,0:T(8,128)(2,1)S(1)} collective-permute-done((bf16[512,1152]{1,0:T(8,128)(2,1)S(1)}, bf16[512,1152]{1,0:T(8,128)(2,1)S(1)}, u32[]{:S(2)}, u32[]{:S(2)}) %collective-permute-start.7) | collective-permute-done | bytes 1179680 | tf_op jit(solution)/shard_map/ppermute | solution.py:37
  70.7 9.9 %first_phase.1.grad_in = f32[1024,1152]{1,0:T(8,128)S(1)} custom-call(f32[1]{0:T(128)S(6)} %exp.3.scale, f32[1]{0:T(128)S(6)} %copy.15.bias, bf16[1024,1152]{1,0:T(8,128)(2,1)S(1)} %get-tuple-element.106.z, bf16[512,1152]{1,0:T(8,128)(2,1)S(1)} %collective-permute-done.6.one, bf16[512,1152]{1,0:T(8,128)(2,1)S(1)} %get-tuple-element.104.two, ...), custom_call_target="tpu_custom_call" | custom-call | tf_op jit(solution)/shard_map/first_phase/pallas_call | solution.py:220
  80.7 11.3 %collective-permute-done.5.block = bf16[512,1152]{1,0:T(8,128)(2,1)S(1)} collective-permute-done((bf16[512,1152]{1,0:T(8,128)(2,1)S(1)}, bf16[512,1152]{1,0:T(8,128)(2,1)S(1)}, u32[]{:S(2)}, u32[]{:S(2)}) %collective-permute-start.5) | collective-permute-done | bytes 1179680 | tf_op jit(solution)/shard_map/ppermute | solution.py:41
  92.0 3.2 %relayed.1.grad_in = f32[1024,1152]{1,0:T(8,128)S(1)} custom-call(f32[1]{0:T(128)S(6)} %exp.3.scale, f32[1]{0:T(128)S(6)} %copy.15.bias, bf16[1024,1152]{1,0:T(8,128)(2,1)S(1)} %get-tuple-element.106.z, bf16[512,1152]{1,0:T(8,128)(2,1)S(1)} %collective-permute-done.5.block, f32[1024,1152]{1,0:T(8,128)S(1)} %first_phase.1.grad_in), custom_call_target="tpu_custom_call" | custom-call | tf_op jit(solution)/shard_map/relayed/pallas_call | solution.py:220
  96.0 6.1 %last_phase.1 = (bf16[1024,1152]{1,0:T(8,128)(2,1)S(1)}, bf16[192,1152]{1,0:T(8,128)(2,1)S(1)}) custom-call(s32[8]{0:T(128)S(1)} %copy-done.9, f32[1]{0:T(128)S(6)} %exp.3.scale, f32[1]{0:T(128)S(6)} %copy.15.bias, bf16[1024,1152]{1,0:T(8,128)(2,1)S(1)} %get-tuple-element.106.z, bf16[512,1152]{1,0:T(8,128)(2,1)S(1)} %collective-permute-done.4.block, ...), custom_call_target="tpu_custom_call" | custom-call | tf_op jit(solution)/shard_map/last_phase/pallas_call | solution.py:264
  102.2 2.3 %sent_parts.1 = (bf16[192,1152]{1,0:T(8,128)(2,1)S(1)}, bf16[192,1152]{1,0:T(8,128)(2,1)S(1)}, bf16[192,1152]{1,0:T(8,128)(2,1)S(1)}) custom-call(s32[8]{0:T(128)S(1)} %copy-done.9, bf16[1152,1024]{1,0:T(8,128)(2,1)S(1)} %get-tuple-element.98.emb_t, bf16[1024,1152]{1,0:T(8,128)(2,1)S(1)} %get-tuple-element.123.du), custom_call_target="tpu_custom_call" | custom-call | tf_op jit(solution)/shard_map/sent_parts/pallas_call | solution.py:308
  104.5 1.3 collective-permute-start.10
  105.8 0.9 collective-permute-start.11
  106.6 1.4 collective-permute-start.9
  108.0 6.4 %collective-permute-done.8.got = bf16[192,1152]{1,0:T(8,128)(2,1)S(1)} collective-permute-done((bf16[192,1152]{1,0:T(8,128)(2,1)S(1)}, bf16[192,1152]{1,0:T(8,128)(2,1)S(1)}, u32[]{:S(2)}, u32[]{:S(2)}) %collective-permute-start.8) | collective-permute-done | bytes 442400 | tf_op jit(solution)/shard_map/ppermute | solution.py:41
  114.4 1.7 kept_parts.1
  116.9 4.6 %rows_back.1 = (bf16[512,1152]{1,0:T(8,128)(2,1)S(1)}, bf16[512,1152]{1,0:T(8,128)(2,1)S(1)}) custom-call(s32[8]{0:T(128)S(1)} %copy-done.9, bf16[1024,1152]{1,0:T(8,128)(2,1)S(1)} %get-tuple-element.123.du, bf16[1152,1152]{1,0:T(8,128)(2,1)S(1)} %get-tuple-element.124.weight), custom_call_target="tpu_custom_call" | custom-call | tf_op jit(solution)/shard_map/rows_back/pallas_call | solution.py:334
  121.5 4.7 %collective-permute-done.10.refs_2_ = bf16[192,1152]{1,0:T(8,128)(2,1)S(1)} collective-permute-done((bf16[192,1152]{1,0:T(8,128)(2,1)S(1)}, bf16[192,1152]{1,0:T(8,128)(2,1)S(1)}, u32[]{:S(2)}, u32[]{:S(2)}) %collective-permute-start.10) | collective-permute-done | bytes 442400 | tf_op jit(solution)/shard_map/ppermute | solution.py:41
  126.2 1.2 collective-permute-done.9.refs_1_
  127.5 1.7 collective-permute-done.12.got
  129.2 1.0 a_split.1
  131.4 2.0 %collective-permute-start.13 = (bf16[48,1152]{1,0:T(8,128)(2,1)S(1)}, bf16[48,1152]{1,0:T(8,128)(2,1)S(1)}, u32[]{:S(2)}, u32[]{:S(2)}) collective-permute-start(bf16[48,1152]{1,0:T(8,128)(2,1)S(1)} %get-tuple-element.131), channel_id=1, source_target_pairs={{0,24},{1,25},{2,26},{3,27},{4,28},{5,29},{6,30},{7,31},{8,16},{9,... | collective-permute-start | bytes 331784 | tf_op jit(solution)/shard_map/ppermute | solution.py:41
  133.5 2.3 %collective-permute-start.15 = (bf16[48,1152]{1,0:T(8,128)(2,1)S(1)}, bf16[48,1152]{1,0:T(8,128)(2,1)S(1)}, u32[]{:S(2)}, u32[]{:S(2)}) collective-permute-start(bf16[48,1152]{1,0:T(8,128)(2,1)S(1)} %get-tuple-element.133), channel_id=1, source_target_pairs={{0,8},{1,9},{2,10},{3,11},{4,12},{5,13},{6,14},{7,15},{8,0},{9,1},... | collective-permute-start | bytes 331784 | tf_op jit(solution)/shard_map/ppermute | solution.py:41
  137.1 2.0 %rows_pick.1 = (bf16[512,1152]{1,0:T(8,128)(2,1)}, bf16[512,1152]{1,0:T(8,128)(2,1)}) custom-call(s32[8]{0:T(128)S(1)} %copy-done.9, bf16[512,1152]{1,0:T(8,128)(2,1)S(1)} %get-tuple-element.134.refs_0_.refs_3_, bf16[512,1152]{1,0:T(8,128)(2,1)S(1)} %collective-permute-done.16.refs_1_.refs_2_, bf16[512,1152]{1,0:T(8,128)(2,1)S(1)} %collective-permute-done.16.refs_1_.refs_2_, ...), custom_call_target="tpu_custom_call" | custom-call | tf_op jit(solution)/shard_map/rows_pick/pallas_call | solution.py:159
  139.2 4.0 %collective-permute-done.14.refs_2_ = bf16[48,1152]{1,0:T(8,128)(2,1)S(1)} collective-permute-done((bf16[48,1152]{1,0:T(8,128)(2,1)S(1)}, bf16[48,1152]{1,0:T(8,128)(2,1)S(1)}, u32[]{:S(2)}, u32[]{:S(2)}) %collective-permute-start.14) | collective-permute-done | bytes 110624 | tf_op jit(solution)/shard_map/ppermute | solution.py:41
  144.4 1.4 collective-permute-start.22
  145.8 1.0 collective-permute-start.19
  146.8 2.0 %collective-permute-start.20 = (bf16[48,1152]{1,0:T(8,128)(2,1)S(1)}, bf16[48,1152]{1,0:T(8,128)(2,1)S(1)}, u32[]{:S(2)}, u32[]{:S(2)}) collective-permute-start(bf16[48,1152]{1,0:T(8,128)(2,1)S(1)} %a_last.1.refs_0_), channel_id=1, source_target_pairs={{0,16},{1,17},{2,18},{3,19},{4,20},{5,21},{6,22},{7,23},{8,24},{9,... | collective-permute-start | bytes 331784 | tf_op jit(solution)/shard_map/ppermute | solution.py:41
  148.8 1.3 collective-permute-start.21
  151.5 5.9 %collective-permute-done.20.refs_2_ = bf16[48,1152]{1,0:T(8,128)(2,1)S(1)} collective-permute-done((bf16[48,1152]{1,0:T(8,128)(2,1)S(1)}, bf16[48,1152]{1,0:T(8,128)(2,1)S(1)}, u32[]{:S(2)}, u32[]{:S(2)}) %collective-permute-start.20) | collective-permute-done | bytes 110624 | tf_op jit(solution)/shard_map/ppermute | solution.py:41
  158.7 2.3 %collective-permute-start.27 = (bf16[96,1152]{1,0:T(8,128)(2,1)S(1)}, bf16[96,1152]{1,0:T(8,128)(2,1)S(1)}, u32[]{:S(2)}, u32[]{:S(2)}) collective-permute-start(bf16[96,1152]{1,0:T(8,128)(2,1)S(1)} %b_join_x.1.mine), channel_id=1, source_target_pairs={{0,16},{1,17},{2,18},{3,19},{4,20},{5,21},{6,22},{7,23},{8,24},{9,... | collective-permute-start | bytes 663560 | tf_op jit(solution)/shard_map/ppermute | solution.py:41
  161.5 0.9 collective-permute-start.25
  162.5 2.0 %collective-permute-start.26 = (bf16[192,1152]{1,0:T(8,128)(2,1)S(1)}, bf16[192,1152]{1,0:T(8,128)(2,1)S(1)}, u32[]{:S(2)}, u32[]{:S(2)}) collective-permute-start(bf16[192,1152]{1,0:T(8,128)(2,1)S(1)} %a_join.1.refs_0_), channel_id=1, source_target_pairs={{0,6},{1,7},{2,4},{3,5},{4,2},{5,3},{6,0},{7,1},{8,14},{9,15},{10,... | collective-permute-start | bytes 1327112 | tf_op jit(solution)/shard_map/ppermute | solution.py:41
  164.5 5.2 %collective-permute-done.27.got = bf16[96,1152]{1,0:T(8,128)(2,1)S(1)} collective-permute-done((bf16[96,1152]{1,0:T(8,128)(2,1)S(1)}, bf16[96,1152]{1,0:T(8,128)(2,1)S(1)}, u32[]{:S(2)}, u32[]{:S(2)}) %collective-permute-start.27) | collective-permute-done | bytes 221216 | tf_op jit(solution)/shard_map/ppermute | solution.py:41
  170.4 3.7 %collective-permute-done.24.refs_1_ = bf16[192,1152]{1,0:T(8,128)(2,1)S(1)} collective-permute-done((bf16[192,1152]{1,0:T(8,128)(2,1)S(1)}, bf16[192,1152]{1,0:T(8,128)(2,1)S(1)}, u32[]{:S(2)}, u32[]{:S(2)}) %collective-permute-start.24) | collective-permute-done | bytes 442400 | tf_op jit(solution)/shard_map/ppermute | solution.py:41
  174.1 7.6 %collective-permute-done.26.refs_3_ = bf16[192,1152]{1,0:T(8,128)(2,1)S(1)} collective-permute-done((bf16[192,1152]{1,0:T(8,128)(2,1)S(1)}, bf16[192,1152]{1,0:T(8,128)(2,1)S(1)}, u32[]{:S(2)}, u32[]{:S(2)}) %collective-permute-start.26) | collective-permute-done | bytes 442400 | tf_op jit(solution)/shard_map/ppermute | solution.py:41
  182.5 3.0 %widen_own.1 = (f32[1152,1152]{1,0:T(8,128)}, f32[1152,1152]{1,0:T(8,128)}) custom-call(s32[8]{0:T(128)S(1)} %copy-done.9, bf16[1152,1152]{1,0:T(8,128)(2,1)S(1)} %join_all.1.weight), custom_call_target="tpu_custom_call" | custom-call | tf_op jit(solution)/shard_map/widen_own/pallas_call | solution.py:467
  185.5 1.9 %collective-permute-done.29.weight = bf16[1152,1152]{1,0:T(8,128)(2,1)S(1)} collective-permute-done((bf16[1152,1152]{1,0:T(8,128)(2,1)S(1)}, bf16[1152,1152]{1,0:T(8,128)(2,1)S(1)}, u32[]{:S(2)}, u32[]{:S(2)}) %collective-permute-start.29) | collective-permute-done | bytes 2654240 | tf_op jit(solution)/shard_map/ppermute | solution.py:41
  187.4 3.0 %widen_other.1 = (f32[1152,1152]{1,0:T(8,128)}, f32[1152,1152]{1,0:T(8,128)}) custom-call(s32[8]{0:T(128)S(1)} %copy-done.9, bf16[1152,1152]{1,0:T(8,128)(2,1)S(1)} %collective-permute-done.29.weight, f32[1152,1152]{1,0:T(8,128)} %get-tuple-element.172.refs_0_, f32[1152,1152]{1,0:T(8,128)} %get-tuple-element.173.refs_1_), custom_call_target="tpu_custom_call", output_to_operand_aliasing={{0}: (2, {}), {1}: (3, {})} | custom-call | tf_op jit(solution)/shard_map/widen_other/pallas_call | solution.py:467
  (59 shorter events, 11.5 us)
Async XLA Ops:
  0.6 12.8 %collective-permute-start = (bf16[512,1152]{1,0:T(8,128)(2,1)}, bf16[512,1152]{1,0:T(8,128)(2,1)S(1)}, u32[]{:S(2)}, u32[]{:S(2)}) collective-permute-start(bf16[512,1152]{1,0:T(8,128)(2,1)} %refs_1_), channel_id=1, source_target_pairs={{0,1},{1,0},{2,3},{3,2},{4,5},{5,4},{6,7},{7,6},{8,9},{9,8},{10,11... | collective-permute-start | bytes 3538952 | tf_op jit(solution)/shard_map/ppermute | solution.py:41
  1.1 13.3 %collective-permute-start.1 = (bf16[512,1152]{1,0:T(8,128)(2,1)}, bf16[512,1152]{1,0:T(8,128)(2,1)}, u32[]{:S(2)}, u32[]{:S(2)}) collective-permute-start(bf16[512,1152]{1,0:T(8,128)(2,1)} %refs_4_.3), channel_id=1, source_target_pairs={{0,1},{1,0},{2,3},{3,2},{4,5},{5,4},{6,7},{7,6},{8,9},{9,8},{10,11... | collective-permute-start | bytes 3538952 | tf_op jit(solution)/shard_map/ppermute | solution.py:41
  2.0 4.5 %copy-start.8 = (s32[8]{0:T(128)}, s32[8]{0:T(128)S(1)}, u32[]{:S(2)}) copy-start(s32[8]{0:T(128)S(1)} %stack.35.place) | copy-start | bytes 100
  6.5 25.4 %collective-permute-start.2 = (bf16[512,1152]{1,0:T(8,128)(2,1)}, bf16[512,1152]{1,0:T(8,128)(2,1)}, u32[]{:S(2)}, u32[]{:S(2)}) collective-permute-start(bf16[512,1152]{1,0:T(8,128)(2,1)} %get-tuple-element.177), channel_id=1, source_target_pairs={{0,28},{1,3},{2,1},{3,6},{4,0},{5,7},{6,5},{7,10},{8,4},{9,11},{10... | collective-permute-start | bytes 3538952 | tf_op jit(solution)/shard_map/ppermute | solution.py:505
  12.5 10.3 %copy-start.9 = (s32[8]{0:T(128)S(1)}, s32[8]{0:T(128)}, u32[]{:S(2)}) copy-start(s32[8]{0:T(128)} %copy-done.8) | copy-start | bytes 100
  12.5 26.7 %collective-permute-start.3 = (bf16[512,1152]{1,0:T(8,128)(2,1)}, bf16[512,1152]{1,0:T(8,128)(2,1)}, u32[]{:S(2)}, u32[]{:S(2)}) collective-permute-start(bf16[512,1152]{1,0:T(8,128)(2,1)} %get-tuple-element.176), channel_id=1, source_target_pairs={{0,29},{1,2},{2,0},{3,7},{4,1},{5,6},{6,4},{7,11},{8,5},{9,10},{10... | collective-permute-start | bytes 3538952 | tf_op jit(solution)/shard_map/ppermute | solution.py:506
  13.4 1.0 copy-start.4
  14.4 8.4 %copy-start = (bf16[1152,1152]{1,0:T(8,128)(2,1)S(1)}, bf16[1152,1152]{1,0:T(8,128)(2,1)}, u32[]{:S(2)}) copy-start(bf16[1152,1152]{1,0:T(8,128)(2,1)} %refs_5_.3) | copy-start | bytes 7962628
  14.4 8.4 %copy-start.1 = (bf16[1152,1152]{1,0:T(8,128)(2,1)S(1)}, bf16[1152,1152]{1,0:T(8,128)(2,1)}, u32[]{:S(2)}) copy-start(bf16[1152,1152]{1,0:T(8,128)(2,1)} %refs_4_.4) | copy-start | bytes 7962628
  22.8 1.3 copy-start.2
  24.1 1.3 copy-start.3
  25.4 1.3 copy-start.5
  26.6 12.6 %copy-start.7 = (bf16[512,1152]{1,0:T(8,128)(2,1)S(1)}, bf16[512,1152]{1,0:T(8,128)(2,1)}, u32[]{:S(2)}) copy-start(bf16[512,1152]{1,0:T(8,128)(2,1)} %get-tuple-element.107.met) | copy-start | bytes 3538948
  26.6 12.6 %copy-start.6 = (bf16[512,1152]{1,0:T(8,128)(2,1)S(1)}, bf16[512,1152]{1,0:T(8,128)(2,1)}, u32[]{:S(2)}) copy-start(bf16[512,1152]{1,0:T(8,128)(2,1)} %get-tuple-element.108.met_other) | copy-start | bytes 3538948
  39.2 28.9 %collective-permute-start.6 = (bf16[512,1152]{1,0:T(8,128)(2,1)S(1)}, bf16[512,1152]{1,0:T(8,128)(2,1)S(1)}, u32[]{:S(2)}, u32[]{:S(2)}) collective-permute-start(bf16[512,1152]{1,0:T(8,128)(2,1)S(1)} %copy-done.7), channel_id=1, source_target_pairs={{0,2},{1,3},{2,0},{3,1},{4,6},{5,7},{6,4},{7,5},{8,10},{9,11},{10,... | collective-permute-start | bytes 3538952 | tf_op jit(solution)/shard_map/ppermute | solution.py:41
  39.2 31.5 %collective-permute-start.7 = (bf16[512,1152]{1,0:T(8,128)(2,1)S(1)}, bf16[512,1152]{1,0:T(8,128)(2,1)S(1)}, u32[]{:S(2)}, u32[]{:S(2)}) collective-permute-start(bf16[512,1152]{1,0:T(8,128)(2,1)S(1)} %copy-done.6), channel_id=1, source_target_pairs={{0,4},{1,5},{2,30},{3,31},{4,8},{5,9},{6,2},{7,3},{8,12},{9,13},{1... | collective-permute-start | bytes 3538952 | tf_op jit(solution)/shard_map/ppermute | solution.py:37
  45.4 46.5 %collective-permute-start.5 = (bf16[512,1152]{1,0:T(8,128)(2,1)S(1)}, bf16[512,1152]{1,0:T(8,128)(2,1)S(1)}, u32[]{:S(2)}, u32[]{:S(2)}) collective-permute-start(bf16[512,1152]{1,0:T(8,128)(2,1)S(1)} %get-tuple-element.105.far_other), channel_id=1, source_target_pairs={{0,2},{1,3},{2,0},{3,1},{4,6},{5,7},{6,4},{7,5},{8,10},{9,11},{10,... | collective-permute-start | bytes 3538952 | tf_op jit(solution)/shard_map/ppermute | solution.py:41
  49.6 46.4 %collective-permute-start.4 = (bf16[512,1152]{1,0:T(8,128)(2,1)S(1)}, bf16[512,1152]{1,0:T(8,128)(2,1)S(1)}, u32[]{:S(2)}, u32[]{:S(2)}) collective-permute-start(bf16[512,1152]{1,0:T(8,128)(2,1)S(1)} %get-tuple-element.104.two), channel_id=1, source_target_pairs={{0,4},{1,5},{2,30},{3,31},{4,8},{5,9},{6,2},{7,3},{8,12},{9,13},{1... | collective-permute-start | bytes 3538952 | tf_op jit(solution)/shard_map/ppermute | solution.py:37
  102.1 12.3 %collective-permute-start.8 = (bf16[192,1152]{1,0:T(8,128)(2,1)S(1)}, bf16[192,1152]{1,0:T(8,128)(2,1)S(1)}, u32[]{:S(2)}, u32[]{:S(2)}) collective-permute-start(bf16[192,1152]{1,0:T(8,128)(2,1)S(1)} %get-tuple-element.114), channel_id=1, source_target_pairs={{0,8},{1,9},{2,10},{3,11},{4,12},{5,13},{6,14},{7,15},{8,0},{9,1},... | collective-permute-start | bytes 1327112 | tf_op jit(solution)/shard_map/ppermute | solution.py:41
  104.5 21.7 %collective-permute-start.10 = (bf16[192,1152]{1,0:T(8,128)(2,1)S(1)}, bf16[192,1152]{1,0:T(8,128)(2,1)S(1)}, u32[]{:S(2)}, u32[]{:S(2)}) collective-permute-start(bf16[192,1152]{1,0:T(8,128)(2,1)S(1)} %get-tuple-element.118), channel_id=1, source_target_pairs={{0,4},{1,5},{2,6},{3,7},{4,0},{5,1},{6,2},{7,3},{8,12},{9,13},{10,... | collective-permute-start | bytes 1327112 | tf_op jit(solution)/shard_map/ppermute | solution.py:41
  105.8 20.4 %collective-permute-start.11 = (bf16[192,1152]{1,0:T(8,128)(2,1)S(1)}, bf16[192,1152]{1,0:T(8,128)(2,1)S(1)}, u32[]{:S(2)}, u32[]{:S(2)}) collective-permute-start(bf16[192,1152]{1,0:T(8,128)(2,1)S(1)} %get-tuple-element.119), channel_id=1, source_target_pairs={{0,6},{1,7},{2,4},{3,5},{4,2},{5,3},{6,0},{7,1},{8,14},{9,15},{10,... | collective-permute-start | bytes 1327112 | tf_op jit(solution)/shard_map/ppermute | solution.py:41
  106.6 20.8 %collective-permute-start.9 = (bf16[192,1152]{1,0:T(8,128)(2,1)S(1)}, bf16[192,1152]{1,0:T(8,128)(2,1)S(1)}, u32[]{:S(2)}, u32[]{:S(2)}) collective-permute-start(bf16[192,1152]{1,0:T(8,128)(2,1)S(1)} %get-tuple-element.117), channel_id=1, source_target_pairs={{0,2},{1,3},{2,0},{3,1},{4,6},{5,7},{6,4},{7,5},{8,10},{9,11},{10,... | collective-permute-start | bytes 1327112 | tf_op jit(solution)/shard_map/ppermute | solution.py:41
  116.9 12.3 %collective-permute-start.12 = (bf16[96,1152]{1,0:T(8,128)(2,1)S(1)}, bf16[96,1152]{1,0:T(8,128)(2,1)S(1)}, u32[]{:S(2)}, u32[]{:S(2)}) collective-permute-start(bf16[96,1152]{1,0:T(8,128)(2,1)S(1)} %get-tuple-element.122), channel_id=1, source_target_pairs={{0,16},{1,17},{2,18},{3,19},{4,20},{5,21},{6,22},{7,23},{8,24},{9,... | collective-permute-start | bytes 663560 | tf_op jit(solution)/shard_map/ppermute | solution.py:41
  129.2 7.9 %collective-permute-start.16 = (bf16[512,1152]{1,0:T(8,128)(2,1)S(1)}, bf16[512,1152]{1,0:T(8,128)(2,1)S(1)}, u32[]{:S(2)}, u32[]{:S(2)}) collective-permute-start(bf16[512,1152]{1,0:T(8,128)(2,1)S(1)} %get-tuple-element.135), channel_id=1, source_target_pairs={{0,1},{1,0},{2,3},{3,2},{4,5},{5,4},{6,7},{7,6},{8,9},{9,8},{10,11... | collective-permute-start | bytes 3538952 | tf_op jit(solution)/shard_map/ppermute | solution.py:41
  130.8 5.5 %collective-permute-start.17 = (bf16[48,1152]{1,0:T(8,128)(2,1)S(1)}, bf16[48,1152]{1,0:T(8,128)(2,1)S(1)}, u32[]{:S(2)}, u32[]{:S(2)}) collective-permute-start(bf16[48,1152]{1,0:T(8,128)(2,1)S(1)} %get-tuple-element.142), channel_id=1, source_target_pairs={{0,2},{1,3},{2,0},{3,1},{4,6},{5,7},{6,4},{7,5},{8,10},{9,11},{10,... | collective-permute-start | bytes 331784 | tf_op jit(solution)/shard_map/ppermute | solution.py:41
  131.4 7.8 %collective-permute-start.13 = (bf16[48,1152]{1,0:T(8,128)(2,1)S(1)}, bf16[48,1152]{1,0:T(8,128)(2,1)S(1)}, u32[]{:S(2)}, u32[]{:S(2)}) collective-permute-start(bf16[48,1152]{1,0:T(8,128)(2,1)S(1)} %get-tuple-element.131), channel_id=1, source_target_pairs={{0,24},{1,25},{2,26},{3,27},{4,28},{5,29},{6,30},{7,31},{8,16},{9,... | collective-permute-start | bytes 331784 | tf_op jit(solution)/shard_map/ppermute | solution.py:41
  133.5 9.7 %collective-permute-start.14 = (bf16[48,1152]{1,0:T(8,128)(2,1)S(1)}, bf16[48,1152]{1,0:T(8,128)(2,1)S(1)}, u32[]{:S(2)}, u32[]{:S(2)}) collective-permute-start(bf16[48,1152]{1,0:T(8,128)(2,1)S(1)} %get-tuple-element.132), channel_id=1, source_target_pairs={{0,16},{1,17},{2,18},{3,19},{4,20},{5,21},{6,22},{7,23},{8,24},{9,... | collective-permute-start | bytes 331784 | tf_op jit(solution)/shard_map/ppermute | solution.py:41
  133.5 9.7 %collective-permute-start.15 = (bf16[48,1152]{1,0:T(8,128)(2,1)S(1)}, bf16[48,1152]{1,0:T(8,128)(2,1)S(1)}, u32[]{:S(2)}, u32[]{:S(2)}) collective-permute-start(bf16[48,1152]{1,0:T(8,128)(2,1)S(1)} %get-tuple-element.133), channel_id=1, source_target_pairs={{0,8},{1,9},{2,10},{3,11},{4,12},{5,13},{6,14},{7,15},{8,0},{9,1},... | collective-permute-start | bytes 331784 | tf_op jit(solution)/shard_map/ppermute | solution.py:41
  136.9 6.3 %collective-permute-start.18 = (bf16[24,1152]{1,0:T(8,128)(2,1)S(1)}, bf16[24,1152]{1,0:T(8,128)(2,1)S(1)}, u32[]{:S(2)}, u32[]{:S(2)}) collective-permute-start(bf16[24,1152]{1,0:T(8,128)(2,1)S(1)} %get-tuple-element.143), channel_id=1, source_target_pairs={{0,4},{1,5},{2,6},{3,7},{4,0},{5,1},{6,2},{7,3},{8,12},{9,13},{10,... | collective-permute-start | bytes 165896 | tf_op jit(solution)/shard_map/ppermute | solution.py:41
  144.4 5.8 %collective-permute-start.22 = (bf16[24,1152]{1,0:T(8,128)(2,1)S(1)}, bf16[24,1152]{1,0:T(8,128)(2,1)S(1)}, u32[]{:S(2)}, u32[]{:S(2)}) collective-permute-start(bf16[24,1152]{1,0:T(8,128)(2,1)S(1)} %b_last.1.mine), channel_id=1, source_target_pairs={{0,4},{1,5},{2,6},{3,7},{4,0},{5,1},{6,2},{7,3},{8,12},{9,13},{10,... | collective-permute-start | bytes 165896 | tf_op jit(solution)/shard_map/ppermute | solution.py:41
  145.8 5.7 %collective-permute-start.19 = (bf16[48,1152]{1,0:T(8,128)(2,1)S(1)}, bf16[48,1152]{1,0:T(8,128)(2,1)S(1)}, u32[]{:S(2)}, u32[]{:S(2)}) collective-permute-start(bf16[48,1152]{1,0:T(8,128)(2,1)S(1)} %a_last.1.refs_0_), channel_id=1, source_target_pairs={{0,8},{1,9},{2,10},{3,11},{4,12},{5,13},{6,14},{7,15},{8,0},{9,1},... | collective-permute-start | bytes 331784 | tf_op jit(solution)/shard_map/ppermute | solution.py:41
  146.8 10.6 %collective-permute-start.20 = (bf16[48,1152]{1,0:T(8,128)(2,1)S(1)}, bf16[48,1152]{1,0:T(8,128)(2,1)S(1)}, u32[]{:S(2)}, u32[]{:S(2)}) collective-permute-start(bf16[48,1152]{1,0:T(8,128)(2,1)S(1)} %a_last.1.refs_0_), channel_id=1, source_target_pairs={{0,16},{1,17},{2,18},{3,19},{4,20},{5,21},{6,22},{7,23},{8,24},{9,... | collective-permute-start | bytes 331784 | tf_op jit(solution)/shard_map/ppermute | solution.py:41
  148.8 8.6 %collective-permute-start.21 = (bf16[48,1152]{1,0:T(8,128)(2,1)S(1)}, bf16[48,1152]{1,0:T(8,128)(2,1)S(1)}, u32[]{:S(2)}, u32[]{:S(2)}) collective-permute-start(bf16[48,1152]{1,0:T(8,128)(2,1)S(1)} %a_last.1.refs_0_), channel_id=1, source_target_pairs={{0,24},{1,25},{2,26},{3,27},{4,28},{5,29},{6,30},{7,31},{8,16},{9,... | collective-permute-start | bytes 331784 | tf_op jit(solution)/shard_map/ppermute | solution.py:41
  150.8 6.6 %collective-permute-start.23 = (bf16[48,1152]{1,0:T(8,128)(2,1)S(1)}, bf16[48,1152]{1,0:T(8,128)(2,1)S(1)}, u32[]{:S(2)}, u32[]{:S(2)}) collective-permute-start(bf16[48,1152]{1,0:T(8,128)(2,1)S(1)} %b_join_y.1.mine), channel_id=1, source_target_pairs={{0,2},{1,3},{2,0},{3,1},{4,6},{5,7},{6,4},{7,5},{8,10},{9,11},{10,... | collective-permute-start | bytes 331784 | tf_op jit(solution)/shard_map/ppermute | solution.py:41
  158.7 11.0 %collective-permute-start.27 = (bf16[96,1152]{1,0:T(8,128)(2,1)S(1)}, bf16[96,1152]{1,0:T(8,128)(2,1)S(1)}, u32[]{:S(2)}, u32[]{:S(2)}) collective-permute-start(bf16[96,1152]{1,0:T(8,128)(2,1)S(1)} %b_join_x.1.mine), channel_id=1, source_target_pairs={{0,16},{1,17},{2,18},{3,19},{4,20},{5,21},{6,22},{7,23},{8,24},{9,... | collective-permute-start | bytes 663560 | tf_op jit(solution)/shard_map/ppermute | solution.py:41
  161.0 13.1 %collective-permute-start.24 = (bf16[192,1152]{1,0:T(8,128)(2,1)S(1)}, bf16[192,1152]{1,0:T(8,128)(2,1)S(1)}, u32[]{:S(2)}, u32[]{:S(2)}) collective-permute-start(bf16[192,1152]{1,0:T(8,128)(2,1)S(1)} %a_join.1.refs_0_), channel_id=1, source_target_pairs={{0,2},{1,3},{2,0},{3,1},{4,6},{5,7},{6,4},{7,5},{8,10},{9,11},{10,... | collective-permute-start | bytes 1327112 | tf_op jit(solution)/shard_map/ppermute | solution.py:41
  161.5 12.5 %collective-permute-start.25 = (bf16[192,1152]{1,0:T(8,128)(2,1)S(1)}, bf16[192,1152]{1,0:T(8,128)(2,1)S(1)}, u32[]{:S(2)}, u32[]{:S(2)}) collective-permute-start(bf16[192,1152]{1,0:T(8,128)(2,1)S(1)} %a_join.1.refs_0_), channel_id=1, source_target_pairs={{0,4},{1,5},{2,6},{3,7},{4,0},{5,1},{6,2},{7,3},{8,12},{9,13},{10,... | collective-permute-start | bytes 1327112 | tf_op jit(solution)/shard_map/ppermute | solution.py:41
  162.5 19.2 %collective-permute-start.26 = (bf16[192,1152]{1,0:T(8,128)(2,1)S(1)}, bf16[192,1152]{1,0:T(8,128)(2,1)S(1)}, u32[]{:S(2)}, u32[]{:S(2)}) collective-permute-start(bf16[192,1152]{1,0:T(8,128)(2,1)S(1)} %a_join.1.refs_0_), channel_id=1, source_target_pairs={{0,6},{1,7},{2,4},{3,5},{4,2},{5,3},{6,0},{7,1},{8,14},{9,15},{10,... | collective-permute-start | bytes 1327112 | tf_op jit(solution)/shard_map/ppermute | solution.py:41
  170.3 11.3 %collective-permute-start.28 = (bf16[192,1152]{1,0:T(8,128)(2,1)S(1)}, bf16[192,1152]{1,0:T(8,128)(2,1)S(1)}, u32[]{:S(2)}, u32[]{:S(2)}) collective-permute-start(bf16[192,1152]{1,0:T(8,128)(2,1)S(1)} %b_join_high.1.refs_4_), channel_id=1, source_target_pairs={{0,8},{1,9},{2,10},{3,11},{4,12},{5,13},{6,14},{7,15},{8,0},{9,1},... | collective-permute-start | bytes 1327112 | tf_op jit(solution)/shard_map/ppermute | solution.py:41
  182.4 5.0 %collective-permute-start.29 = (bf16[1152,1152]{1,0:T(8,128)(2,1)S(1)}, bf16[1152,1152]{1,0:T(8,128)(2,1)S(1)}, u32[]{:S(2)}, u32[]{:S(2)}) collective-permute-start(bf16[1152,1152]{1,0:T(8,128)(2,1)S(1)} %join_all.1.weight), channel_id=1, source_target_pairs={{0,1},{1,0},{2,3},{3,2},{4,5},{5,4},{6,7},{7,6},{8,9},{9,8},{10,11... | collective-permute-start | bytes 7962632 | tf_op jit(solution)/shard_map/ppermute | solution.py:41

commit v2 on v1

--- a/solution.py
+++ b/solution.py
@@ -499,7 +499,7 @@
                 pairs.append((i, 2 * (chip ^ 1) + to_pair))
         return pairs
 
-    same = place[SAME] == 1
+    same = (chip + side) % 2 == 0
     raw_one = jnp.where(same, txt_emb, img_emb)
     raw_two = jnp.where(same, img_emb, txt_emb)
     got_one = lax.ppermute(raw_one, "dp", raw_target(0, 1))
@@ -574,7 +574,6 @@
     got_b = swap(give_b, size, low_bit[1])
     sends = parts(sent_parts_kernel, place, emb_t, du, (BF16,) * 3, "sent_parts")
     got_a = exchange(sends, plane_masks)
-    du, got_b = together((du, got_b))
     keep_a, keep_b = parts(kept_parts_kernel, place, emb_t, du, (F32, F32), "kept_parts")
     parts_a = [keep_a, *got_a]
     keep_b, got_b, give_b = halve(keep_b, got_b, high_bit, "b_high")
@@ -582,6 +581,7 @@
     d_emb, d_emb_send = rows_back(place, du, weight)
     parts_a, got_b, d_emb_send = together((parts_a, got_b, d_emb_send))
     d_emb_other = swap(d_emb_send, size, 1)
+
     pieces = add_split(place, parts_a, "a_split")
     parts_a = [pieces[0], *exchange(pieces[:0:-1], line_masks[::-1])]
     got_b, _ = together((got_b, pieces))
@@ -589,27 +589,27 @@
     d_img_emb, d_txt_emb = pick(
         place, SIDE, (d_emb, d_emb_other), (d_emb_other, d_emb), "rows_pick"
     )
-    keep_b, got_b, give_b = halve(keep_b, got_b, y_bit, "b_y")
-    parts_a, d_img_emb, d_txt_emb, _ = together((parts_a, d_img_emb, d_txt_emb, give_b))
-
-    parts_a, got_b = together((parts_a, got_b))
+    keep_b, got_b, _ = halve(keep_b, got_b, y_bit, "b_y")
+    shard_b = add_two(place, keep_b, got_b, "b_last")
+    parts_a, d_img_emb, d_txt_emb, _ = together((parts_a, d_img_emb, d_txt_emb, shard_b))
+
     shard_a = add_all(place, parts_a, "a_last")
-    got_b, _ = together((got_b, shard_a))
-    shard_b = add_two(place, keep_b, got_b, "b_last")
     if size > 32:
         groups = [[i for i in range(size) if i % 32 == k] for k in range(32)]
         shard_a, shard_b = lax.psum((shard_a, shard_b), "dp", axis_index_groups=groups)
     parts_a = [shard_a, *exchange([shard_a] * 3, line_masks)]
+    shard_b, _ = together((shard_b, shard_a))
     shard_b = join_two(place, y_bit[0], *gather(shard_b, y_bit), "b_join_y")
     got_b = swap(shard_b, size, x_bit[1])
     parts_a, _ = together((parts_a, shard_b))
 
     parts_a, got_b = together((parts_a, got_b))
     piece_a = join_four(place, IN_LINE, parts_a, "a_join")
-    parts_a = [piece_a, *exchange([piece_a] * 3, plane_masks)]
     got_b, _ = together((got_b, piece_a))
     shard_b = join_two(place, x_bit[0], shard_b, got_b, "b_join_x")
-    shard_b = join_two(place, high_bit[0], *gather(shard_b, high_bit), "b_join_high")
+    got_b = swap(shard_b, size, high_bit[1])
+    parts_a = [piece_a, *exchange([piece_a] * 3, plane_masks)]
+    shard_b = join_two(place, high_bit[0], shard_b, got_b, "b_join_high")
     got_b = swap(shard_b, size, low_bit[1])
     parts_a, got_b = together((parts_a, got_b))
 

time: 191 us -> 187 us (0.979)
  waiting for transfers between devices: 75.8 us -> 71.7 us
    ppermute x26, waiting for transfers between devices: 65.2 us -> 62.4 us  [swap(): return lax.ppermute(value, 'dp', [(i, i ^ mask) for i in range(size)])]
    unnamed x20 -> x18, local copies, waits for them, and re-layouts: 4.84 us -> 4.84 us
  transfers between devices with their start and end apart: 30 -> 30, of which waited for: 18 -> 18; matrix products, arithmetic and copies ran while one was open for 2% -> 2% of each run, Pallas kernels for 30% -> 31%
where the time goes in v2:
time: 187 us
  waiting for transfers between devices  71.7 us (38%)
  Pallas kernels  69.9 us (37%)
  starting transfers between devices  34.1 us (18%)
  local copies, waits for them, and re-layouts  5.5 us (3%)
  other arithmetic  3.24 us (2%)
  between operations  2.47 us (1%)
    ppermute x26, waiting for transfers between devices, swap(): return lax.ppermute(value, 'dp', [(i, i ^ mask) for i in range(size)])  62.4 us
    ppermute x26, starting transfers between devices, swap(): return lax.ppermute(value, 'dp', [(i, i ^ mask) for i in range(size)])  27.2 us
    pallas_call x3, Pallas kernels, call_tiles(): pl.pallas_call(kernel, grid=(rows // TILE,), out_shape=jax.ShapeDtypeStru...  20.1 us
    pallas_call x2, Pallas kernels, met_units(): pl.pallas_call(functools.partial(met_kernel, own_chip), out_shape=(out, o...  14.5 us
    pallas_call x11, Pallas kernels, small_call(): pl.pallas_call(kernel, out_shape=tuple((jax.ShapeDtypeStruct(shape, kind)...  7.23 us
    pallas_call x1, Pallas kernels, last_phase(): pl.pallas_call(last_phase_kernel, grid=(rows // TILE,), out_shape=(jax.Sh...  6.13 us
    pallas_call x2, Pallas kernels, widen(): pl.pallas_call(functools.partial(widen_kernel, own), out_shape=(out, out)...  6.06 us
    ppermute x1, starting transfers between devices, body(): got_one = lax.ppermute(raw_one, 'dp', raw_target(0, 1))  5.98 us
  transfers between devices with their start and end apart: 30, of which 18 were waited for; matrix products, arithmetic and copies ran while one was open for 2% of the time, Pallas kernels for 31%

profile of v2, /device:TPU:0, one launch (start us, length us, event | category | flops | bytes accessed | tf_op | source)
XLA Modules:
  0.0 186.9 jit_solution(4072562536142163875)
XLA Ops:
  1.2 3.2 %broadcast_select_fusion = (bf16[512,1152]{1,0:T(8,128)(2,1)}, bf16[512,1152]{1,0:T(8,128)(2,1)}) fusion(bf16[512,1152]{1,0:T(8,128)(2,1)} %refs_1_, bf16[512,1152]{1,0:T(8,128)(2,1)} %refs_4_.3, pred[]{:T(512)S(6)} %eq.13), kind=kLoop, calls=%fused_computation | loop fusion | flops 1179648 | bytes 4718593 | tf_op jit(solution)/shard_map/jit(_where)/select_n | solution.py:504
  4.5 6.0 %collective-permute-start.2 = (bf16[512,1152]{1,0:T(8,128)(2,1)}, bf16[512,1152]{1,0:T(8,128)(2,1)}, u32[]{:S(2)}, u32[]{:S(2)}) collective-permute-start(bf16[512,1152]{1,0:T(8,128)(2,1)} %get-tuple-element.163), channel_id=1, source_target_pairs={{0,28},{1,3},{2,1},{3,6},{4,0},{5,7},{6,5},{7,10},{8,4},{9,11},{10... | collective-permute-start | bytes 3538952 | tf_op jit(solution)/shard_map/ppermute | solution.py:505
  10.5 0.9 collective-permute-start.3
  12.7 1.0 copy-done.4
  13.8 8.3 %own_met.1 = (bf16[512,1152]{1,0:T(8,128)(2,1)}, bf16[512,1152]{1,0:T(8,128)(2,1)}) custom-call(s32[8]{0:T(128)} %stack.35.place, bf16[512,1152]{1,0:T(8,128)(2,1)} %refs_4_.3, bf16[512,1152]{1,0:T(8,128)(2,1)} %collective-permute-done.1.refs_1_.refs_5_, bf16[512,1152]{1,0:T(8,128)(2,1)} %refs_1_, bf16[512,1152]{1,0:T(8,128)(2,1)} %copy-done.4, ...), custom_call_target="tpu_custom_call" | custom-call | tf_op jit(solution)/shard_map/own_met/pallas_call | solution.py:72
  22.1 1.3 copy-done.2
  23.4 1.3 copy-done.3
  24.7 1.3 copy-done.5
  25.9 5.3 %second_units.1 = (f32[1024,1152]{1,0:T(8,128)S(1)}, f32[1024,1]{1,0:T(8,128)S(1)}, bf16[1024,1152]{1,0:T(8,128)(2,1)S(1)}, bf16[1152,1152]{1,0:T(8,128)(2,1)S(1)}, bf16[1152,1024]{1,0:T(8,128)(2,1)S(1)}) custom-call(s32[8]{0:T(128)S(1)} %copy-done.8, bf16[1152,1152]{1,0:T(8,128)(2,1)S(1)} %copy-done, bf16[512,1152]{1,0:T(8,128)(2,1)S(1)} %copy-done.2, ...), custom_call_target="tpu_custom_call" | custom-call | tf_op jit(solution)/shard_map/second_units/pallas_call | solution.py:118
  31.3 5.9 %collective-permute-done.3.refs_0_.refs_3_ = bf16[512,1152]{1,0:T(8,128)(2,1)} collective-permute-done((bf16[512,1152]{1,0:T(8,128)(2,1)}, bf16[512,1152]{1,0:T(8,128)(2,1)}, u32[]{:S(2)}, u32[]{:S(2)}) %collective-permute-start.3) | collective-permute-done | bytes 1179680 | tf_op jit(solution)/shard_map/ppermute | solution.py:506
  37.2 6.2 %raw_met.1 = (bf16[512,1152]{1,0:T(8,128)(2,1)S(1)}, bf16[512,1152]{1,0:T(8,128)(2,1)S(1)}) custom-call(s32[8]{0:T(128)S(1)} %copy-done.8, bf16[512,1152]{1,0:T(8,128)(2,1)} %collective-permute-done.3.refs_0_.refs_3_, bf16[512,1152]{1,0:T(8,128)(2,1)} %collective-permute-done.2.refs_1_.refs_2_, bf16[512,1152]{1,0:T(8,128)(2,1)} %collective-permute-done.2.refs_1_.refs_2_, ...), custom_call_target="tpu_custom_call" | custom-call | tf_op jit(solution)/shard_map/raw_met/pallas_call | solution.py:72
  43.4 4.2 %collective-permute-start.5 = (bf16[512,1152]{1,0:T(8,128)(2,1)S(1)}, bf16[512,1152]{1,0:T(8,128)(2,1)S(1)}, u32[]{:S(2)}, u32[]{:S(2)}) collective-permute-start(bf16[512,1152]{1,0:T(8,128)(2,1)S(1)} %get-tuple-element.98.far_other), channel_id=1, source_target_pairs={{0,2},{1,3},{2,0},{3,1},{4,6},{5,7},{6,4},{7,5},{8,10},{9,11},{10,... | collective-permute-start | bytes 3538952 | tf_op jit(solution)/shard_map/ppermute | solution.py:41
  48.2 6.9 %own_chip.1.grad_in = f32[1024,1152]{1,0:T(8,128)S(1)} custom-call(f32[1]{0:T(128)S(6)} %exp.3.scale, f32[1]{0:T(128)S(6)} %copy.15.bias, bf16[1024,1152]{1,0:T(8,128)(2,1)S(1)} %get-tuple-element.99.z, bf16[512,1152]{1,0:T(8,128)(2,1)S(1)} %copy-done.7, bf16[512,1152]{1,0:T(8,128)(2,1)S(1)} %copy-done.6), custom_call_target="tpu_custom_call" | custom-call | tf_op jit(solution)/shard_map/own_chip/pallas_call | solution.py:220
  55.1 10.9 %collective-permute-done.6.one = bf16[512,1152]{1,0:T(8,128)(2,1)S(1)} collective-permute-done((bf16[512,1152]{1,0:T(8,128)(2,1)S(1)}, bf16[512,1152]{1,0:T(8,128)(2,1)S(1)}, u32[]{:S(2)}, u32[]{:S(2)}) %collective-permute-start.6) | collective-permute-done | bytes 1179680 | tf_op jit(solution)/shard_map/ppermute | solution.py:41
  66.0 2.6 %collective-permute-done.7.far_own = bf16[512,1152]{1,0:T(8,128)(2,1)S(1)} collective-permute-done((bf16[512,1152]{1,0:T(8,128)(2,1)S(1)}, bf16[512,1152]{1,0:T(8,128)(2,1)S(1)}, u32[]{:S(2)}, u32[]{:S(2)}) %collective-permute-start.7) | collective-permute-done | bytes 1179680 | tf_op jit(solution)/shard_map/ppermute | solution.py:37
  68.7 9.9 %first_phase.1.grad_in = f32[1024,1152]{1,0:T(8,128)S(1)} custom-call(f32[1]{0:T(128)S(6)} %exp.3.scale, f32[1]{0:T(128)S(6)} %copy.15.bias, bf16[1024,1152]{1,0:T(8,128)(2,1)S(1)} %get-tuple-element.99.z, bf16[512,1152]{1,0:T(8,128)(2,1)S(1)} %collective-permute-done.6.one, bf16[512,1152]{1,0:T(8,128)(2,1)S(1)} %get-tuple-element.97.two, ...), custom_call_target="tpu_custom_call" | custom-call | tf_op jit(solution)/shard_map/first_phase/pallas_call | solution.py:220
  78.6 11.3 %collective-permute-done.5.block = bf16[512,1152]{1,0:T(8,128)(2,1)S(1)} collective-permute-done((bf16[512,1152]{1,0:T(8,128)(2,1)S(1)}, bf16[512,1152]{1,0:T(8,128)(2,1)S(1)}, u32[]{:S(2)}, u32[]{:S(2)}) %collective-permute-start.5) | collective-permute-done | bytes 1179680 | tf_op jit(solution)/shard_map/ppermute | solution.py:41
  89.9 3.2 %relayed.1.grad_in = f32[1024,1152]{1,0:T(8,128)S(1)} custom-call(f32[1]{0:T(128)S(6)} %exp.3.scale, f32[1]{0:T(128)S(6)} %copy.15.bias, bf16[1024,1152]{1,0:T(8,128)(2,1)S(1)} %get-tuple-element.99.z, bf16[512,1152]{1,0:T(8,128)(2,1)S(1)} %collective-permute-done.5.block, f32[1024,1152]{1,0:T(8,128)S(1)} %first_phase.1.grad_in), custom_call_target="tpu_custom_call" | custom-call | tf_op jit(solution)/shard_map/relayed/pallas_call | solution.py:220
  93.2 0.8 collective-permute-done.4.block
  93.9 6.1 %last_phase.1 = (bf16[1024,1152]{1,0:T(8,128)(2,1)S(1)}, bf16[192,1152]{1,0:T(8,128)(2,1)S(1)}) custom-call(s32[8]{0:T(128)S(1)} %copy-done.8, f32[1]{0:T(128)S(6)} %exp.3.scale, f32[1]{0:T(128)S(6)} %copy.15.bias, bf16[1024,1152]{1,0:T(8,128)(2,1)S(1)} %get-tuple-element.99.z, bf16[512,1152]{1,0:T(8,128)(2,1)S(1)} %collective-permute-done.4.block, ...), custom_call_target="tpu_custom_call" | custom-call | tf_op jit(solution)/shard_map/last_phase/pallas_call | solution.py:264
  100.2 2.3 %sent_parts.1 = (bf16[192,1152]{1,0:T(8,128)(2,1)S(1)}, bf16[192,1152]{1,0:T(8,128)(2,1)S(1)}, bf16[192,1152]{1,0:T(8,128)(2,1)S(1)}) custom-call(s32[8]{0:T(128)S(1)} %copy-done.8, bf16[1152,1024]{1,0:T(8,128)(2,1)S(1)} %get-tuple-element.91.emb_t, bf16[1024,1152]{1,0:T(8,128)(2,1)S(1)} %get-tuple-element.114.du), custom_call_target="tpu_custom_call" | custom-call | tf_op jit(solution)/shard_map/sent_parts/pallas_call | solution.py:308
  102.4 1.1 collective-permute-start.10
  103.6 1.6 collective-permute-start.8
  105.2 0.8 collective-permute-start.9
  106.0 1.7 kept_parts.1
  107.7 4.6 %collective-permute-done.11.got = bf16[192,1152]{1,0:T(8,128)(2,1)S(1)} collective-permute-done((bf16[192,1152]{1,0:T(8,128)(2,1)S(1)}, bf16[192,1152]{1,0:T(8,128)(2,1)S(1)}, u32[]{:S(2)}, u32[]{:S(2)}) %collective-permute-start.11) | collective-permute-done | bytes 442400 | tf_op jit(solution)/shard_map/ppermute | solution.py:41
  113.1 4.6 %rows_back.1 = (bf16[512,1152]{1,0:T(8,128)(2,1)S(1)}, bf16[512,1152]{1,0:T(8,128)(2,1)S(1)}) custom-call(s32[8]{0:T(128)S(1)} %copy-done.8, bf16[1024,1152]{1,0:T(8,128)(2,1)S(1)} %get-tuple-element.114.du, bf16[1152,1152]{1,0:T(8,128)(2,1)S(1)} %get-tuple-element.115.weight), custom_call_target="tpu_custom_call" | custom-call | tf_op jit(solution)/shard_map/rows_back/pallas_call | solution.py:334
  117.7 6.9 %collective-permute-done.8.refs_1_ = bf16[192,1152]{1,0:T(8,128)(2,1)S(1)} collective-permute-done((bf16[192,1152]{1,0:T(8,128)(2,1)S(1)}, bf16[192,1152]{1,0:T(8,128)(2,1)S(1)}, u32[]{:S(2)}, u32[]{:S(2)}) %collective-permute-start.8) | collective-permute-done | bytes 442400 | tf_op jit(solution)/shard_map/ppermute | solution.py:41
  125.4 1.0 a_split.1
  127.7 2.1 %collective-permute-start.13 = (bf16[48,1152]{1,0:T(8,128)(2,1)S(1)}, bf16[48,1152]{1,0:T(8,128)(2,1)S(1)}, u32[]{:S(2)}, u32[]{:S(2)}) collective-permute-start(bf16[48,1152]{1,0:T(8,128)(2,1)S(1)} %get-tuple-element.122), channel_id=1, source_target_pairs={{0,24},{1,25},{2,26},{3,27},{4,28},{5,29},{6,30},{7,31},{8,16},{9,... | collective-permute-start | bytes 331784 | tf_op jit(solution)/shard_map/ppermute | solution.py:41
  130.6 1.5 collective-permute-start.15
  133.1 0.8 collective-permute-start.18
  133.9 3.4 %collective-permute-done.18.got = bf16[24,1152]{1,0:T(8,128)(2,1)S(1)} collective-permute-done((bf16[24,1152]{1,0:T(8,128)(2,1)S(1)}, bf16[24,1152]{1,0:T(8,128)(2,1)S(1)}, u32[]{:S(2)}, u32[]{:S(2)}) %collective-permute-start.18) | collective-permute-done | bytes 55328 | tf_op jit(solution)/shard_map/ppermute | solution.py:41
  137.9 2.0 %rows_pick.1 = (bf16[512,1152]{1,0:T(8,128)(2,1)}, bf16[512,1152]{1,0:T(8,128)(2,1)}) custom-call(s32[8]{0:T(128)S(1)} %copy-done.8, bf16[512,1152]{1,0:T(8,128)(2,1)S(1)} %get-tuple-element.125.refs_0_.refs_3_, bf16[512,1152]{1,0:T(8,128)(2,1)S(1)} %collective-permute-done.16.refs_1_.refs_2_, bf16[512,1152]{1,0:T(8,128)(2,1)S(1)} %collective-permute-done.16.refs_1_.refs_2_, ...), custom_call_target="tpu_custom_call" | custom-call | tf_op jit(solution)/shard_map/rows_pick/pallas_call | solution.py:159
  139.8 1.0 collective-permute-done.14.refs_2_
  141.4 1.1 collective-permute-start.22
  142.6 3.1 %collective-permute-start.20 = (bf16[48,1152]{1,0:T(8,128)(2,1)S(1)}, bf16[48,1152]{1,0:T(8,128)(2,1)S(1)}, u32[]{:S(2)}, u32[]{:S(2)}) collective-permute-start(bf16[48,1152]{1,0:T(8,128)(2,1)S(1)} %a_last.1.refs_0_), channel_id=1, source_target_pairs={{0,16},{1,17},{2,18},{3,19},{4,20},{5,21},{6,22},{7,23},{8,24},{9,... | collective-permute-start | bytes 331784 | tf_op jit(solution)/shard_map/ppermute | solution.py:41
  145.7 1.2 collective-permute-start.21
  147.4 1.1 collective-permute-start.23
  148.5 5.2 %collective-permute-done.20.refs_2_ = bf16[48,1152]{1,0:T(8,128)(2,1)S(1)} collective-permute-done((bf16[48,1152]{1,0:T(8,128)(2,1)S(1)}, bf16[48,1152]{1,0:T(8,128)(2,1)S(1)}, u32[]{:S(2)}, u32[]{:S(2)}) %collective-permute-start.20) | collective-permute-done | bytes 110624 | tf_op jit(solution)/shard_map/ppermute | solution.py:41
  155.0 2.7 %collective-permute-start.27 = (bf16[96,1152]{1,0:T(8,128)(2,1)S(1)}, bf16[96,1152]{1,0:T(8,128)(2,1)S(1)}, u32[]{:S(2)}, u32[]{:S(2)}) collective-permute-start(bf16[96,1152]{1,0:T(8,128)(2,1)S(1)} %b_join_x.1.mine), channel_id=1, source_target_pairs={{0,16},{1,17},{2,18},{3,19},{4,20},{5,21},{6,22},{7,23},{8,24},{9,... | collective-permute-start | bytes 663560 | tf_op jit(solution)/shard_map/ppermute | solution.py:41
  158.9 2.3 %collective-permute-start.26 = (bf16[192,1152]{1,0:T(8,128)(2,1)S(1)}, bf16[192,1152]{1,0:T(8,128)(2,1)S(1)}, u32[]{:S(2)}, u32[]{:S(2)}) collective-permute-start(bf16[192,1152]{1,0:T(8,128)(2,1)S(1)} %a_join.1.refs_0_), channel_id=1, source_target_pairs={{0,6},{1,7},{2,4},{3,5},{4,2},{5,3},{6,0},{7,1},{8,14},{9,15},{10,... | collective-permute-start | bytes 1327112 | tf_op jit(solution)/shard_map/ppermute | solution.py:41
  161.2 5.2 %collective-permute-done.27.got = bf16[96,1152]{1,0:T(8,128)(2,1)S(1)} collective-permute-done((bf16[96,1152]{1,0:T(8,128)(2,1)S(1)}, bf16[96,1152]{1,0:T(8,128)(2,1)S(1)}, u32[]{:S(2)}, u32[]{:S(2)}) %collective-permute-start.27) | collective-permute-done | bytes 221216 | tf_op jit(solution)/shard_map/ppermute | solution.py:41
  167.1 3.7 %collective-permute-done.24.refs_1_ = bf16[192,1152]{1,0:T(8,128)(2,1)S(1)} collective-permute-done((bf16[192,1152]{1,0:T(8,128)(2,1)S(1)}, bf16[192,1152]{1,0:T(8,128)(2,1)S(1)}, u32[]{:S(2)}, u32[]{:S(2)}) %collective-permute-start.24) | collective-permute-done | bytes 442400 | tf_op jit(solution)/shard_map/ppermute | solution.py:41
  170.8 6.6 %collective-permute-done.25.refs_2_ = bf16[192,1152]{1,0:T(8,128)(2,1)S(1)} collective-permute-done((bf16[192,1152]{1,0:T(8,128)(2,1)S(1)}, bf16[192,1152]{1,0:T(8,128)(2,1)S(1)}, u32[]{:S(2)}, u32[]{:S(2)}) %collective-permute-start.25) | collective-permute-done | bytes 442400 | tf_op jit(solution)/shard_map/ppermute | solution.py:41
  178.8 3.0 %widen_own.1 = (f32[1152,1152]{1,0:T(8,128)}, f32[1152,1152]{1,0:T(8,128)}) custom-call(s32[8]{0:T(128)S(1)} %copy-done.8, bf16[1152,1152]{1,0:T(8,128)(2,1)S(1)} %join_all.1.weight), custom_call_target="tpu_custom_call" | custom-call | tf_op jit(solution)/shard_map/widen_own/pallas_call | solution.py:467
  181.8 1.9 %collective-permute-done.29.weight = bf16[1152,1152]{1,0:T(8,128)(2,1)S(1)} collective-permute-done((bf16[1152,1152]{1,0:T(8,128)(2,1)S(1)}, bf16[1152,1152]{1,0:T(8,128)(2,1)S(1)}, u32[]{:S(2)}, u32[]{:S(2)}) %collective-permute-start.29) | collective-permute-done | bytes 2654240 | tf_op jit(solution)/shard_map/ppermute | solution.py:41
  183.7 3.0 %widen_other.1 = (f32[1152,1152]{1,0:T(8,128)}, f32[1152,1152]{1,0:T(8,128)}) custom-call(s32[8]{0:T(128)S(1)} %copy-done.8, bf16[1152,1152]{1,0:T(8,128)(2,1)S(1)} %collective-permute-done.29.weight, f32[1152,1152]{1,0:T(8,128)} %get-tuple-element.158.refs_0_, f32[1152,1152]{1,0:T(8,128)} %get-tuple-element.159.refs_1_), custom_call_target="tpu_custom_call", output_to_operand_aliasing={{0}: (2, {}), {1}: (3, {})} | custom-call | tf_op jit(solution)/shard_map/widen_other/pallas_call | solution.py:467
  (56 shorter events, 12.4 us)
Async XLA Ops:
  0.6 12.1 %collective-permute-start = (bf16[512,1152]{1,0:T(8,128)(2,1)}, bf16[512,1152]{1,0:T(8,128)(2,1)S(1)}, u32[]{:S(2)}, u32[]{:S(2)}) collective-permute-start(bf16[512,1152]{1,0:T(8,128)(2,1)} %refs_1_), channel_id=1, source_target_pairs={{0,1},{1,0},{2,3},{3,2},{4,5},{5,4},{6,7},{7,6},{8,9},{9,8},{10,11... | collective-permute-start | bytes 3538952 | tf_op jit(solution)/shard_map/ppermute | solution.py:41
  1.1 12.6 %collective-permute-start.1 = (bf16[512,1152]{1,0:T(8,128)(2,1)}, bf16[512,1152]{1,0:T(8,128)(2,1)}, u32[]{:S(2)}, u32[]{:S(2)}) collective-permute-start(bf16[512,1152]{1,0:T(8,128)(2,1)} %refs_4_.3), channel_id=1, source_target_pairs={{0,1},{1,0},{2,3},{3,2},{4,5},{5,4},{6,7},{7,6},{8,9},{9,8},{10,11... | collective-permute-start | bytes 3538952 | tf_op jit(solution)/shard_map/ppermute | solution.py:41
  4.5 26.8 %collective-permute-start.2 = (bf16[512,1152]{1,0:T(8,128)(2,1)}, bf16[512,1152]{1,0:T(8,128)(2,1)}, u32[]{:S(2)}, u32[]{:S(2)}) collective-permute-start(bf16[512,1152]{1,0:T(8,128)(2,1)} %get-tuple-element.163), channel_id=1, source_target_pairs={{0,28},{1,3},{2,1},{3,6},{4,0},{5,7},{6,5},{7,10},{8,4},{9,11},{10... | collective-permute-start | bytes 3538952 | tf_op jit(solution)/shard_map/ppermute | solution.py:505
  10.5 26.7 %collective-permute-start.3 = (bf16[512,1152]{1,0:T(8,128)(2,1)}, bf16[512,1152]{1,0:T(8,128)(2,1)}, u32[]{:S(2)}, u32[]{:S(2)}) collective-permute-start(bf16[512,1152]{1,0:T(8,128)(2,1)} %get-tuple-element.162), channel_id=1, source_target_pairs={{0,29},{1,2},{2,0},{3,7},{4,1},{5,6},{6,4},{7,11},{8,5},{9,10},{10... | collective-permute-start | bytes 3538952 | tf_op jit(solution)/shard_map/ppermute | solution.py:506
  12.7 9.4 %copy-start.8 = (s32[8]{0:T(128)S(1)}, s32[8]{0:T(128)}, u32[]{:S(2)}) copy-start(s32[8]{0:T(128)} %stack.35.place) | copy-start | bytes 100
  12.7 1.0 copy-start.4
  13.8 8.4 %copy-start = (bf16[1152,1152]{1,0:T(8,128)(2,1)S(1)}, bf16[1152,1152]{1,0:T(8,128)(2,1)}, u32[]{:S(2)}) copy-start(bf16[1152,1152]{1,0:T(8,128)(2,1)} %refs_5_.3) | copy-start | bytes 7962628
  13.8 8.4 %copy-start.1 = (bf16[1152,1152]{1,0:T(8,128)(2,1)S(1)}, bf16[1152,1152]{1,0:T(8,128)(2,1)}, u32[]{:S(2)}) copy-start(bf16[1152,1152]{1,0:T(8,128)(2,1)} %refs_4_.4) | copy-start | bytes 7962628
  22.1 1.3 copy-start.2
  23.4 1.3 copy-start.3
  24.7 1.3 copy-start.5
  25.9 11.2 %copy-start.7 = (bf16[512,1152]{1,0:T(8,128)(2,1)S(1)}, bf16[512,1152]{1,0:T(8,128)(2,1)}, u32[]{:S(2)}) copy-start(bf16[512,1152]{1,0:T(8,128)(2,1)} %get-tuple-element.100.met) | copy-start | bytes 3538948
  25.9 11.2 %copy-start.6 = (bf16[512,1152]{1,0:T(8,128)(2,1)S(1)}, bf16[512,1152]{1,0:T(8,128)(2,1)}, u32[]{:S(2)}) copy-start(bf16[512,1152]{1,0:T(8,128)(2,1)} %get-tuple-element.101.met_other) | copy-start | bytes 3538948
  37.1 28.9 %collective-permute-start.6 = (bf16[512,1152]{1,0:T(8,128)(2,1)S(1)}, bf16[512,1152]{1,0:T(8,128)(2,1)S(1)}, u32[]{:S(2)}, u32[]{:S(2)}) collective-permute-start(bf16[512,1152]{1,0:T(8,128)(2,1)S(1)} %copy-done.7), channel_id=1, source_target_pairs={{0,2},{1,3},{2,0},{3,1},{4,6},{5,7},{6,4},{7,5},{8,10},{9,11},{10,... | collective-permute-start | bytes 3538952 | tf_op jit(solution)/shard_map/ppermute | solution.py:41
  37.1 31.5 %collective-permute-start.7 = (bf16[512,1152]{1,0:T(8,128)(2,1)S(1)}, bf16[512,1152]{1,0:T(8,128)(2,1)S(1)}, u32[]{:S(2)}, u32[]{:S(2)}) collective-permute-start(bf16[512,1152]{1,0:T(8,128)(2,1)S(1)} %copy-done.6), channel_id=1, source_target_pairs={{0,4},{1,5},{2,30},{3,31},{4,8},{5,9},{6,2},{7,3},{8,12},{9,13},{1... | collective-permute-start | bytes 3538952 | tf_op jit(solution)/shard_map/ppermute | solution.py:37
  43.4 46.5 %collective-permute-start.5 = (bf16[512,1152]{1,0:T(8,128)(2,1)S(1)}, bf16[512,1152]{1,0:T(8,128)(2,1)S(1)}, u32[]{:S(2)}, u32[]{:S(2)}) collective-permute-start(bf16[512,1152]{1,0:T(8,128)(2,1)S(1)} %get-tuple-element.98.far_other), channel_id=1, source_target_pairs={{0,2},{1,3},{2,0},{3,1},{4,6},{5,7},{6,4},{7,5},{8,10},{9,11},{10,... | collective-permute-start | bytes 3538952 | tf_op jit(solution)/shard_map/ppermute | solution.py:41
  47.6 46.4 %collective-permute-start.4 = (bf16[512,1152]{1,0:T(8,128)(2,1)S(1)}, bf16[512,1152]{1,0:T(8,128)(2,1)S(1)}, u32[]{:S(2)}, u32[]{:S(2)}) collective-permute-start(bf16[512,1152]{1,0:T(8,128)(2,1)S(1)} %get-tuple-element.97.two), channel_id=1, source_target_pairs={{0,4},{1,5},{2,30},{3,31},{4,8},{5,9},{6,2},{7,3},{8,12},{9,13},{1... | collective-permute-start | bytes 3538952 | tf_op jit(solution)/shard_map/ppermute | solution.py:37
  100.1 12.3 %collective-permute-start.11 = (bf16[192,1152]{1,0:T(8,128)(2,1)S(1)}, bf16[192,1152]{1,0:T(8,128)(2,1)S(1)}, u32[]{:S(2)}, u32[]{:S(2)}) collective-permute-start(bf16[192,1152]{1,0:T(8,128)(2,1)S(1)} %get-tuple-element.112), channel_id=1, source_target_pairs={{0,8},{1,9},{2,10},{3,11},{4,12},{5,13},{6,14},{7,15},{8,0},{9,1},... | collective-permute-start | bytes 1327112 | tf_op jit(solution)/shard_map/ppermute | solution.py:41
  102.4 15.3 %collective-permute-start.10 = (bf16[192,1152]{1,0:T(8,128)(2,1)S(1)}, bf16[192,1152]{1,0:T(8,128)(2,1)S(1)}, u32[]{:S(2)}, u32[]{:S(2)}) collective-permute-start(bf16[192,1152]{1,0:T(8,128)(2,1)S(1)} %get-tuple-element.110), channel_id=1, source_target_pairs={{0,6},{1,7},{2,4},{3,5},{4,2},{5,3},{6,0},{7,1},{8,14},{9,15},{10,... | collective-permute-start | bytes 1327112 | tf_op jit(solution)/shard_map/ppermute | solution.py:41
  103.6 21.1 %collective-permute-start.8 = (bf16[192,1152]{1,0:T(8,128)(2,1)S(1)}, bf16[192,1152]{1,0:T(8,128)(2,1)S(1)}, u32[]{:S(2)}, u32[]{:S(2)}) collective-permute-start(bf16[192,1152]{1,0:T(8,128)(2,1)S(1)} %get-tuple-element.108), channel_id=1, source_target_pairs={{0,2},{1,3},{2,0},{3,1},{4,6},{5,7},{6,4},{7,5},{8,10},{9,11},{10,... | collective-permute-start | bytes 1327112 | tf_op jit(solution)/shard_map/ppermute | solution.py:41
  105.2 19.9 %collective-permute-start.9 = (bf16[192,1152]{1,0:T(8,128)(2,1)S(1)}, bf16[192,1152]{1,0:T(8,128)(2,1)S(1)}, u32[]{:S(2)}, u32[]{:S(2)}) collective-permute-start(bf16[192,1152]{1,0:T(8,128)(2,1)S(1)} %get-tuple-element.109), channel_id=1, source_target_pairs={{0,4},{1,5},{2,6},{3,7},{4,0},{5,1},{6,2},{7,3},{8,12},{9,13},{10,... | collective-permute-start | bytes 1327112 | tf_op jit(solution)/shard_map/ppermute | solution.py:41
  113.0 12.3 %collective-permute-start.12 = (bf16[96,1152]{1,0:T(8,128)(2,1)S(1)}, bf16[96,1152]{1,0:T(8,128)(2,1)S(1)}, u32[]{:S(2)}, u32[]{:S(2)}) collective-permute-start(bf16[96,1152]{1,0:T(8,128)(2,1)S(1)} %get-tuple-element.113), channel_id=1, source_target_pairs={{0,16},{1,17},{2,18},{3,19},{4,20},{5,21},{6,22},{7,23},{8,24},{9,... | collective-permute-start | bytes 663560 | tf_op jit(solution)/shard_map/ppermute | solution.py:41
  125.4 12.5 %collective-permute-start.16 = (bf16[512,1152]{1,0:T(8,128)(2,1)S(1)}, bf16[512,1152]{1,0:T(8,128)(2,1)S(1)}, u32[]{:S(2)}, u32[]{:S(2)}) collective-permute-start(bf16[512,1152]{1,0:T(8,128)(2,1)S(1)} %get-tuple-element.126), channel_id=1, source_target_pairs={{0,1},{1,0},{2,3},{3,2},{4,5},{5,4},{6,7},{7,6},{8,9},{9,8},{10,11... | collective-permute-start | bytes 3538952 | tf_op jit(solution)/shard_map/ppermute | solution.py:41
  127.0 5.5 %collective-permute-start.17 = (bf16[48,1152]{1,0:T(8,128)(2,1)S(1)}, bf16[48,1152]{1,0:T(8,128)(2,1)S(1)}, u32[]{:S(2)}, u32[]{:S(2)}) collective-permute-start(bf16[48,1152]{1,0:T(8,128)(2,1)S(1)} %get-tuple-element.133), channel_id=1, source_target_pairs={{0,2},{1,3},{2,0},{3,1},{4,6},{5,7},{6,4},{7,5},{8,10},{9,11},{10,... | collective-permute-start | bytes 331784 | tf_op jit(solution)/shard_map/ppermute | solution.py:41
  127.7 12.2 %collective-permute-start.13 = (bf16[48,1152]{1,0:T(8,128)(2,1)S(1)}, bf16[48,1152]{1,0:T(8,128)(2,1)S(1)}, u32[]{:S(2)}, u32[]{:S(2)}) collective-permute-start(bf16[48,1152]{1,0:T(8,128)(2,1)S(1)} %get-tuple-element.122), channel_id=1, source_target_pairs={{0,24},{1,25},{2,26},{3,27},{4,28},{5,29},{6,30},{7,31},{8,16},{9,... | collective-permute-start | bytes 331784 | tf_op jit(solution)/shard_map/ppermute | solution.py:41
  129.8 11.0 %collective-permute-start.14 = (bf16[48,1152]{1,0:T(8,128)(2,1)S(1)}, bf16[48,1152]{1,0:T(8,128)(2,1)S(1)}, u32[]{:S(2)}, u32[]{:S(2)}) collective-permute-start(bf16[48,1152]{1,0:T(8,128)(2,1)S(1)} %get-tuple-element.123), channel_id=1, source_target_pairs={{0,16},{1,17},{2,18},{3,19},{4,20},{5,21},{6,22},{7,23},{8,24},{9,... | collective-permute-start | bytes 331784 | tf_op jit(solution)/shard_map/ppermute | solution.py:41
  130.6 10.3 %collective-permute-start.15 = (bf16[48,1152]{1,0:T(8,128)(2,1)S(1)}, bf16[48,1152]{1,0:T(8,128)(2,1)S(1)}, u32[]{:S(2)}, u32[]{:S(2)}) collective-permute-start(bf16[48,1152]{1,0:T(8,128)(2,1)S(1)} %get-tuple-element.124), channel_id=1, source_target_pairs={{0,8},{1,9},{2,10},{3,11},{4,12},{5,13},{6,14},{7,15},{8,0},{9,1},... | collective-permute-start | bytes 331784 | tf_op jit(solution)/shard_map/ppermute | solution.py:41
  133.1 4.2 %collective-permute-start.18 = (bf16[24,1152]{1,0:T(8,128)(2,1)S(1)}, bf16[24,1152]{1,0:T(8,128)(2,1)S(1)}, u32[]{:S(2)}, u32[]{:S(2)}) collective-permute-start(bf16[24,1152]{1,0:T(8,128)(2,1)S(1)} %get-tuple-element.135), channel_id=1, source_target_pairs={{0,4},{1,5},{2,6},{3,7},{4,0},{5,1},{6,2},{7,3},{8,12},{9,13},{10,... | collective-permute-start | bytes 165896 | tf_op jit(solution)/shard_map/ppermute | solution.py:41
  141.4 5.4 %collective-permute-start.22 = (bf16[24,1152]{1,0:T(8,128)(2,1)S(1)}, bf16[24,1152]{1,0:T(8,128)(2,1)S(1)}, u32[]{:S(2)}, u32[]{:S(2)}) collective-permute-start(bf16[24,1152]{1,0:T(8,128)(2,1)S(1)} %b_last.1.mine), channel_id=1, source_target_pairs={{0,4},{1,5},{2,6},{3,7},{4,0},{5,1},{6,2},{7,3},{8,12},{9,13},{10,... | collective-permute-start | bytes 165896 | tf_op jit(solution)/shard_map/ppermute | solution.py:41
  142.5 6.1 %collective-permute-start.19 = (bf16[48,1152]{1,0:T(8,128)(2,1)S(1)}, bf16[48,1152]{1,0:T(8,128)(2,1)S(1)}, u32[]{:S(2)}, u32[]{:S(2)}) collective-permute-start(bf16[48,1152]{1,0:T(8,128)(2,1)S(1)} %a_last.1.refs_0_), channel_id=1, source_target_pairs={{0,8},{1,9},{2,10},{3,11},{4,12},{5,13},{6,14},{7,15},{8,0},{9,1},... | collective-permute-start | bytes 331784 | tf_op jit(solution)/shard_map/ppermute | solution.py:41
  142.6 11.2 %collective-permute-start.20 = (bf16[48,1152]{1,0:T(8,128)(2,1)S(1)}, bf16[48,1152]{1,0:T(8,128)(2,1)S(1)}, u32[]{:S(2)}, u32[]{:S(2)}) collective-permute-start(bf16[48,1152]{1,0:T(8,128)(2,1)S(1)} %a_last.1.refs_0_), channel_id=1, source_target_pairs={{0,16},{1,17},{2,18},{3,19},{4,20},{5,21},{6,22},{7,23},{8,24},{9,... | collective-permute-start | bytes 331784 | tf_op jit(solution)/shard_map/ppermute | solution.py:41
  145.7 8.1 %collective-permute-start.21 = (bf16[48,1152]{1,0:T(8,128)(2,1)S(1)}, bf16[48,1152]{1,0:T(8,128)(2,1)S(1)}, u32[]{:S(2)}, u32[]{:S(2)}) collective-permute-start(bf16[48,1152]{1,0:T(8,128)(2,1)S(1)} %a_last.1.refs_0_), channel_id=1, source_target_pairs={{0,24},{1,25},{2,26},{3,27},{4,28},{5,29},{6,30},{7,31},{8,16},{9,... | collective-permute-start | bytes 331784 | tf_op jit(solution)/shard_map/ppermute | solution.py:41
  147.4 6.3 %collective-permute-start.23 = (bf16[48,1152]{1,0:T(8,128)(2,1)S(1)}, bf16[48,1152]{1,0:T(8,128)(2,1)S(1)}, u32[]{:S(2)}, u32[]{:S(2)}) collective-permute-start(bf16[48,1152]{1,0:T(8,128)(2,1)S(1)} %b_join_y.1.mine), channel_id=1, source_target_pairs={{0,2},{1,3},{2,0},{3,1},{4,6},{5,7},{6,4},{7,5},{8,10},{9,11},{10,... | collective-permute-start | bytes 331784 | tf_op jit(solution)/shard_map/ppermute | solution.py:41
  155.0 11.4 %collective-permute-start.27 = (bf16[96,1152]{1,0:T(8,128)(2,1)S(1)}, bf16[96,1152]{1,0:T(8,128)(2,1)S(1)}, u32[]{:S(2)}, u32[]{:S(2)}) collective-permute-start(bf16[96,1152]{1,0:T(8,128)(2,1)S(1)} %b_join_x.1.mine), channel_id=1, source_target_pairs={{0,16},{1,17},{2,18},{3,19},{4,20},{5,21},{6,22},{7,23},{8,24},{9,... | collective-permute-start | bytes 663560 | tf_op jit(solution)/shard_map/ppermute | solution.py:41
  157.7 13.1 %collective-permute-start.24 = (bf16[192,1152]{1,0:T(8,128)(2,1)S(1)}, bf16[192,1152]{1,0:T(8,128)(2,1)S(1)}, u32[]{:S(2)}, u32[]{:S(2)}) collective-permute-start(bf16[192,1152]{1,0:T(8,128)(2,1)S(1)} %a_join.1.refs_0_), channel_id=1, source_target_pairs={{0,2},{1,3},{2,0},{3,1},{4,6},{5,7},{6,4},{7,5},{8,10},{9,11},{10,... | collective-permute-start | bytes 1327112 | tf_op jit(solution)/shard_map/ppermute | solution.py:41
  158.3 19.1 %collective-permute-start.25 = (bf16[192,1152]{1,0:T(8,128)(2,1)S(1)}, bf16[192,1152]{1,0:T(8,128)(2,1)S(1)}, u32[]{:S(2)}, u32[]{:S(2)}) collective-permute-start(bf16[192,1152]{1,0:T(8,128)(2,1)S(1)} %a_join.1.refs_0_), channel_id=1, source_target_pairs={{0,4},{1,5},{2,6},{3,7},{4,0},{5,1},{6,2},{7,3},{8,12},{9,13},{10,... | collective-permute-start | bytes 1327112 | tf_op jit(solution)/shard_map/ppermute | solution.py:41
  158.9 18.5 %collective-permute-start.26 = (bf16[192,1152]{1,0:T(8,128)(2,1)S(1)}, bf16[192,1152]{1,0:T(8,128)(2,1)S(1)}, u32[]{:S(2)}, u32[]{:S(2)}) collective-permute-start(bf16[192,1152]{1,0:T(8,128)(2,1)S(1)} %a_join.1.refs_0_), channel_id=1, source_target_pairs={{0,6},{1,7},{2,4},{3,5},{4,2},{5,3},{6,0},{7,1},{8,14},{9,15},{10,... | collective-permute-start | bytes 1327112 | tf_op jit(solution)/shard_map/ppermute | solution.py:41
  167.1 10.9 %collective-permute-start.28 = (bf16[192,1152]{1,0:T(8,128)(2,1)S(1)}, bf16[192,1152]{1,0:T(8,128)(2,1)S(1)}, u32[]{:S(2)}, u32[]{:S(2)}) collective-permute-start(bf16[192,1152]{1,0:T(8,128)(2,1)S(1)} %b_join_high.1.refs_4_), channel_id=1, source_target_pairs={{0,8},{1,9},{2,10},{3,11},{4,12},{5,13},{6,14},{7,15},{8,0},{9,1},... | collective-permute-start | bytes 1327112 | tf_op jit(solution)/shard_map/ppermute | solution.py:41
  178.7 5.0 %collective-permute-start.29 = (bf16[1152,1152]{1,0:T(8,128)(2,1)S(1)}, bf16[1152,1152]{1,0:T(8,128)(2,1)S(1)}, u32[]{:S(2)}, u32[]{:S(2)}) collective-permute-start(bf16[1152,1152]{1,0:T(8,128)(2,1)S(1)} %join_all.1.weight), channel_id=1, source_target_pairs={{0,1},{1,0},{2,3},{3,2},{4,5},{5,4},{6,7},{7,6},{8,9},{9,8},{10,11... | collective-permute-start | bytes 7962632 | tf_op jit(solution)/shard_map/ppermute | solution.py:41

commit v3 on v2

--- a/solution.py
+++ b/solution.py
@@ -359,38 +359,73 @@
     )(place, *arrays)
 
 
-def add_split_kernel(place, *refs):
-    total = refs[8]
-    total[...] = summed(refs[:4])
-    for m, out in enumerate(refs[4:8]):
-        out[...] = total[piece_at(place[IN_LINE], m, out.shape[0]), :].astype(out.dtype)
-
-
-def add_split(place, parts, name):
+def cut(place, bit, total, mine, give, first=0):
+    for m, out in enumerate((mine, give)):
+        out[...] = total[piece_at(place[bit], m, out.shape[0], first), :].astype(out.dtype)
+
+
+def middle_one_kernel(place, *refs):
+    parts, (keep, got), outs, (total, total_b) = refs[:4], refs[4:6], refs[6:12], refs[12:]
+    total[...] = summed(parts)
+    total_b[...] = keep[...] + got[...].astype(F32)
+    cut(place, Z_LOW, total, outs[0], outs[1])
+    cut(place, Z_HIGH, total, outs[2], outs[3], total.shape[0] // 2)
+    cut(place, X, total_b, outs[4], outs[5])
+
+
+def middle_one(place, parts, keep, got, name):
     rows, columns = parts[0].shape
-    outs = [((rows // 4, columns), F32 if m == 0 else BF16) for m in range(4)]
-    return small_call(add_split_kernel, place, parts, outs, [(rows, columns)], 4, name)
-
-
-def add_all_kernel(place, *refs):
-    refs[4][...] = summed(refs[:4]).astype(BF16)
-
-
-def add_all(place, parts, name):
-    return small_call(add_all_kernel, place, parts, [(parts[0].shape, BF16)], [], 2, name)[0]
-
-
-def join_four_kernel(digit, place, *refs):
-    out, total = refs[4:]
-    for m, piece in enumerate(refs[:4]):
-        total[piece_at(place[digit], m, piece.shape[0]), :] = piece[...].astype(F32)
+    shape = (rows // 4, columns)
+    outs = [(shape, F32), (shape, BF16)] * 3
+    scratch = [(rows, columns), keep.shape]
+    return small_call(middle_one_kernel, place, [*parts, keep, got], outs, scratch, 5, name)
+
+
+def middle_two_kernel(place, *refs):
+    (keep_low, got_low, keep_high, got_high, keep, got), outs, total = refs[:6], refs[6:10], refs[10]
+    outs[0][...] = (keep_low[...] + got_low[...].astype(F32)).astype(BF16)
+    outs[1][...] = (keep_high[...] + got_high[...].astype(F32)).astype(BF16)
+    total[...] = keep[...] + got[...].astype(F32)
+    cut(place, Y, total, outs[2], outs[3])
+
+
+def middle_two(place, arrays, name):
+    shape = arrays[0].shape
+    half = (shape[0] // 2, shape[1])
+    outs = [(shape, BF16), (shape, BF16), (half, F32), (half, BF16)]
+    return small_call(middle_two_kernel, place, arrays, outs, [shape], 3, name)
+
+
+def middle_three_kernel(place, *refs):
+    for k in range(3):
+        refs[6 + k][...] = (refs[2 * k][...].astype(F32) + refs[2 * k + 1][...].astype(F32)).astype(BF16)
+
+
+def middle_three(place, arrays, name):
+    outs = [(array.shape, BF16) for array in arrays[::2]]
+    return small_call(middle_three_kernel, place, arrays, outs, [], 2, name)
+
+
+def middle_four_kernel(place, *refs):
+    (low, got_low, high, got_high), quarters = refs[:4], refs[4:8]
+    out, out_b, total, total_b = refs[8:]
+    height = low.shape[0]
+    for m, piece in enumerate((low, got_low)):
+        total[piece_at(place[Z_LOW], m, height), :] = piece[...].astype(F32)
+    for m, piece in enumerate((high, got_high)):
+        total[piece_at(place[Z_HIGH], m, height, 2 * height), :] = piece[...].astype(F32)
     out[...] = total[...].astype(BF16)
-
-
-def join_four(place, digit, parts, name):
-    shape = (4 * parts[0].shape[0], parts[0].shape[1])
-    kernel = functools.partial(join_four_kernel, digit)
-    return small_call(kernel, place, parts, [(shape, BF16)], [shape], 7, name)[0]
+    height = quarters[0].shape[0]
+    for k, piece in enumerate(quarters):
+        first = (place[X] ^ (k // 2)) * 2 * height
+        total_b[piece_at(place[Y], k % 2, height, first), :] = piece[...].astype(F32)
+    out_b[...] = total_b[...].astype(BF16)
+
+
+def middle_four(place, arrays, quarters, name):
+    shapes = [(4 * a[0].shape[0], a[0].shape[1]) for a in (arrays, quarters)]
+    outs = [(shape, BF16) for shape in shapes]
+    return small_call(middle_four_kernel, place, [*arrays, *quarters], outs, shapes, 5, name)
 
 
 def add_halve_kernel(bit, place, keep, got, mine, give, total):
@@ -404,14 +439,6 @@
     outs = [((rows // 2, columns), kind) for kind in (F32, BF16)]
     kernel = functools.partial(add_halve_kernel, bit)
     return small_call(kernel, place, [keep, got], outs, [keep.shape], 3, name)
-
-
-def add_two_kernel(place, keep, got, out):
-    out[...] = (keep[...] + got[...].astype(F32)).astype(BF16)
-
-
-def add_two(place, keep, got, name):
-    return small_call(add_two_kernel, place, [keep, got], [(keep.shape, BF16)], [], 2, name)[0]
 
 
 def join_two_kernel(bit, place, mine, got, out, total):
@@ -582,31 +609,39 @@
     parts_a, got_b, d_emb_send = together((parts_a, got_b, d_emb_send))
     d_emb_other = swap(d_emb_send, size, 1)
 
-    pieces = add_split(place, parts_a, "a_split")
-    parts_a = [pieces[0], *exchange(pieces[:0:-1], line_masks[::-1])]
-    got_b, _ = together((got_b, pieces))
-    keep_b, got_b, _ = halve(keep_b, got_b, x_bit, "b_x")
+    near, far = low_bit[1], high_bit[1]
+    keep_low, give_low, keep_high, give_high, keep_b, give_b = middle_one(
+        place, parts_a, keep_b, got_b, "middle_one"
+    )
+    got_high, got_low = swap(give_high, size, far), swap(give_low, size, near)
+    got_b = swap(give_b, size, x_bit[1])
+    got_low, got_high, got_b = together((got_low, got_high, got_b))
+    low, high, keep_b, give_b = middle_two(
+        place, (keep_low, got_low, keep_high, got_high, keep_b, got_b), "middle_two"
+    )
+    got_low, got_high = swap(low, size, far), swap(high, size, near)
+    got_b = swap(give_b, size, y_bit[1])
     d_img_emb, d_txt_emb = pick(
         place, SIDE, (d_emb, d_emb_other), (d_emb_other, d_emb), "rows_pick"
     )
-    keep_b, got_b, _ = halve(keep_b, got_b, y_bit, "b_y")
-    shard_b = add_two(place, keep_b, got_b, "b_last")
-    parts_a, d_img_emb, d_txt_emb, _ = together((parts_a, d_img_emb, d_txt_emb, shard_b))
-
-    shard_a = add_all(place, parts_a, "a_last")
+    got_low, got_high, got_b, d_img_emb, d_txt_emb = together(
+        (got_low, got_high, got_b, d_img_emb, d_txt_emb)
+    )
+    low, high, shard_b = middle_three(
+        place, (low, got_low, high, got_high, keep_b, got_b), "middle_three"
+    )
     if size > 32:
         groups = [[i for i in range(size) if i % 32 == k] for k in range(32)]
-        shard_a, shard_b = lax.psum((shard_a, shard_b), "dp", axis_index_groups=groups)
-    parts_a = [shard_a, *exchange([shard_a] * 3, line_masks)]
-    shard_b, _ = together((shard_b, shard_a))
-    shard_b = join_two(place, y_bit[0], *gather(shard_b, y_bit), "b_join_y")
-    got_b = swap(shard_b, size, x_bit[1])
-    parts_a, _ = together((parts_a, shard_b))
-
-    parts_a, got_b = together((parts_a, got_b))
-    piece_a = join_four(place, IN_LINE, parts_a, "a_join")
-    got_b, _ = together((got_b, piece_a))
-    shard_b = join_two(place, x_bit[0], shard_b, got_b, "b_join_x")
+        low, high, shard_b = lax.psum((low, high, shard_b), "dp", axis_index_groups=groups)
+    got_high, got_low = swap(high, size, far), swap(low, size, near)
+    got_y, got_x = swap(shard_b, size, y_bit[1]), swap(shard_b, size, x_bit[1])
+    got_xy = swap(got_y, size, x_bit[1])
+    piece_a, shard_b = middle_four(
+        place,
+        (low, got_low, high, got_high),
+        (shard_b, got_y, got_x, got_xy),
+        "middle_four",
+    )
     got_b = swap(shard_b, size, high_bit[1])
     parts_a = [piece_a, *exchange([piece_a] * 3, plane_masks)]
     shard_b = join_two(place, high_bit[0], shard_b, got_b, "b_join_high")

time: 187 us -> 185 us (0.989)
  waiting for transfers between devices: 71.7 us -> 74 us
  Pallas kernels: 69.9 us -> 67.7 us
  starting transfers between devices: 34.1 us -> 32 us
    ppermute x26 -> x27, waiting for transfers between devices: 62.4 us -> 64.7 us  [swap(): return lax.ppermute(value, 'dp', [(i, i ^ mask) for i in range(size)])]
    pallas_call x11 -> x7, Pallas kernels: 7.23 us -> 5.06 us  [small_call(): pl.pallas_call(kernel, out_shape=tuple((jax.ShapeDtypeStruct(shape, kind)...]
    ppermute x26 -> x27, starting transfers between devices: 27.2 us -> 25.1 us  [swap(): return lax.ppermute(value, 'dp', [(i, i ^ mask) for i in range(size)])]
  transfers between devices with their start and end apart: 30 -> 31, of which waited for: 18 -> 21; matrix products, arithmetic and copies ran while one was open for 2% -> 2% of each run, Pallas kernels for 31% -> 31%
where the time goes in v3:
time: 185 us
  waiting for transfers between devices  74 us (40%)
  Pallas kernels  67.7 us (37%)
  starting transfers between devices  32 us (17%)
  local copies, waits for them, and re-layouts  5.52 us (3%)
  other arithmetic  3.24 us (2%)
  between operations  2.43 us (1%)
    ppermute x27, waiting for transfers between devices, swap(): return lax.ppermute(value, 'dp', [(i, i ^ mask) for i in range(size)])  64.7 us
    ppermute x27, starting transfers between devices, swap(): return lax.ppermute(value, 'dp', [(i, i ^ mask) for i in range(size)])  25.1 us
    pallas_call x3, Pallas kernels, call_tiles(): pl.pallas_call(kernel, grid=(rows // TILE,), out_shape=jax.ShapeDtypeStru...  20.1 us
    pallas_call x2, Pallas kernels, met_units(): pl.pallas_call(functools.partial(met_kernel, own_chip), out_shape=(out, o...  14.5 us
    pallas_call x1, Pallas kernels, last_phase(): pl.pallas_call(last_phase_kernel, grid=(rows // TILE,), out_shape=(jax.Sh...  6.13 us
    pallas_call x2, Pallas kernels, widen(): pl.pallas_call(functools.partial(widen_kernel, own), out_shape=(out, out)...  6.06 us
    ppermute x1, starting transfers between devices, body(): got_one = lax.ppermute(raw_one, 'dp', raw_target(0, 1))  5.98 us
    ppermute x1, waiting for transfers between devices, body(): got_two = lax.ppermute(raw_two, 'dp', raw_target(1, 0))  5.83 us
  transfers between devices with their start and end apart: 31, of which 21 were waited for; matrix products, arithmetic and copies ran while one was open for 2% of the time, Pallas kernels for 31%

profile of v3, /device:TPU:0, one launch (start us, length us, event | category | flops | bytes accessed | tf_op | source)
XLA Modules:
  0.0 184.9 jit_solution(6554029843198064151)
XLA Ops:
  1.2 3.2 %broadcast_select_fusion = (bf16[512,1152]{1,0:T(8,128)(2,1)}, bf16[512,1152]{1,0:T(8,128)(2,1)}) fusion(bf16[512,1152]{1,0:T(8,128)(2,1)} %refs_1_, bf16[512,1152]{1,0:T(8,128)(2,1)} %refs_4_.3, pred[]{:T(512)S(6)} %eq.13), kind=kLoop, calls=%fused_computation | loop fusion | flops 1179648 | bytes 4718593 | tf_op jit(solution)/shard_map/jit(_where)/select_n | solution.py:531
  4.5 6.0 %collective-permute-start.2 = (bf16[512,1152]{1,0:T(8,128)(2,1)}, bf16[512,1152]{1,0:T(8,128)(2,1)}, u32[]{:S(2)}, u32[]{:S(2)}) collective-permute-start(bf16[512,1152]{1,0:T(8,128)(2,1)} %get-tuple-element.157), channel_id=1, source_target_pairs={{0,28},{1,3},{2,1},{3,6},{4,0},{5,7},{6,5},{7,10},{8,4},{9,11},{10... | collective-permute-start | bytes 3538952 | tf_op jit(solution)/shard_map/ppermute | solution.py:532
  10.5 0.9 collective-permute-start.3
  12.8 1.0 copy-done.4
  13.8 8.3 %own_met.1 = (bf16[512,1152]{1,0:T(8,128)(2,1)}, bf16[512,1152]{1,0:T(8,128)(2,1)}) custom-call(s32[8]{0:T(128)} %stack.35.place, bf16[512,1152]{1,0:T(8,128)(2,1)} %refs_4_.3, bf16[512,1152]{1,0:T(8,128)(2,1)} %collective-permute-done.1.refs_1_.refs_5_, bf16[512,1152]{1,0:T(8,128)(2,1)} %refs_1_, bf16[512,1152]{1,0:T(8,128)(2,1)} %copy-done.4, ...), custom_call_target="tpu_custom_call" | custom-call | tf_op jit(solution)/shard_map/own_met/pallas_call | solution.py:72
  22.2 1.3 copy-done.2
  23.4 1.3 copy-done.3
  24.7 1.3 copy-done.5
  26.0 5.3 %second_units.1 = (f32[1024,1152]{1,0:T(8,128)S(1)}, f32[1024,1]{1,0:T(8,128)S(1)}, bf16[1024,1152]{1,0:T(8,128)(2,1)S(1)}, bf16[1152,1152]{1,0:T(8,128)(2,1)S(1)}, bf16[1152,1024]{1,0:T(8,128)(2,1)S(1)}) custom-call(s32[8]{0:T(128)S(1)} %copy-done.8, bf16[1152,1152]{1,0:T(8,128)(2,1)S(1)} %copy-done, bf16[512,1152]{1,0:T(8,128)(2,1)S(1)} %copy-done.2, ...), custom_call_target="tpu_custom_call" | custom-call | tf_op jit(solution)/shard_map/second_units/pallas_call | solution.py:118
  31.3 5.8 %collective-permute-done.3.refs_0_.refs_3_ = bf16[512,1152]{1,0:T(8,128)(2,1)} collective-permute-done((bf16[512,1152]{1,0:T(8,128)(2,1)}, bf16[512,1152]{1,0:T(8,128)(2,1)}, u32[]{:S(2)}, u32[]{:S(2)}) %collective-permute-start.3) | collective-permute-done | bytes 1179680 | tf_op jit(solution)/shard_map/ppermute | solution.py:533
  37.2 6.2 %raw_met.1 = (bf16[512,1152]{1,0:T(8,128)(2,1)S(1)}, bf16[512,1152]{1,0:T(8,128)(2,1)S(1)}) custom-call(s32[8]{0:T(128)S(1)} %copy-done.8, bf16[512,1152]{1,0:T(8,128)(2,1)} %collective-permute-done.3.refs_0_.refs_3_, bf16[512,1152]{1,0:T(8,128)(2,1)} %collective-permute-done.2.refs_1_.refs_2_, bf16[512,1152]{1,0:T(8,128)(2,1)} %collective-permute-done.2.refs_1_.refs_2_, ...), custom_call_target="tpu_custom_call" | custom-call | tf_op jit(solution)/shard_map/raw_met/pallas_call | solution.py:72
  43.4 4.2 %collective-permute-start.5 = (bf16[512,1152]{1,0:T(8,128)(2,1)S(1)}, bf16[512,1152]{1,0:T(8,128)(2,1)S(1)}, u32[]{:S(2)}, u32[]{:S(2)}) collective-permute-start(bf16[512,1152]{1,0:T(8,128)(2,1)S(1)} %get-tuple-element.95.far_other), channel_id=1, source_target_pairs={{0,2},{1,3},{2,0},{3,1},{4,6},{5,7},{6,4},{7,5},{8,10},{9,11},{10,... | collective-permute-start | bytes 3538952 | tf_op jit(solution)/shard_map/ppermute | solution.py:41
  48.2 6.9 %own_chip.1.grad_in = f32[1024,1152]{1,0:T(8,128)S(1)} custom-call(f32[1]{0:T(128)S(6)} %exp.3.scale, f32[1]{0:T(128)S(6)} %copy.15.bias, bf16[1024,1152]{1,0:T(8,128)(2,1)S(1)} %get-tuple-element.96.z, bf16[512,1152]{1,0:T(8,128)(2,1)S(1)} %copy-done.7, bf16[512,1152]{1,0:T(8,128)(2,1)S(1)} %copy-done.6), custom_call_target="tpu_custom_call" | custom-call | tf_op jit(solution)/shard_map/own_chip/pallas_call | solution.py:220
  55.1 10.9 %collective-permute-done.6.one = bf16[512,1152]{1,0:T(8,128)(2,1)S(1)} collective-permute-done((bf16[512,1152]{1,0:T(8,128)(2,1)S(1)}, bf16[512,1152]{1,0:T(8,128)(2,1)S(1)}, u32[]{:S(2)}, u32[]{:S(2)}) %collective-permute-start.6) | collective-permute-done | bytes 1179680 | tf_op jit(solution)/shard_map/ppermute | solution.py:41
  66.0 2.6 %collective-permute-done.7.far_own = bf16[512,1152]{1,0:T(8,128)(2,1)S(1)} collective-permute-done((bf16[512,1152]{1,0:T(8,128)(2,1)S(1)}, bf16[512,1152]{1,0:T(8,128)(2,1)S(1)}, u32[]{:S(2)}, u32[]{:S(2)}) %collective-permute-start.7) | collective-permute-done | bytes 1179680 | tf_op jit(solution)/shard_map/ppermute | solution.py:37
  68.7 9.9 %first_phase.1.grad_in = f32[1024,1152]{1,0:T(8,128)S(1)} custom-call(f32[1]{0:T(128)S(6)} %exp.3.scale, f32[1]{0:T(128)S(6)} %copy.15.bias, bf16[1024,1152]{1,0:T(8,128)(2,1)S(1)} %get-tuple-element.96.z, bf16[512,1152]{1,0:T(8,128)(2,1)S(1)} %collective-permute-done.6.one, bf16[512,1152]{1,0:T(8,128)(2,1)S(1)} %get-tuple-element.94.two, ...), custom_call_target="tpu_custom_call" | custom-call | tf_op jit(solution)/shard_map/first_phase/pallas_call | solution.py:220
  78.6 11.3 %collective-permute-done.5.block = bf16[512,1152]{1,0:T(8,128)(2,1)S(1)} collective-permute-done((bf16[512,1152]{1,0:T(8,128)(2,1)S(1)}, bf16[512,1152]{1,0:T(8,128)(2,1)S(1)}, u32[]{:S(2)}, u32[]{:S(2)}) %collective-permute-start.5) | collective-permute-done | bytes 1179680 | tf_op jit(solution)/shard_map/ppermute | solution.py:41
  89.9 3.2 %relayed.1.grad_in = f32[1024,1152]{1,0:T(8,128)S(1)} custom-call(f32[1]{0:T(128)S(6)} %exp.3.scale, f32[1]{0:T(128)S(6)} %copy.15.bias, bf16[1024,1152]{1,0:T(8,128)(2,1)S(1)} %get-tuple-element.96.z, bf16[512,1152]{1,0:T(8,128)(2,1)S(1)} %collective-permute-done.5.block, f32[1024,1152]{1,0:T(8,128)S(1)} %first_phase.1.grad_in), custom_call_target="tpu_custom_call" | custom-call | tf_op jit(solution)/shard_map/relayed/pallas_call | solution.py:220
  93.9 6.1 %last_phase.1 = (bf16[1024,1152]{1,0:T(8,128)(2,1)S(1)}, bf16[192,1152]{1,0:T(8,128)(2,1)S(1)}) custom-call(s32[8]{0:T(128)S(1)} %copy-done.8, f32[1]{0:T(128)S(6)} %exp.3.scale, f32[1]{0:T(128)S(6)} %copy.15.bias, bf16[1024,1152]{1,0:T(8,128)(2,1)S(1)} %get-tuple-element.96.z, bf16[512,1152]{1,0:T(8,128)(2,1)S(1)} %collective-permute-done.4.block, ...), custom_call_target="tpu_custom_call" | custom-call | tf_op jit(solution)/shard_map/last_phase/pallas_call | solution.py:264
  100.2 2.3 %sent_parts.1 = (bf16[192,1152]{1,0:T(8,128)(2,1)S(1)}, bf16[192,1152]{1,0:T(8,128)(2,1)S(1)}, bf16[192,1152]{1,0:T(8,128)(2,1)S(1)}) custom-call(s32[8]{0:T(128)S(1)} %copy-done.8, bf16[1152,1024]{1,0:T(8,128)(2,1)S(1)} %get-tuple-element.88.emb_t, bf16[1024,1152]{1,0:T(8,128)(2,1)S(1)} %get-tuple-element.111.du), custom_call_target="tpu_custom_call" | custom-call | tf_op jit(solution)/shard_map/sent_parts/pallas_call | solution.py:308
  102.4 1.1 collective-permute-start.10
  103.6 1.6 collective-permute-start.8
  105.2 0.8 collective-permute-start.9
  106.0 1.7 kept_parts.1
  107.7 4.6 %collective-permute-done.11.got = bf16[192,1152]{1,0:T(8,128)(2,1)S(1)} collective-permute-done((bf16[192,1152]{1,0:T(8,128)(2,1)S(1)}, bf16[192,1152]{1,0:T(8,128)(2,1)S(1)}, u32[]{:S(2)}, u32[]{:S(2)}) %collective-permute-start.11) | collective-permute-done | bytes 442400 | tf_op jit(solution)/shard_map/ppermute | solution.py:41
  113.1 4.6 %rows_back.1 = (bf16[512,1152]{1,0:T(8,128)(2,1)S(1)}, bf16[512,1152]{1,0:T(8,128)(2,1)S(1)}) custom-call(s32[8]{0:T(128)S(1)} %copy-done.8, bf16[1024,1152]{1,0:T(8,128)(2,1)S(1)} %get-tuple-element.111.du, bf16[1152,1152]{1,0:T(8,128)(2,1)S(1)} %get-tuple-element.112.weight), custom_call_target="tpu_custom_call" | custom-call | tf_op jit(solution)/shard_map/rows_back/pallas_call | solution.py:334
  117.7 6.9 %collective-permute-done.8.refs_1_ = bf16[192,1152]{1,0:T(8,128)(2,1)S(1)} collective-permute-done((bf16[192,1152]{1,0:T(8,128)(2,1)S(1)}, bf16[192,1152]{1,0:T(8,128)(2,1)S(1)}, u32[]{:S(2)}, u32[]{:S(2)}) %collective-permute-start.8) | collective-permute-done | bytes 442400 | tf_op jit(solution)/shard_map/ppermute | solution.py:41
  125.4 1.0 middle_one.1
  126.4 1.5 collective-permute-start.13
  127.9 0.9 collective-permute-start.14
  128.8 1.0 collective-permute-start.15
  129.8 2.9 %collective-permute-done.13.refs_1_ = bf16[48,1152]{1,0:T(8,128)(2,1)S(1)} collective-permute-done((bf16[48,1152]{1,0:T(8,128)(2,1)S(1)}, bf16[48,1152]{1,0:T(8,128)(2,1)S(1)}, u32[]{:S(2)}, u32[]{:S(2)}) %collective-permute-start.13) | collective-permute-done | bytes 110624 | tf_op jit(solution)/shard_map/ppermute | solution.py:41
  132.7 3.7 %collective-permute-done.14.refs_3_ = bf16[48,1152]{1,0:T(8,128)(2,1)S(1)} collective-permute-done((bf16[48,1152]{1,0:T(8,128)(2,1)S(1)}, bf16[48,1152]{1,0:T(8,128)(2,1)S(1)}, u32[]{:S(2)}, u32[]{:S(2)}) %collective-permute-start.14) | collective-permute-done | bytes 110624 | tf_op jit(solution)/shard_map/ppermute | solution.py:41
  137.5 1.5 collective-permute-start.17
  139.0 1.5 collective-permute-start.18
  140.5 2.0 %rows_pick.1 = (bf16[512,1152]{1,0:T(8,128)(2,1)}, bf16[512,1152]{1,0:T(8,128)(2,1)}) custom-call(s32[8]{0:T(128)S(1)} %copy-done.8, bf16[512,1152]{1,0:T(8,128)(2,1)S(1)} %get-tuple-element.132.refs_0_.refs_3_, bf16[512,1152]{1,0:T(8,128)(2,1)S(1)} %collective-permute-done.19.refs_1_.refs_2_, bf16[512,1152]{1,0:T(8,128)(2,1)S(1)} %collective-permute-done.19.refs_1_.refs_2_, ...), custom_call_target="tpu_custom_call" | custom-call | tf_op jit(solution)/shard_map/rows_pick/pallas_call | solution.py:159
  145.9 2.7 %collective-permute-start.21 = (bf16[48,1152]{1,0:T(8,128)(2,1)S(1)}, bf16[48,1152]{1,0:T(8,128)(2,1)S(1)}, u32[]{:S(2)}, u32[]{:S(2)}) collective-permute-start(bf16[48,1152]{1,0:T(8,128)(2,1)S(1)} %get-tuple-element.143.refs_2_), channel_id=1, source_target_pairs={{0,16},{1,17},{2,18},{3,19},{4,20},{5,21},{6,22},{7,23},{8,24},{9,... | collective-permute-start | bytes 331784 | tf_op jit(solution)/shard_map/ppermute | solution.py:41
  148.6 1.3 collective-permute-start.23
  150.6 2.1 %collective-permute-done.23.refs_6_ = bf16[24,1152]{1,0:T(8,128)(2,1)S(1)} collective-permute-done((bf16[24,1152]{1,0:T(8,128)(2,1)S(1)}, bf16[24,1152]{1,0:T(8,128)(2,1)S(1)}, u32[]{:S(2)}, u32[]{:S(2)}) %collective-permute-start.23) | collective-permute-done | bytes 55328 | tf_op jit(solution)/shard_map/ppermute | solution.py:41
  152.7 1.3 collective-permute-done.24.refs_7_
  155.2 1.2 collective-permute-start.25
  157.0 1.6 collective-permute-start.27
  158.7 5.8 %collective-permute-done.28.got = bf16[96,1152]{1,0:T(8,128)(2,1)S(1)} collective-permute-done((bf16[96,1152]{1,0:T(8,128)(2,1)S(1)}, bf16[96,1152]{1,0:T(8,128)(2,1)S(1)}, u32[]{:S(2)}, u32[]{:S(2)}) %collective-permute-start.28) | collective-permute-done | bytes 221216 | tf_op jit(solution)/shard_map/ppermute | solution.py:41
  165.2 3.1 %collective-permute-done.25.refs_1_ = bf16[192,1152]{1,0:T(8,128)(2,1)S(1)} collective-permute-done((bf16[192,1152]{1,0:T(8,128)(2,1)S(1)}, bf16[192,1152]{1,0:T(8,128)(2,1)S(1)}, u32[]{:S(2)}, u32[]{:S(2)}) %collective-permute-start.25) | collective-permute-done | bytes 442400 | tf_op jit(solution)/shard_map/ppermute | solution.py:41
  168.3 6.8 %collective-permute-done.26.refs_2_ = bf16[192,1152]{1,0:T(8,128)(2,1)S(1)} collective-permute-done((bf16[192,1152]{1,0:T(8,128)(2,1)S(1)}, bf16[192,1152]{1,0:T(8,128)(2,1)S(1)}, u32[]{:S(2)}, u32[]{:S(2)}) %collective-permute-start.26) | collective-permute-done | bytes 442400 | tf_op jit(solution)/shard_map/ppermute | solution.py:41
  176.7 3.0 %widen_own.1 = (f32[1152,1152]{1,0:T(8,128)}, f32[1152,1152]{1,0:T(8,128)}) custom-call(s32[8]{0:T(128)S(1)} %copy-done.8, bf16[1152,1152]{1,0:T(8,128)(2,1)S(1)} %join_all.1.weight), custom_call_target="tpu_custom_call" | custom-call | tf_op jit(solution)/shard_map/widen_own/pallas_call | solution.py:494
  179.7 1.9 %collective-permute-done.30.weight = bf16[1152,1152]{1,0:T(8,128)(2,1)S(1)} collective-permute-done((bf16[1152,1152]{1,0:T(8,128)(2,1)S(1)}, bf16[1152,1152]{1,0:T(8,128)(2,1)S(1)}, u32[]{:S(2)}, u32[]{:S(2)}) %collective-permute-start.30) | collective-permute-done | bytes 2654240 | tf_op jit(solution)/shard_map/ppermute | solution.py:41
  181.6 3.0 %widen_other.1 = (f32[1152,1152]{1,0:T(8,128)}, f32[1152,1152]{1,0:T(8,128)}) custom-call(s32[8]{0:T(128)S(1)} %copy-done.8, bf16[1152,1152]{1,0:T(8,128)(2,1)S(1)} %collective-permute-done.30.weight, f32[1152,1152]{1,0:T(8,128)} %get-tuple-element.152.refs_0_, f32[1152,1152]{1,0:T(8,128)} %get-tuple-element.153.refs_1_), custom_call_target="tpu_custom_call", output_to_operand_aliasing={{0}: (2, {}), {1}: (3, {})} | custom-call | tf_op jit(solution)/shard_map/widen_other/pallas_call | solution.py:494
  (54 shorter events, 13.0 us)
Async XLA Ops:
  0.6 12.1 %collective-permute-start = (bf16[512,1152]{1,0:T(8,128)(2,1)}, bf16[512,1152]{1,0:T(8,128)(2,1)S(1)}, u32[]{:S(2)}, u32[]{:S(2)}) collective-permute-start(bf16[512,1152]{1,0:T(8,128)(2,1)} %refs_1_), channel_id=1, source_target_pairs={{0,1},{1,0},{2,3},{3,2},{4,5},{5,4},{6,7},{7,6},{8,9},{9,8},{10,11... | collective-permute-start | bytes 3538952 | tf_op jit(solution)/shard_map/ppermute | solution.py:41
  1.1 12.6 %collective-permute-start.1 = (bf16[512,1152]{1,0:T(8,128)(2,1)}, bf16[512,1152]{1,0:T(8,128)(2,1)}, u32[]{:S(2)}, u32[]{:S(2)}) collective-permute-start(bf16[512,1152]{1,0:T(8,128)(2,1)} %refs_4_.3), channel_id=1, source_target_pairs={{0,1},{1,0},{2,3},{3,2},{4,5},{5,4},{6,7},{7,6},{8,9},{9,8},{10,11... | collective-permute-start | bytes 3538952 | tf_op jit(solution)/shard_map/ppermute | solution.py:41
  4.5 26.8 %collective-permute-start.2 = (bf16[512,1152]{1,0:T(8,128)(2,1)}, bf16[512,1152]{1,0:T(8,128)(2,1)}, u32[]{:S(2)}, u32[]{:S(2)}) collective-permute-start(bf16[512,1152]{1,0:T(8,128)(2,1)} %get-tuple-element.157), channel_id=1, source_target_pairs={{0,28},{1,3},{2,1},{3,6},{4,0},{5,7},{6,5},{7,10},{8,4},{9,11},{10... | collective-permute-start | bytes 3538952 | tf_op jit(solution)/shard_map/ppermute | solution.py:532
  10.5 26.7 %collective-permute-start.3 = (bf16[512,1152]{1,0:T(8,128)(2,1)}, bf16[512,1152]{1,0:T(8,128)(2,1)}, u32[]{:S(2)}, u32[]{:S(2)}) collective-permute-start(bf16[512,1152]{1,0:T(8,128)(2,1)} %get-tuple-element.156), channel_id=1, source_target_pairs={{0,29},{1,2},{2,0},{3,7},{4,1},{5,6},{6,4},{7,11},{8,5},{9,10},{10... | collective-permute-start | bytes 3538952 | tf_op jit(solution)/shard_map/ppermute | solution.py:533
  12.8 9.4 %copy-start.8 = (s32[8]{0:T(128)S(1)}, s32[8]{0:T(128)}, u32[]{:S(2)}) copy-start(s32[8]{0:T(128)} %stack.35.place) | copy-start | bytes 100
  12.8 1.0 copy-start.4
  13.8 8.4 %copy-start = (bf16[1152,1152]{1,0:T(8,128)(2,1)S(1)}, bf16[1152,1152]{1,0:T(8,128)(2,1)}, u32[]{:S(2)}) copy-start(bf16[1152,1152]{1,0:T(8,128)(2,1)} %refs_5_.3) | copy-start | bytes 7962628
  13.8 8.4 %copy-start.1 = (bf16[1152,1152]{1,0:T(8,128)(2,1)S(1)}, bf16[1152,1152]{1,0:T(8,128)(2,1)}, u32[]{:S(2)}) copy-start(bf16[1152,1152]{1,0:T(8,128)(2,1)} %refs_4_.4) | copy-start | bytes 7962628
  22.2 1.3 copy-start.2
  23.4 1.3 copy-start.3
  24.7 1.3 copy-start.5
  26.0 11.2 %copy-start.7 = (bf16[512,1152]{1,0:T(8,128)(2,1)S(1)}, bf16[512,1152]{1,0:T(8,128)(2,1)}, u32[]{:S(2)}) copy-start(bf16[512,1152]{1,0:T(8,128)(2,1)} %get-tuple-element.97.met) | copy-start | bytes 3538948
  26.0 11.2 %copy-start.6 = (bf16[512,1152]{1,0:T(8,128)(2,1)S(1)}, bf16[512,1152]{1,0:T(8,128)(2,1)}, u32[]{:S(2)}) copy-start(bf16[512,1152]{1,0:T(8,128)(2,1)} %get-tuple-element.98.met_other) | copy-start | bytes 3538948
  37.1 28.9 %collective-permute-start.6 = (bf16[512,1152]{1,0:T(8,128)(2,1)S(1)}, bf16[512,1152]{1,0:T(8,128)(2,1)S(1)}, u32[]{:S(2)}, u32[]{:S(2)}) collective-permute-start(bf16[512,1152]{1,0:T(8,128)(2,1)S(1)} %copy-done.7), channel_id=1, source_target_pairs={{0,2},{1,3},{2,0},{3,1},{4,6},{5,7},{6,4},{7,5},{8,10},{9,11},{10,... | collective-permute-start | bytes 3538952 | tf_op jit(solution)/shard_map/ppermute | solution.py:41
  37.1 31.5 %collective-permute-start.7 = (bf16[512,1152]{1,0:T(8,128)(2,1)S(1)}, bf16[512,1152]{1,0:T(8,128)(2,1)S(1)}, u32[]{:S(2)}, u32[]{:S(2)}) collective-permute-start(bf16[512,1152]{1,0:T(8,128)(2,1)S(1)} %copy-done.6), channel_id=1, source_target_pairs={{0,4},{1,5},{2,30},{3,31},{4,8},{5,9},{6,2},{7,3},{8,12},{9,13},{1... | collective-permute-start | bytes 3538952 | tf_op jit(solution)/shard_map/ppermute | solution.py:37
  43.4 46.5 %collective-permute-start.5 = (bf16[512,1152]{1,0:T(8,128)(2,1)S(1)}, bf16[512,1152]{1,0:T(8,128)(2,1)S(1)}, u32[]{:S(2)}, u32[]{:S(2)}) collective-permute-start(bf16[512,1152]{1,0:T(8,128)(2,1)S(1)} %get-tuple-element.95.far_other), channel_id=1, source_target_pairs={{0,2},{1,3},{2,0},{3,1},{4,6},{5,7},{6,4},{7,5},{8,10},{9,11},{10,... | collective-permute-start | bytes 3538952 | tf_op jit(solution)/shard_map/ppermute | solution.py:41
  47.6 46.4 %collective-permute-start.4 = (bf16[512,1152]{1,0:T(8,128)(2,1)S(1)}, bf16[512,1152]{1,0:T(8,128)(2,1)S(1)}, u32[]{:S(2)}, u32[]{:S(2)}) collective-permute-start(bf16[512,1152]{1,0:T(8,128)(2,1)S(1)} %get-tuple-element.94.two), channel_id=1, source_target_pairs={{0,4},{1,5},{2,30},{3,31},{4,8},{5,9},{6,2},{7,3},{8,12},{9,13},{1... | collective-permute-start | bytes 3538952 | tf_op jit(solution)/shard_map/ppermute | solution.py:37
  100.1 12.3 %collective-permute-start.11 = (bf16[192,1152]{1,0:T(8,128)(2,1)S(1)}, bf16[192,1152]{1,0:T(8,128)(2,1)S(1)}, u32[]{:S(2)}, u32[]{:S(2)}) collective-permute-start(bf16[192,1152]{1,0:T(8,128)(2,1)S(1)} %get-tuple-element.109), channel_id=1, source_target_pairs={{0,8},{1,9},{2,10},{3,11},{4,12},{5,13},{6,14},{7,15},{8,0},{9,1},... | collective-permute-start | bytes 1327112 | tf_op jit(solution)/shard_map/ppermute | solution.py:41
  102.4 15.3 %collective-permute-start.10 = (bf16[192,1152]{1,0:T(8,128)(2,1)S(1)}, bf16[192,1152]{1,0:T(8,128)(2,1)S(1)}, u32[]{:S(2)}, u32[]{:S(2)}) collective-permute-start(bf16[192,1152]{1,0:T(8,128)(2,1)S(1)} %get-tuple-element.107), channel_id=1, source_target_pairs={{0,6},{1,7},{2,4},{3,5},{4,2},{5,3},{6,0},{7,1},{8,14},{9,15},{10,... | collective-permute-start | bytes 1327112 | tf_op jit(solution)/shard_map/ppermute | solution.py:41
  103.6 21.1 %collective-permute-start.8 = (bf16[192,1152]{1,0:T(8,128)(2,1)S(1)}, bf16[192,1152]{1,0:T(8,128)(2,1)S(1)}, u32[]{:S(2)}, u32[]{:S(2)}) collective-permute-start(bf16[192,1152]{1,0:T(8,128)(2,1)S(1)} %get-tuple-element.105), channel_id=1, source_target_pairs={{0,2},{1,3},{2,0},{3,1},{4,6},{5,7},{6,4},{7,5},{8,10},{9,11},{10,... | collective-permute-start | bytes 1327112 | tf_op jit(solution)/shard_map/ppermute | solution.py:41
  105.2 19.9 %collective-permute-start.9 = (bf16[192,1152]{1,0:T(8,128)(2,1)S(1)}, bf16[192,1152]{1,0:T(8,128)(2,1)S(1)}, u32[]{:S(2)}, u32[]{:S(2)}) collective-permute-start(bf16[192,1152]{1,0:T(8,128)(2,1)S(1)} %get-tuple-element.106), channel_id=1, source_target_pairs={{0,4},{1,5},{2,6},{3,7},{4,0},{5,1},{6,2},{7,3},{8,12},{9,13},{10,... | collective-permute-start | bytes 1327112 | tf_op jit(solution)/shard_map/ppermute | solution.py:41
  113.0 12.3 %collective-permute-start.12 = (bf16[96,1152]{1,0:T(8,128)(2,1)S(1)}, bf16[96,1152]{1,0:T(8,128)(2,1)S(1)}, u32[]{:S(2)}, u32[]{:S(2)}) collective-permute-start(bf16[96,1152]{1,0:T(8,128)(2,1)S(1)} %get-tuple-element.110), channel_id=1, source_target_pairs={{0,16},{1,17},{2,18},{3,19},{4,20},{5,21},{6,22},{7,23},{8,24},{9,... | collective-permute-start | bytes 663560 | tf_op jit(solution)/shard_map/ppermute | solution.py:41
  125.4 15.1 %collective-permute-start.19 = (bf16[512,1152]{1,0:T(8,128)(2,1)S(1)}, bf16[512,1152]{1,0:T(8,128)(2,1)S(1)}, u32[]{:S(2)}, u32[]{:S(2)}) collective-permute-start(bf16[512,1152]{1,0:T(8,128)(2,1)S(1)} %get-tuple-element.133), channel_id=1, source_target_pairs={{0,1},{1,0},{2,3},{3,2},{4,5},{5,4},{6,7},{7,6},{8,9},{9,8},{10,11... | collective-permute-start | bytes 3538952 | tf_op jit(solution)/shard_map/ppermute | solution.py:41
  126.4 6.3 %collective-permute-start.13 = (bf16[48,1152]{1,0:T(8,128)(2,1)S(1)}, bf16[48,1152]{1,0:T(8,128)(2,1)S(1)}, u32[]{:S(2)}, u32[]{:S(2)}) collective-permute-start(bf16[48,1152]{1,0:T(8,128)(2,1)S(1)} %get-tuple-element.121), channel_id=1, source_target_pairs={{0,8},{1,9},{2,10},{3,11},{4,12},{5,13},{6,14},{7,15},{8,0},{9,1},... | collective-permute-start | bytes 331784 | tf_op jit(solution)/shard_map/ppermute | solution.py:41
  127.9 8.4 %collective-permute-start.14 = (bf16[48,1152]{1,0:T(8,128)(2,1)S(1)}, bf16[48,1152]{1,0:T(8,128)(2,1)S(1)}, u32[]{:S(2)}, u32[]{:S(2)}) collective-permute-start(bf16[48,1152]{1,0:T(8,128)(2,1)S(1)} %get-tuple-element.122), channel_id=1, source_target_pairs={{0,16},{1,17},{2,18},{3,19},{4,20},{5,21},{6,22},{7,23},{8,24},{9,... | collective-permute-start | bytes 331784 | tf_op jit(solution)/shard_map/ppermute | solution.py:41
  128.8 7.5 %collective-permute-start.15 = (bf16[48,1152]{1,0:T(8,128)(2,1)S(1)}, bf16[48,1152]{1,0:T(8,128)(2,1)S(1)}, u32[]{:S(2)}, u32[]{:S(2)}) collective-permute-start(bf16[48,1152]{1,0:T(8,128)(2,1)S(1)} %get-tuple-element.123), channel_id=1, source_target_pairs={{0,2},{1,3},{2,0},{3,1},{4,6},{5,7},{6,4},{7,5},{8,10},{9,11},{10,... | collective-permute-start | bytes 331784 | tf_op jit(solution)/shard_map/ppermute | solution.py:41
  137.0 6.8 %collective-permute-start.16 = (bf16[48,1152]{1,0:T(8,128)(2,1)S(1)}, bf16[48,1152]{1,0:T(8,128)(2,1)S(1)}, u32[]{:S(2)}, u32[]{:S(2)}) collective-permute-start(bf16[48,1152]{1,0:T(8,128)(2,1)S(1)} %get-tuple-element.129.refs_0_), channel_id=1, source_target_pairs={{0,16},{1,17},{2,18},{3,19},{4,20},{5,21},{6,22},{7,23},{8,24},{9,... | collective-permute-start | bytes 331784 | tf_op jit(solution)/shard_map/ppermute | solution.py:41
  137.5 6.9 %collective-permute-start.17 = (bf16[48,1152]{1,0:T(8,128)(2,1)S(1)}, bf16[48,1152]{1,0:T(8,128)(2,1)S(1)}, u32[]{:S(2)}, u32[]{:S(2)}) collective-permute-start(bf16[48,1152]{1,0:T(8,128)(2,1)S(1)} %get-tuple-element.130.refs_2_), channel_id=1, source_target_pairs={{0,8},{1,9},{2,10},{3,11},{4,12},{5,13},{6,14},{7,15},{8,0},{9,1},... | collective-permute-start | bytes 331784 | tf_op jit(solution)/shard_map/ppermute | solution.py:41
  139.0 4.2 %collective-permute-start.18 = (bf16[24,1152]{1,0:T(8,128)(2,1)S(1)}, bf16[24,1152]{1,0:T(8,128)(2,1)S(1)}, u32[]{:S(2)}, u32[]{:S(2)}) collective-permute-start(bf16[24,1152]{1,0:T(8,128)(2,1)S(1)} %get-tuple-element.131), channel_id=1, source_target_pairs={{0,4},{1,5},{2,6},{3,7},{4,0},{5,1},{6,2},{7,3},{8,12},{9,13},{10,... | collective-permute-start | bytes 165896 | tf_op jit(solution)/shard_map/ppermute | solution.py:41
  144.9 4.9 %collective-permute-start.22 = (bf16[24,1152]{1,0:T(8,128)(2,1)S(1)}, bf16[24,1152]{1,0:T(8,128)(2,1)S(1)}, u32[]{:S(2)}, u32[]{:S(2)}) collective-permute-start(bf16[24,1152]{1,0:T(8,128)(2,1)S(1)} %get-tuple-element.144.refs_4_), channel_id=1, source_target_pairs={{0,4},{1,5},{2,6},{3,7},{4,0},{5,1},{6,2},{7,3},{8,12},{9,13},{10,... | collective-permute-start | bytes 165896 | tf_op jit(solution)/shard_map/ppermute | solution.py:41
  145.3 8.7 %collective-permute-start.20 = (bf16[48,1152]{1,0:T(8,128)(2,1)S(1)}, bf16[48,1152]{1,0:T(8,128)(2,1)S(1)}, u32[]{:S(2)}, u32[]{:S(2)}) collective-permute-start(bf16[48,1152]{1,0:T(8,128)(2,1)S(1)} %get-tuple-element.142.refs_0_), channel_id=1, source_target_pairs={{0,8},{1,9},{2,10},{3,11},{4,12},{5,13},{6,14},{7,15},{8,0},{9,1},... | collective-permute-start | bytes 331784 | tf_op jit(solution)/shard_map/ppermute | solution.py:41
  145.9 8.1 %collective-permute-start.21 = (bf16[48,1152]{1,0:T(8,128)(2,1)S(1)}, bf16[48,1152]{1,0:T(8,128)(2,1)S(1)}, u32[]{:S(2)}, u32[]{:S(2)}) collective-permute-start(bf16[48,1152]{1,0:T(8,128)(2,1)S(1)} %get-tuple-element.143.refs_2_), channel_id=1, source_target_pairs={{0,16},{1,17},{2,18},{3,19},{4,20},{5,21},{6,22},{7,23},{8,24},{9,... | collective-permute-start | bytes 331784 | tf_op jit(solution)/shard_map/ppermute | solution.py:41
  148.6 4.2 %collective-permute-start.23 = (bf16[24,1152]{1,0:T(8,128)(2,1)S(1)}, bf16[24,1152]{1,0:T(8,128)(2,1)S(1)}, u32[]{:S(2)}, u32[]{:S(2)}) collective-permute-start(bf16[24,1152]{1,0:T(8,128)(2,1)S(1)} %get-tuple-element.144.refs_4_), channel_id=1, source_target_pairs={{0,2},{1,3},{2,0},{3,1},{4,6},{5,7},{6,4},{7,5},{8,10},{9,11},{10,... | collective-permute-start | bytes 165896 | tf_op jit(solution)/shard_map/ppermute | solution.py:41
  149.9 4.2 %collective-permute-start.24 = (bf16[24,1152]{1,0:T(8,128)(2,1)S(1)}, bf16[24,1152]{1,0:T(8,128)(2,1)S(1)}, u32[]{:S(2)}, u32[]{:S(2)}) collective-permute-start(bf16[24,1152]{1,0:T(8,128)(2,1)S(1)} %collective-permute-done.22.refs_5_), channel_id=1, source_target_pairs={{0,2},{1,3},{2,0},{3,1},{4,6},{5,7},{6,4},{7,5},{8,10},{9,11},{10,... | collective-permute-start | bytes 165896 | tf_op jit(solution)/shard_map/ppermute | solution.py:41
  154.7 9.7 %collective-permute-start.28 = (bf16[96,1152]{1,0:T(8,128)(2,1)S(1)}, bf16[96,1152]{1,0:T(8,128)(2,1)S(1)}, u32[]{:S(2)}, u32[]{:S(2)}) collective-permute-start(bf16[96,1152]{1,0:T(8,128)(2,1)S(1)} %get-tuple-element.146.mine), channel_id=1, source_target_pairs={{0,16},{1,17},{2,18},{3,19},{4,20},{5,21},{6,22},{7,23},{8,24},{9,... | collective-permute-start | bytes 663560 | tf_op jit(solution)/shard_map/ppermute | solution.py:41
  155.2 13.1 %collective-permute-start.25 = (bf16[192,1152]{1,0:T(8,128)(2,1)S(1)}, bf16[192,1152]{1,0:T(8,128)(2,1)S(1)}, u32[]{:S(2)}, u32[]{:S(2)}) collective-permute-start(bf16[192,1152]{1,0:T(8,128)(2,1)S(1)} %get-tuple-element.147.refs_0_), channel_id=1, source_target_pairs={{0,2},{1,3},{2,0},{3,1},{4,6},{5,7},{6,4},{7,5},{8,10},{9,11},{10,... | collective-permute-start | bytes 1327112 | tf_op jit(solution)/shard_map/ppermute | solution.py:41
  156.3 18.8 %collective-permute-start.26 = (bf16[192,1152]{1,0:T(8,128)(2,1)S(1)}, bf16[192,1152]{1,0:T(8,128)(2,1)S(1)}, u32[]{:S(2)}, u32[]{:S(2)}) collective-permute-start(bf16[192,1152]{1,0:T(8,128)(2,1)S(1)} %get-tuple-element.147.refs_0_), channel_id=1, source_target_pairs={{0,4},{1,5},{2,6},{3,7},{4,0},{5,1},{6,2},{7,3},{8,12},{9,13},{10,... | collective-permute-start | bytes 1327112 | tf_op jit(solution)/shard_map/ppermute | solution.py:41
  157.0 18.1 %collective-permute-start.27 = (bf16[192,1152]{1,0:T(8,128)(2,1)S(1)}, bf16[192,1152]{1,0:T(8,128)(2,1)S(1)}, u32[]{:S(2)}, u32[]{:S(2)}) collective-permute-start(bf16[192,1152]{1,0:T(8,128)(2,1)S(1)} %get-tuple-element.147.refs_0_), channel_id=1, source_target_pairs={{0,6},{1,7},{2,4},{3,5},{4,2},{5,3},{6,0},{7,1},{8,14},{9,15},{10,... | collective-permute-start | bytes 1327112 | tf_op jit(solution)/shard_map/ppermute | solution.py:41
  165.1 10.7 %collective-permute-start.29 = (bf16[192,1152]{1,0:T(8,128)(2,1)S(1)}, bf16[192,1152]{1,0:T(8,128)(2,1)S(1)}, u32[]{:S(2)}, u32[]{:S(2)}) collective-permute-start(bf16[192,1152]{1,0:T(8,128)(2,1)S(1)} %b_join_high.1.refs_4_), channel_id=1, source_target_pairs={{0,8},{1,9},{2,10},{3,11},{4,12},{5,13},{6,14},{7,15},{8,0},{9,1},... | collective-permute-start | bytes 1327112 | tf_op jit(solution)/shard_map/ppermute | solution.py:41
  176.6 5.0 %collective-permute-start.30 = (bf16[1152,1152]{1,0:T(8,128)(2,1)S(1)}, bf16[1152,1152]{1,0:T(8,128)(2,1)S(1)}, u32[]{:S(2)}, u32[]{:S(2)}) collective-permute-start(bf16[1152,1152]{1,0:T(8,128)(2,1)S(1)} %join_all.1.weight), channel_id=1, source_target_pairs={{0,1},{1,0},{2,3},{3,2},{4,5},{5,4},{6,7},{7,6},{8,9},{9,8},{10,11... | collective-permute-start | bytes 7962632 | tf_op jit(solution)/shard_map/ppermute | solution.py:41

commit v4 on v3

--- a/solution.py
+++ b/solution.py
@@ -382,18 +382,13 @@
 
 
 def middle_two_kernel(place, *refs):
-    (keep_low, got_low, keep_high, got_high, keep, got), outs, total = refs[:6], refs[6:10], refs[10]
-    outs[0][...] = (keep_low[...] + got_low[...].astype(F32)).astype(BF16)
-    outs[1][...] = (keep_high[...] + got_high[...].astype(F32)).astype(BF16)
-    total[...] = keep[...] + got[...].astype(F32)
-    cut(place, Y, total, outs[2], outs[3])
+    for k in range(3):
+        refs[6 + k][...] = (refs[2 * k][...] + refs[2 * k + 1][...].astype(F32)).astype(BF16)
 
 
 def middle_two(place, arrays, name):
-    shape = arrays[0].shape
-    half = (shape[0] // 2, shape[1])
-    outs = [(shape, BF16), (shape, BF16), (half, F32), (half, BF16)]
-    return small_call(middle_two_kernel, place, arrays, outs, [shape], 3, name)
+    outs = [(array.shape, BF16) for array in arrays[::2]]
+    return small_call(middle_two_kernel, place, arrays, outs, [], 3, name)
 
 
 def middle_three_kernel(place, *refs):
@@ -407,25 +402,23 @@
 
 
 def middle_four_kernel(place, *refs):
-    (low, got_low, high, got_high), quarters = refs[:4], refs[4:8]
-    out, out_b, total, total_b = refs[8:]
+    (low, got_low, high, got_high), (mine, got) = refs[:4], refs[4:6]
+    out, out_b, total, total_b = refs[6:]
     height = low.shape[0]
     for m, piece in enumerate((low, got_low)):
         total[piece_at(place[Z_LOW], m, height), :] = piece[...].astype(F32)
     for m, piece in enumerate((high, got_high)):
         total[piece_at(place[Z_HIGH], m, height, 2 * height), :] = piece[...].astype(F32)
     out[...] = total[...].astype(BF16)
-    height = quarters[0].shape[0]
-    for k, piece in enumerate(quarters):
-        first = (place[X] ^ (k // 2)) * 2 * height
-        total_b[piece_at(place[Y], k % 2, height, first), :] = piece[...].astype(F32)
+    for m, piece in enumerate((mine, got)):
+        total_b[piece_at(place[X], m, mine.shape[0]), :] = piece[...].astype(F32)
     out_b[...] = total_b[...].astype(BF16)
 
 
-def middle_four(place, arrays, quarters, name):
-    shapes = [(4 * a[0].shape[0], a[0].shape[1]) for a in (arrays, quarters)]
+def middle_four(place, arrays, pair, name):
+    shapes = [(len(a) * a[0].shape[0], a[0].shape[1]) for a in (arrays, pair)]
     outs = [(shape, BF16) for shape in shapes]
-    return small_call(middle_four_kernel, place, [*arrays, *quarters], outs, shapes, 5, name)
+    return small_call(middle_four_kernel, place, [*arrays, *pair], outs, shapes, 5, name)
 
 
 def add_halve_kernel(bit, place, keep, got, mine, give, total):
@@ -616,11 +609,11 @@
     got_high, got_low = swap(give_high, size, far), swap(give_low, size, near)
     got_b = swap(give_b, size, x_bit[1])
     got_low, got_high, got_b = together((got_low, got_high, got_b))
-    low, high, keep_b, give_b = middle_two(
+    low, high, shard_b = middle_two(
         place, (keep_low, got_low, keep_high, got_high, keep_b, got_b), "middle_two"
     )
     got_low, got_high = swap(low, size, far), swap(high, size, near)
-    got_b = swap(give_b, size, y_bit[1])
+    got_b = swap(shard_b, size, y_bit[1])
     d_img_emb, d_txt_emb = pick(
         place, SIDE, (d_emb, d_emb_other), (d_emb_other, d_emb), "rows_pick"
     )
@@ -628,19 +621,15 @@
         (got_low, got_high, got_b, d_img_emb, d_txt_emb)
     )
     low, high, shard_b = middle_three(
-        place, (low, got_low, high, got_high, keep_b, got_b), "middle_three"
+        place, (low, got_low, high, got_high, shard_b, got_b), "middle_three"
     )
     if size > 32:
         groups = [[i for i in range(size) if i % 32 == k] for k in range(32)]
         low, high, shard_b = lax.psum((low, high, shard_b), "dp", axis_index_groups=groups)
     got_high, got_low = swap(high, size, far), swap(low, size, near)
-    got_y, got_x = swap(shard_b, size, y_bit[1]), swap(shard_b, size, x_bit[1])
-    got_xy = swap(got_y, size, x_bit[1])
+    got_b = swap(shard_b, size, x_bit[1])
     piece_a, shard_b = middle_four(
-        place,
-        (low, got_low, high, got_high),
-        (shard_b, got_y, got_x, got_xy),
-        "middle_four",
+        place, (low, got_low, high, got_high), (shard_b, got_b), "middle_four"
     )
     got_b = swap(shard_b, size, high_bit[1])
     parts_a = [piece_a, *exchange([piece_a] * 3, plane_masks)]

time: 185 us -> 184 us (level)
  starting transfers between devices: 32 us -> 29.6 us
    ppermute x27 -> x25, starting transfers between devices: 25.1 us -> 22.6 us  [swap(): return lax.ppermute(value, 'dp', [(i, i ^ mask) for i in range(size)])]
    ppermute x27 -> x25, waiting for transfers between devices: 64.7 us -> 65.7 us  [swap(): return lax.ppermute(value, 'dp', [(i, i ^ mask) for i in range(size)])]
  transfers between devices with their start and end apart: 31 -> 29, of which waited for: 21 -> 21; matrix products, arithmetic and copies ran while one was open for 2% -> 2% of each run, Pallas kernels for 31% -> 31%
where the time goes in v4:
time: 184 us; the launch traced here: 183 us
  waiting for transfers between devices  75 us (41%)
  Pallas kernels  67.7 us (37%)
  starting transfers between devices  29.6 us (16%)
  local copies, waits for them, and re-layouts  5.5 us (3%)
  other arithmetic  3.24 us (2%)
  between operations  2.43 us (1%)
    ppermute x25, waiting for transfers between devices, swap(): return lax.ppermute(value, 'dp', [(i, i ^ mask) for i in range(size)])  65.7 us
    ppermute x25, starting transfers between devices, swap(): return lax.ppermute(value, 'dp', [(i, i ^ mask) for i in range(size)])  22.6 us
    pallas_call x3, Pallas kernels, call_tiles(): pl.pallas_call(kernel, grid=(rows // TILE,), out_shape=jax.ShapeDtypeStru...  20.1 us
    pallas_call x2, Pallas kernels, met_units(): pl.pallas_call(functools.partial(met_kernel, own_chip), out_shape=(out, o...  14.5 us
    pallas_call x1, Pallas kernels, last_phase(): pl.pallas_call(last_phase_kernel, grid=(rows // TILE,), out_shape=(jax.Sh...  6.13 us
    pallas_call x2, Pallas kernels, widen(): pl.pallas_call(functools.partial(widen_kernel, own), out_shape=(out, out)...  6.06 us
    ppermute x1, starting transfers between devices, body(): got_one = lax.ppermute(raw_one, 'dp', raw_target(0, 1))  5.98 us
    ppermute x1, waiting for transfers between devices, body(): got_two = lax.ppermute(raw_two, 'dp', raw_target(1, 0))  5.86 us
  transfers between devices with their start and end apart: 29, of which 21 were waited for; matrix products, arithmetic and copies ran while one was open for 2% of the time, Pallas kernels for 31%

profile of v4, /device:TPU:0, one launch (start us, length us, event | category | flops | bytes accessed | tf_op | source)
XLA Modules:
  0.0 183.5 jit_solution(10894688846610947372)
XLA Ops:
  1.2 3.2 %broadcast_select_fusion = (bf16[512,1152]{1,0:T(8,128)(2,1)}, bf16[512,1152]{1,0:T(8,128)(2,1)}) fusion(bf16[512,1152]{1,0:T(8,128)(2,1)} %refs_1_, bf16[512,1152]{1,0:T(8,128)(2,1)} %refs_4_.3, pred[]{:T(512)S(6)} %eq.13), kind=kLoop, calls=%fused_computation | loop fusion | flops 1179648 | bytes 4718593 | tf_op jit(solution)/shard_map/jit(_where)/select_n | solution.py:524
  4.5 6.0 %collective-permute-start.2 = (bf16[512,1152]{1,0:T(8,128)(2,1)}, bf16[512,1152]{1,0:T(8,128)(2,1)}, u32[]{:S(2)}, u32[]{:S(2)}) collective-permute-start(bf16[512,1152]{1,0:T(8,128)(2,1)} %get-tuple-element.155), channel_id=1, source_target_pairs={{0,28},{1,3},{2,1},{3,6},{4,0},{5,7},{6,5},{7,10},{8,4},{9,11},{10... | collective-permute-start | bytes 3538952 | tf_op jit(solution)/shard_map/ppermute | solution.py:525
  10.5 0.9 collective-permute-start.3
  12.7 1.0 copy-done.4
  13.8 8.3 %own_met.1 = (bf16[512,1152]{1,0:T(8,128)(2,1)}, bf16[512,1152]{1,0:T(8,128)(2,1)}) custom-call(s32[8]{0:T(128)} %stack.35.place, bf16[512,1152]{1,0:T(8,128)(2,1)} %refs_4_.3, bf16[512,1152]{1,0:T(8,128)(2,1)} %collective-permute-done.1.refs_1_.refs_5_, bf16[512,1152]{1,0:T(8,128)(2,1)} %refs_1_, bf16[512,1152]{1,0:T(8,128)(2,1)} %copy-done.4, ...), custom_call_target="tpu_custom_call" | custom-call | tf_op jit(solution)/shard_map/own_met/pallas_call | solution.py:72
  22.1 1.3 copy-done.2
  23.4 1.3 copy-done.3
  24.7 1.3 copy-done.5
  25.9 5.3 %second_units.1 = (f32[1024,1152]{1,0:T(8,128)S(1)}, f32[1024,1]{1,0:T(8,128)S(1)}, bf16[1024,1152]{1,0:T(8,128)(2,1)S(1)}, bf16[1152,1152]{1,0:T(8,128)(2,1)S(1)}, bf16[1152,1024]{1,0:T(8,128)(2,1)S(1)}) custom-call(s32[8]{0:T(128)S(1)} %copy-done.8, bf16[1152,1152]{1,0:T(8,128)(2,1)S(1)} %copy-done, bf16[512,1152]{1,0:T(8,128)(2,1)S(1)} %copy-done.2, ...), custom_call_target="tpu_custom_call" | custom-call | tf_op jit(solution)/shard_map/second_units/pallas_call | solution.py:118
  31.3 5.9 %collective-permute-done.3.refs_0_.refs_3_ = bf16[512,1152]{1,0:T(8,128)(2,1)} collective-permute-done((bf16[512,1152]{1,0:T(8,128)(2,1)}, bf16[512,1152]{1,0:T(8,128)(2,1)}, u32[]{:S(2)}, u32[]{:S(2)}) %collective-permute-start.3) | collective-permute-done | bytes 1179680 | tf_op jit(solution)/shard_map/ppermute | solution.py:526
  37.2 6.2 %raw_met.1 = (bf16[512,1152]{1,0:T(8,128)(2,1)S(1)}, bf16[512,1152]{1,0:T(8,128)(2,1)S(1)}) custom-call(s32[8]{0:T(128)S(1)} %copy-done.8, bf16[512,1152]{1,0:T(8,128)(2,1)} %collective-permute-done.3.refs_0_.refs_3_, bf16[512,1152]{1,0:T(8,128)(2,1)} %collective-permute-done.2.refs_1_.refs_2_, bf16[512,1152]{1,0:T(8,128)(2,1)} %collective-permute-done.2.refs_1_.refs_2_, ...), custom_call_target="tpu_custom_call" | custom-call | tf_op jit(solution)/shard_map/raw_met/pallas_call | solution.py:72
  43.4 4.2 %collective-permute-start.5 = (bf16[512,1152]{1,0:T(8,128)(2,1)S(1)}, bf16[512,1152]{1,0:T(8,128)(2,1)S(1)}, u32[]{:S(2)}, u32[]{:S(2)}) collective-permute-start(bf16[512,1152]{1,0:T(8,128)(2,1)S(1)} %get-tuple-element.94.far_other), channel_id=1, source_target_pairs={{0,2},{1,3},{2,0},{3,1},{4,6},{5,7},{6,4},{7,5},{8,10},{9,11},{10,... | collective-permute-start | bytes 3538952 | tf_op jit(solution)/shard_map/ppermute | solution.py:41
  48.2 6.9 %own_chip.1.grad_in = f32[1024,1152]{1,0:T(8,128)S(1)} custom-call(f32[1]{0:T(128)S(6)} %exp.3.scale, f32[1]{0:T(128)S(6)} %copy.15.bias, bf16[1024,1152]{1,0:T(8,128)(2,1)S(1)} %get-tuple-element.95.z, bf16[512,1152]{1,0:T(8,128)(2,1)S(1)} %copy-done.7, bf16[512,1152]{1,0:T(8,128)(2,1)S(1)} %copy-done.6), custom_call_target="tpu_custom_call" | custom-call | tf_op jit(solution)/shard_map/own_chip/pallas_call | solution.py:220
  55.1 10.9 %collective-permute-done.6.one = bf16[512,1152]{1,0:T(8,128)(2,1)S(1)} collective-permute-done((bf16[512,1152]{1,0:T(8,128)(2,1)S(1)}, bf16[512,1152]{1,0:T(8,128)(2,1)S(1)}, u32[]{:S(2)}, u32[]{:S(2)}) %collective-permute-start.6) | collective-permute-done | bytes 1179680 | tf_op jit(solution)/shard_map/ppermute | solution.py:41
  66.0 2.6 %collective-permute-done.7.far_own = bf16[512,1152]{1,0:T(8,128)(2,1)S(1)} collective-permute-done((bf16[512,1152]{1,0:T(8,128)(2,1)S(1)}, bf16[512,1152]{1,0:T(8,128)(2,1)S(1)}, u32[]{:S(2)}, u32[]{:S(2)}) %collective-permute-start.7) | collective-permute-done | bytes 1179680 | tf_op jit(solution)/shard_map/ppermute | solution.py:37
  68.7 9.9 %first_phase.1.grad_in = f32[1024,1152]{1,0:T(8,128)S(1)} custom-call(f32[1]{0:T(128)S(6)} %exp.3.scale, f32[1]{0:T(128)S(6)} %copy.15.bias, bf16[1024,1152]{1,0:T(8,128)(2,1)S(1)} %get-tuple-element.95.z, bf16[512,1152]{1,0:T(8,128)(2,1)S(1)} %collective-permute-done.6.one, bf16[512,1152]{1,0:T(8,128)(2,1)S(1)} %get-tuple-element.93.two, ...), custom_call_target="tpu_custom_call" | custom-call | tf_op jit(solution)/shard_map/first_phase/pallas_call | solution.py:220
  78.6 11.3 %collective-permute-done.5.block = bf16[512,1152]{1,0:T(8,128)(2,1)S(1)} collective-permute-done((bf16[512,1152]{1,0:T(8,128)(2,1)S(1)}, bf16[512,1152]{1,0:T(8,128)(2,1)S(1)}, u32[]{:S(2)}, u32[]{:S(2)}) %collective-permute-start.5) | collective-permute-done | bytes 1179680 | tf_op jit(solution)/shard_map/ppermute | solution.py:41
  89.9 3.2 %relayed.1.grad_in = f32[1024,1152]{1,0:T(8,128)S(1)} custom-call(f32[1]{0:T(128)S(6)} %exp.3.scale, f32[1]{0:T(128)S(6)} %copy.15.bias, bf16[1024,1152]{1,0:T(8,128)(2,1)S(1)} %get-tuple-element.95.z, bf16[512,1152]{1,0:T(8,128)(2,1)S(1)} %collective-permute-done.5.block, f32[1024,1152]{1,0:T(8,128)S(1)} %first_phase.1.grad_in), custom_call_target="tpu_custom_call" | custom-call | tf_op jit(solution)/shard_map/relayed/pallas_call | solution.py:220
  93.9 6.1 %last_phase.1 = (bf16[1024,1152]{1,0:T(8,128)(2,1)S(1)}, bf16[192,1152]{1,0:T(8,128)(2,1)S(1)}) custom-call(s32[8]{0:T(128)S(1)} %copy-done.8, f32[1]{0:T(128)S(6)} %exp.3.scale, f32[1]{0:T(128)S(6)} %copy.15.bias, bf16[1024,1152]{1,0:T(8,128)(2,1)S(1)} %get-tuple-element.95.z, bf16[512,1152]{1,0:T(8,128)(2,1)S(1)} %collective-permute-done.4.block, ...), custom_call_target="tpu_custom_call" | custom-call | tf_op jit(solution)/shard_map/last_phase/pallas_call | solution.py:264
  100.2 2.3 %sent_parts.1 = (bf16[192,1152]{1,0:T(8,128)(2,1)S(1)}, bf16[192,1152]{1,0:T(8,128)(2,1)S(1)}, bf16[192,1152]{1,0:T(8,128)(2,1)S(1)}) custom-call(s32[8]{0:T(128)S(1)} %copy-done.8, bf16[1152,1024]{1,0:T(8,128)(2,1)S(1)} %get-tuple-element.87.emb_t, bf16[1024,1152]{1,0:T(8,128)(2,1)S(1)} %get-tuple-element.110.du), custom_call_target="tpu_custom_call" | custom-call | tf_op jit(solution)/shard_map/sent_parts/pallas_call | solution.py:308
  102.4 1.1 collective-permute-start.10
  103.6 1.6 collective-permute-start.8
  106.0 1.7 kept_parts.1
  107.7 4.6 %collective-permute-done.11.got = bf16[192,1152]{1,0:T(8,128)(2,1)S(1)} collective-permute-done((bf16[192,1152]{1,0:T(8,128)(2,1)S(1)}, bf16[192,1152]{1,0:T(8,128)(2,1)S(1)}, u32[]{:S(2)}, u32[]{:S(2)}) %collective-permute-start.11) | collective-permute-done | bytes 442400 | tf_op jit(solution)/shard_map/ppermute | solution.py:41
  113.1 4.6 %rows_back.1 = (bf16[512,1152]{1,0:T(8,128)(2,1)S(1)}, bf16[512,1152]{1,0:T(8,128)(2,1)S(1)}) custom-call(s32[8]{0:T(128)S(1)} %copy-done.8, bf16[1024,1152]{1,0:T(8,128)(2,1)S(1)} %get-tuple-element.110.du, bf16[1152,1152]{1,0:T(8,128)(2,1)S(1)} %get-tuple-element.111.weight), custom_call_target="tpu_custom_call" | custom-call | tf_op jit(solution)/shard_map/rows_back/pallas_call | solution.py:334
  117.7 6.9 %collective-permute-done.8.refs_1_ = bf16[192,1152]{1,0:T(8,128)(2,1)S(1)} collective-permute-done((bf16[192,1152]{1,0:T(8,128)(2,1)S(1)}, bf16[192,1152]{1,0:T(8,128)(2,1)S(1)}, u32[]{:S(2)}, u32[]{:S(2)}) %collective-permute-start.8) | collective-permute-done | bytes 442400 | tf_op jit(solution)/shard_map/ppermute | solution.py:41
  125.4 1.0 middle_one.1
  126.4 1.5 collective-permute-start.13
  127.9 0.9 collective-permute-start.14
  128.8 1.0 collective-permute-start.15
  129.8 2.9 %collective-permute-done.13.refs_1_ = bf16[48,1152]{1,0:T(8,128)(2,1)S(1)} collective-permute-done((bf16[48,1152]{1,0:T(8,128)(2,1)S(1)}, bf16[48,1152]{1,0:T(8,128)(2,1)S(1)}, u32[]{:S(2)}, u32[]{:S(2)}) %collective-permute-start.13) | collective-permute-done | bytes 110624 | tf_op jit(solution)/shard_map/ppermute | solution.py:41
  132.7 3.7 %collective-permute-done.14.refs_3_ = bf16[48,1152]{1,0:T(8,128)(2,1)S(1)} collective-permute-done((bf16[48,1152]{1,0:T(8,128)(2,1)S(1)}, bf16[48,1152]{1,0:T(8,128)(2,1)S(1)}, u32[]{:S(2)}, u32[]{:S(2)}) %collective-permute-start.14) | collective-permute-done | bytes 110624 | tf_op jit(solution)/shard_map/ppermute | solution.py:41
  137.4 1.5 collective-permute-start.17
  138.9 1.5 collective-permute-start.18
  140.5 2.0 %rows_pick.1 = (bf16[512,1152]{1,0:T(8,128)(2,1)}, bf16[512,1152]{1,0:T(8,128)(2,1)}) custom-call(s32[8]{0:T(128)S(1)} %copy-done.8, bf16[512,1152]{1,0:T(8,128)(2,1)S(1)} %get-tuple-element.131.refs_0_.refs_3_, bf16[512,1152]{1,0:T(8,128)(2,1)S(1)} %collective-permute-done.19.refs_1_.refs_2_, bf16[512,1152]{1,0:T(8,128)(2,1)S(1)} %collective-permute-done.19.refs_1_.refs_2_, ...), custom_call_target="tpu_custom_call" | custom-call | tf_op jit(solution)/shard_map/rows_pick/pallas_call | solution.py:159
  142.4 1.3 collective-permute-done.16.refs_1_
  145.1 2.3 %collective-permute-start.21 = (bf16[48,1152]{1,0:T(8,128)(2,1)S(1)}, bf16[48,1152]{1,0:T(8,128)(2,1)S(1)}, u32[]{:S(2)}, u32[]{:S(2)}) collective-permute-start(bf16[48,1152]{1,0:T(8,128)(2,1)S(1)} %get-tuple-element.141.refs_2_), channel_id=1, source_target_pairs={{0,16},{1,17},{2,18},{3,19},{4,20},{5,21},{6,22},{7,23},{8,24},{9,... | collective-permute-start | bytes 331784 | tf_op jit(solution)/shard_map/ppermute | solution.py:41
  148.1 2.7 %collective-permute-done.20.refs_1_ = bf16[48,1152]{1,0:T(8,128)(2,1)S(1)} collective-permute-done((bf16[48,1152]{1,0:T(8,128)(2,1)S(1)}, bf16[48,1152]{1,0:T(8,128)(2,1)S(1)}, u32[]{:S(2)}, u32[]{:S(2)}) %collective-permute-start.20) | collective-permute-done | bytes 110624 | tf_op jit(solution)/shard_map/ppermute | solution.py:41
  150.8 2.0 %collective-permute-done.21.refs_3_ = bf16[48,1152]{1,0:T(8,128)(2,1)S(1)} collective-permute-done((bf16[48,1152]{1,0:T(8,128)(2,1)S(1)}, bf16[48,1152]{1,0:T(8,128)(2,1)S(1)}, u32[]{:S(2)}, u32[]{:S(2)}) %collective-permute-start.21) | collective-permute-done | bytes 110624 | tf_op jit(solution)/shard_map/ppermute | solution.py:41
  154.5 1.8 collective-permute-start.24
  156.3 1.1 collective-permute-start.25
  157.4 5.6 %collective-permute-done.26.got = bf16[96,1152]{1,0:T(8,128)(2,1)S(1)} collective-permute-done((bf16[96,1152]{1,0:T(8,128)(2,1)S(1)}, bf16[96,1152]{1,0:T(8,128)(2,1)S(1)}, u32[]{:S(2)}, u32[]{:S(2)}) %collective-permute-start.26) | collective-permute-done | bytes 221216 | tf_op jit(solution)/shard_map/ppermute | solution.py:41
  163.8 3.2 %collective-permute-done.23.refs_1_ = bf16[192,1152]{1,0:T(8,128)(2,1)S(1)} collective-permute-done((bf16[192,1152]{1,0:T(8,128)(2,1)S(1)}, bf16[192,1152]{1,0:T(8,128)(2,1)S(1)}, u32[]{:S(2)}, u32[]{:S(2)}) %collective-permute-start.23) | collective-permute-done | bytes 442400 | tf_op jit(solution)/shard_map/ppermute | solution.py:41
  167.0 6.1 %collective-permute-done.24.refs_2_ = bf16[192,1152]{1,0:T(8,128)(2,1)S(1)} collective-permute-done((bf16[192,1152]{1,0:T(8,128)(2,1)S(1)}, bf16[192,1152]{1,0:T(8,128)(2,1)S(1)}, u32[]{:S(2)}, u32[]{:S(2)}) %collective-permute-start.24) | collective-permute-done | bytes 442400 | tf_op jit(solution)/shard_map/ppermute | solution.py:41
  173.1 0.9 collective-permute-done.25.refs_3_
  175.3 3.0 %widen_own.1 = (f32[1152,1152]{1,0:T(8,128)}, f32[1152,1152]{1,0:T(8,128)}) custom-call(s32[8]{0:T(128)S(1)} %copy-done.8, bf16[1152,1152]{1,0:T(8,128)(2,1)S(1)} %join_all.1.weight), custom_call_target="tpu_custom_call" | custom-call | tf_op jit(solution)/shard_map/widen_own/pallas_call | solution.py:487
  178.4 1.9 %collective-permute-done.28.weight = bf16[1152,1152]{1,0:T(8,128)(2,1)S(1)} collective-permute-done((bf16[1152,1152]{1,0:T(8,128)(2,1)S(1)}, bf16[1152,1152]{1,0:T(8,128)(2,1)S(1)}, u32[]{:S(2)}, u32[]{:S(2)}) %collective-permute-start.28) | collective-permute-done | bytes 2654240 | tf_op jit(solution)/shard_map/ppermute | solution.py:41
  180.3 3.0 %widen_other.1 = (f32[1152,1152]{1,0:T(8,128)}, f32[1152,1152]{1,0:T(8,128)}) custom-call(s32[8]{0:T(128)S(1)} %copy-done.8, bf16[1152,1152]{1,0:T(8,128)(2,1)S(1)} %collective-permute-done.28.weight, f32[1152,1152]{1,0:T(8,128)} %get-tuple-element.150.refs_0_, f32[1152,1152]{1,0:T(8,128)} %get-tuple-element.151.refs_1_), custom_call_target="tpu_custom_call", output_to_operand_aliasing={{0}: (2, {}), {1}: (3, {})} | custom-call | tf_op jit(solution)/shard_map/widen_other/pallas_call | solution.py:487
  (50 shorter events, 11.3 us)
Async XLA Ops:
  0.6 12.1 %collective-permute-start = (bf16[512,1152]{1,0:T(8,128)(2,1)}, bf16[512,1152]{1,0:T(8,128)(2,1)S(1)}, u32[]{:S(2)}, u32[]{:S(2)}) collective-permute-start(bf16[512,1152]{1,0:T(8,128)(2,1)} %refs_1_), channel_id=1, source_target_pairs={{0,1},{1,0},{2,3},{3,2},{4,5},{5,4},{6,7},{7,6},{8,9},{9,8},{10,11... | collective-permute-start | bytes 3538952 | tf_op jit(solution)/shard_map/ppermute | solution.py:41
  1.1 12.6 %collective-permute-start.1 = (bf16[512,1152]{1,0:T(8,128)(2,1)}, bf16[512,1152]{1,0:T(8,128)(2,1)}, u32[]{:S(2)}, u32[]{:S(2)}) collective-permute-start(bf16[512,1152]{1,0:T(8,128)(2,1)} %refs_4_.3), channel_id=1, source_target_pairs={{0,1},{1,0},{2,3},{3,2},{4,5},{5,4},{6,7},{7,6},{8,9},{9,8},{10,11... | collective-permute-start | bytes 3538952 | tf_op jit(solution)/shard_map/ppermute | solution.py:41
  4.5 26.8 %collective-permute-start.2 = (bf16[512,1152]{1,0:T(8,128)(2,1)}, bf16[512,1152]{1,0:T(8,128)(2,1)}, u32[]{:S(2)}, u32[]{:S(2)}) collective-permute-start(bf16[512,1152]{1,0:T(8,128)(2,1)} %get-tuple-element.155), channel_id=1, source_target_pairs={{0,28},{1,3},{2,1},{3,6},{4,0},{5,7},{6,5},{7,10},{8,4},{9,11},{10... | collective-permute-start | bytes 3538952 | tf_op jit(solution)/shard_map/ppermute | solution.py:525
  10.5 26.7 %collective-permute-start.3 = (bf16[512,1152]{1,0:T(8,128)(2,1)}, bf16[512,1152]{1,0:T(8,128)(2,1)}, u32[]{:S(2)}, u32[]{:S(2)}) collective-permute-start(bf16[512,1152]{1,0:T(8,128)(2,1)} %get-tuple-element.154), channel_id=1, source_target_pairs={{0,29},{1,2},{2,0},{3,7},{4,1},{5,6},{6,4},{7,11},{8,5},{9,10},{10... | collective-permute-start | bytes 3538952 | tf_op jit(solution)/shard_map/ppermute | solution.py:526
  12.7 9.4 %copy-start.8 = (s32[8]{0:T(128)S(1)}, s32[8]{0:T(128)}, u32[]{:S(2)}) copy-start(s32[8]{0:T(128)} %stack.35.place) | copy-start | bytes 100
  12.7 1.0 copy-start.4
  13.8 8.4 %copy-start = (bf16[1152,1152]{1,0:T(8,128)(2,1)S(1)}, bf16[1152,1152]{1,0:T(8,128)(2,1)}, u32[]{:S(2)}) copy-start(bf16[1152,1152]{1,0:T(8,128)(2,1)} %refs_5_.3) | copy-start | bytes 7962628
  13.8 8.4 %copy-start.1 = (bf16[1152,1152]{1,0:T(8,128)(2,1)S(1)}, bf16[1152,1152]{1,0:T(8,128)(2,1)}, u32[]{:S(2)}) copy-start(bf16[1152,1152]{1,0:T(8,128)(2,1)} %refs_4_.4) | copy-start | bytes 7962628
  22.1 1.3 copy-start.2
  23.4 1.3 copy-start.3
  24.7 1.3 copy-start.5
  25.9 11.2 %copy-start.7 = (bf16[512,1152]{1,0:T(8,128)(2,1)S(1)}, bf16[512,1152]{1,0:T(8,128)(2,1)}, u32[]{:S(2)}) copy-start(bf16[512,1152]{1,0:T(8,128)(2,1)} %get-tuple-element.96.met) | copy-start | bytes 3538948
  25.9 11.2 %copy-start.6 = (bf16[512,1152]{1,0:T(8,128)(2,1)S(1)}, bf16[512,1152]{1,0:T(8,128)(2,1)}, u32[]{:S(2)}) copy-start(bf16[512,1152]{1,0:T(8,128)(2,1)} %get-tuple-element.97.met_other) | copy-start | bytes 3538948
  37.1 28.9 %collective-permute-start.6 = (bf16[512,1152]{1,0:T(8,128)(2,1)S(1)}, bf16[512,1152]{1,0:T(8,128)(2,1)S(1)}, u32[]{:S(2)}, u32[]{:S(2)}) collective-permute-start(bf16[512,1152]{1,0:T(8,128)(2,1)S(1)} %copy-done.7), channel_id=1, source_target_pairs={{0,2},{1,3},{2,0},{3,1},{4,6},{5,7},{6,4},{7,5},{8,10},{9,11},{10,... | collective-permute-start | bytes 3538952 | tf_op jit(solution)/shard_map/ppermute | solution.py:41
  37.1 31.5 %collective-permute-start.7 = (bf16[512,1152]{1,0:T(8,128)(2,1)S(1)}, bf16[512,1152]{1,0:T(8,128)(2,1)S(1)}, u32[]{:S(2)}, u32[]{:S(2)}) collective-permute-start(bf16[512,1152]{1,0:T(8,128)(2,1)S(1)} %copy-done.6), channel_id=1, source_target_pairs={{0,4},{1,5},{2,30},{3,31},{4,8},{5,9},{6,2},{7,3},{8,12},{9,13},{1... | collective-permute-start | bytes 3538952 | tf_op jit(solution)/shard_map/ppermute | solution.py:37
  43.4 46.5 %collective-permute-start.5 = (bf16[512,1152]{1,0:T(8,128)(2,1)S(1)}, bf16[512,1152]{1,0:T(8,128)(2,1)S(1)}, u32[]{:S(2)}, u32[]{:S(2)}) collective-permute-start(bf16[512,1152]{1,0:T(8,128)(2,1)S(1)} %get-tuple-element.94.far_other), channel_id=1, source_target_pairs={{0,2},{1,3},{2,0},{3,1},{4,6},{5,7},{6,4},{7,5},{8,10},{9,11},{10,... | collective-permute-start | bytes 3538952 | tf_op jit(solution)/shard_map/ppermute | solution.py:41
  47.6 46.4 %collective-permute-start.4 = (bf16[512,1152]{1,0:T(8,128)(2,1)S(1)}, bf16[512,1152]{1,0:T(8,128)(2,1)S(1)}, u32[]{:S(2)}, u32[]{:S(2)}) collective-permute-start(bf16[512,1152]{1,0:T(8,128)(2,1)S(1)} %get-tuple-element.93.two), channel_id=1, source_target_pairs={{0,4},{1,5},{2,30},{3,31},{4,8},{5,9},{6,2},{7,3},{8,12},{9,13},{1... | collective-permute-start | bytes 3538952 | tf_op jit(solution)/shard_map/ppermute | solution.py:37
  100.1 12.3 %collective-permute-start.11 = (bf16[192,1152]{1,0:T(8,128)(2,1)S(1)}, bf16[192,1152]{1,0:T(8,128)(2,1)S(1)}, u32[]{:S(2)}, u32[]{:S(2)}) collective-permute-start(bf16[192,1152]{1,0:T(8,128)(2,1)S(1)} %get-tuple-element.108), channel_id=1, source_target_pairs={{0,8},{1,9},{2,10},{3,11},{4,12},{5,13},{6,14},{7,15},{8,0},{9,1},... | collective-permute-start | bytes 1327112 | tf_op jit(solution)/shard_map/ppermute | solution.py:41
  102.4 15.3 %collective-permute-start.10 = (bf16[192,1152]{1,0:T(8,128)(2,1)S(1)}, bf16[192,1152]{1,0:T(8,128)(2,1)S(1)}, u32[]{:S(2)}, u32[]{:S(2)}) collective-permute-start(bf16[192,1152]{1,0:T(8,128)(2,1)S(1)} %get-tuple-element.106), channel_id=1, source_target_pairs={{0,6},{1,7},{2,4},{3,5},{4,2},{5,3},{6,0},{7,1},{8,14},{9,15},{10,... | collective-permute-start | bytes 1327112 | tf_op jit(solution)/shard_map/ppermute | solution.py:41
  103.6 21.1 %collective-permute-start.8 = (bf16[192,1152]{1,0:T(8,128)(2,1)S(1)}, bf16[192,1152]{1,0:T(8,128)(2,1)S(1)}, u32[]{:S(2)}, u32[]{:S(2)}) collective-permute-start(bf16[192,1152]{1,0:T(8,128)(2,1)S(1)} %get-tuple-element.104), channel_id=1, source_target_pairs={{0,2},{1,3},{2,0},{3,1},{4,6},{5,7},{6,4},{7,5},{8,10},{9,11},{10,... | collective-permute-start | bytes 1327112 | tf_op jit(solution)/shard_map/ppermute | solution.py:41
  105.2 19.9 %collective-permute-start.9 = (bf16[192,1152]{1,0:T(8,128)(2,1)S(1)}, bf16[192,1152]{1,0:T(8,128)(2,1)S(1)}, u32[]{:S(2)}, u32[]{:S(2)}) collective-permute-start(bf16[192,1152]{1,0:T(8,128)(2,1)S(1)} %get-tuple-element.105), channel_id=1, source_target_pairs={{0,4},{1,5},{2,6},{3,7},{4,0},{5,1},{6,2},{7,3},{8,12},{9,13},{10,... | collective-permute-start | bytes 1327112 | tf_op jit(solution)/shard_map/ppermute | solution.py:41
  113.0 12.3 %collective-permute-start.12 = (bf16[96,1152]{1,0:T(8,128)(2,1)S(1)}, bf16[96,1152]{1,0:T(8,128)(2,1)S(1)}, u32[]{:S(2)}, u32[]{:S(2)}) collective-permute-start(bf16[96,1152]{1,0:T(8,128)(2,1)S(1)} %get-tuple-element.109), channel_id=1, source_target_pairs={{0,16},{1,17},{2,18},{3,19},{4,20},{5,21},{6,22},{7,23},{8,24},{9,... | collective-permute-start | bytes 663560 | tf_op jit(solution)/shard_map/ppermute | solution.py:41
  125.4 15.1 %collective-permute-start.19 = (bf16[512,1152]{1,0:T(8,128)(2,1)S(1)}, bf16[512,1152]{1,0:T(8,128)(2,1)S(1)}, u32[]{:S(2)}, u32[]{:S(2)}) collective-permute-start(bf16[512,1152]{1,0:T(8,128)(2,1)S(1)} %get-tuple-element.132), channel_id=1, source_target_pairs={{0,1},{1,0},{2,3},{3,2},{4,5},{5,4},{6,7},{7,6},{8,9},{9,8},{10,11... | collective-permute-start | bytes 3538952 | tf_op jit(solution)/shard_map/ppermute | solution.py:41
  126.4 6.3 %collective-permute-start.13 = (bf16[48,1152]{1,0:T(8,128)(2,1)S(1)}, bf16[48,1152]{1,0:T(8,128)(2,1)S(1)}, u32[]{:S(2)}, u32[]{:S(2)}) collective-permute-start(bf16[48,1152]{1,0:T(8,128)(2,1)S(1)} %get-tuple-element.120), channel_id=1, source_target_pairs={{0,8},{1,9},{2,10},{3,11},{4,12},{5,13},{6,14},{7,15},{8,0},{9,1},... | collective-permute-start | bytes 331784 | tf_op jit(solution)/shard_map/ppermute | solution.py:41
  127.9 8.4 %collective-permute-start.14 = (bf16[48,1152]{1,0:T(8,128)(2,1)S(1)}, bf16[48,1152]{1,0:T(8,128)(2,1)S(1)}, u32[]{:S(2)}, u32[]{:S(2)}) collective-permute-start(bf16[48,1152]{1,0:T(8,128)(2,1)S(1)} %get-tuple-element.121), channel_id=1, source_target_pairs={{0,16},{1,17},{2,18},{3,19},{4,20},{5,21},{6,22},{7,23},{8,24},{9,... | collective-permute-start | bytes 331784 | tf_op jit(solution)/shard_map/ppermute | solution.py:41
  128.8 7.5 %collective-permute-start.15 = (bf16[48,1152]{1,0:T(8,128)(2,1)S(1)}, bf16[48,1152]{1,0:T(8,128)(2,1)S(1)}, u32[]{:S(2)}, u32[]{:S(2)}) collective-permute-start(bf16[48,1152]{1,0:T(8,128)(2,1)S(1)} %get-tuple-element.122), channel_id=1, source_target_pairs={{0,2},{1,3},{2,0},{3,1},{4,6},{5,7},{6,4},{7,5},{8,10},{9,11},{10,... | collective-permute-start | bytes 331784 | tf_op jit(solution)/shard_map/ppermute | solution.py:41
  137.0 6.8 %collective-permute-start.16 = (bf16[48,1152]{1,0:T(8,128)(2,1)S(1)}, bf16[48,1152]{1,0:T(8,128)(2,1)S(1)}, u32[]{:S(2)}, u32[]{:S(2)}) collective-permute-start(bf16[48,1152]{1,0:T(8,128)(2,1)S(1)} %get-tuple-element.128.refs_0_), channel_id=1, source_target_pairs={{0,16},{1,17},{2,18},{3,19},{4,20},{5,21},{6,22},{7,23},{8,24},{9,... | collective-permute-start | bytes 331784 | tf_op jit(solution)/shard_map/ppermute | solution.py:41
  137.4 6.9 %collective-permute-start.17 = (bf16[48,1152]{1,0:T(8,128)(2,1)S(1)}, bf16[48,1152]{1,0:T(8,128)(2,1)S(1)}, u32[]{:S(2)}, u32[]{:S(2)}) collective-permute-start(bf16[48,1152]{1,0:T(8,128)(2,1)S(1)} %get-tuple-element.129.refs_2_), channel_id=1, source_target_pairs={{0,8},{1,9},{2,10},{3,11},{4,12},{5,13},{6,14},{7,15},{8,0},{9,1},... | collective-permute-start | bytes 331784 | tf_op jit(solution)/shard_map/ppermute | solution.py:41
  138.9 5.4 %collective-permute-start.18 = (bf16[48,1152]{1,0:T(8,128)(2,1)S(1)}, bf16[48,1152]{1,0:T(8,128)(2,1)S(1)}, u32[]{:S(2)}, u32[]{:S(2)}) collective-permute-start(bf16[48,1152]{1,0:T(8,128)(2,1)S(1)} %get-tuple-element.130.refs_4_), channel_id=1, source_target_pairs={{0,4},{1,5},{2,6},{3,7},{4,0},{5,1},{6,2},{7,3},{8,12},{9,13},{10,... | collective-permute-start | bytes 331784 | tf_op jit(solution)/shard_map/ppermute | solution.py:41
  144.9 5.8 %collective-permute-start.20 = (bf16[48,1152]{1,0:T(8,128)(2,1)S(1)}, bf16[48,1152]{1,0:T(8,128)(2,1)S(1)}, u32[]{:S(2)}, u32[]{:S(2)}) collective-permute-start(bf16[48,1152]{1,0:T(8,128)(2,1)S(1)} %get-tuple-element.140.refs_0_), channel_id=1, source_target_pairs={{0,8},{1,9},{2,10},{3,11},{4,12},{5,13},{6,14},{7,15},{8,0},{9,1},... | collective-permute-start | bytes 331784 | tf_op jit(solution)/shard_map/ppermute | solution.py:41
  145.1 7.6 %collective-permute-start.21 = (bf16[48,1152]{1,0:T(8,128)(2,1)S(1)}, bf16[48,1152]{1,0:T(8,128)(2,1)S(1)}, u32[]{:S(2)}, u32[]{:S(2)}) collective-permute-start(bf16[48,1152]{1,0:T(8,128)(2,1)S(1)} %get-tuple-element.141.refs_2_), channel_id=1, source_target_pairs={{0,16},{1,17},{2,18},{3,19},{4,20},{5,21},{6,22},{7,23},{8,24},{9,... | collective-permute-start | bytes 331784 | tf_op jit(solution)/shard_map/ppermute | solution.py:41
  147.5 5.3 %collective-permute-start.22 = (bf16[48,1152]{1,0:T(8,128)(2,1)S(1)}, bf16[48,1152]{1,0:T(8,128)(2,1)S(1)}, u32[]{:S(2)}, u32[]{:S(2)}) collective-permute-start(bf16[48,1152]{1,0:T(8,128)(2,1)S(1)} %get-tuple-element.142.refs_4_), channel_id=1, source_target_pairs={{0,2},{1,3},{2,0},{3,1},{4,6},{5,7},{6,4},{7,5},{8,10},{9,11},{10,... | collective-permute-start | bytes 331784 | tf_op jit(solution)/shard_map/ppermute | solution.py:41
  153.5 9.6 %collective-permute-start.26 = (bf16[96,1152]{1,0:T(8,128)(2,1)S(1)}, bf16[96,1152]{1,0:T(8,128)(2,1)S(1)}, u32[]{:S(2)}, u32[]{:S(2)}) collective-permute-start(bf16[96,1152]{1,0:T(8,128)(2,1)S(1)} %get-tuple-element.144.mine), channel_id=1, source_target_pairs={{0,16},{1,17},{2,18},{3,19},{4,20},{5,21},{6,22},{7,23},{8,24},{9,... | collective-permute-start | bytes 663560 | tf_op jit(solution)/shard_map/ppermute | solution.py:41
  153.9 13.1 %collective-permute-start.23 = (bf16[192,1152]{1,0:T(8,128)(2,1)S(1)}, bf16[192,1152]{1,0:T(8,128)(2,1)S(1)}, u32[]{:S(2)}, u32[]{:S(2)}) collective-permute-start(bf16[192,1152]{1,0:T(8,128)(2,1)S(1)} %get-tuple-element.145.refs_0_), channel_id=1, source_target_pairs={{0,2},{1,3},{2,0},{3,1},{4,6},{5,7},{6,4},{7,5},{8,10},{9,11},{10,... | collective-permute-start | bytes 1327112 | tf_op jit(solution)/shard_map/ppermute | solution.py:41
  154.5 18.6 %collective-permute-start.24 = (bf16[192,1152]{1,0:T(8,128)(2,1)S(1)}, bf16[192,1152]{1,0:T(8,128)(2,1)S(1)}, u32[]{:S(2)}, u32[]{:S(2)}) collective-permute-start(bf16[192,1152]{1,0:T(8,128)(2,1)S(1)} %get-tuple-element.145.refs_0_), channel_id=1, source_target_pairs={{0,4},{1,5},{2,6},{3,7},{4,0},{5,1},{6,2},{7,3},{8,12},{9,13},{10,... | collective-permute-start | bytes 1327112 | tf_op jit(solution)/shard_map/ppermute | solution.py:41
  156.3 17.7 %collective-permute-start.25 = (bf16[192,1152]{1,0:T(8,128)(2,1)S(1)}, bf16[192,1152]{1,0:T(8,128)(2,1)S(1)}, u32[]{:S(2)}, u32[]{:S(2)}) collective-permute-start(bf16[192,1152]{1,0:T(8,128)(2,1)S(1)} %get-tuple-element.145.refs_0_), channel_id=1, source_target_pairs={{0,6},{1,7},{2,4},{3,5},{4,2},{5,3},{6,0},{7,1},{8,14},{9,15},{10,... | collective-permute-start | bytes 1327112 | tf_op jit(solution)/shard_map/ppermute | solution.py:41
  163.7 10.8 %collective-permute-start.27 = (bf16[192,1152]{1,0:T(8,128)(2,1)S(1)}, bf16[192,1152]{1,0:T(8,128)(2,1)S(1)}, u32[]{:S(2)}, u32[]{:S(2)}) collective-permute-start(bf16[192,1152]{1,0:T(8,128)(2,1)S(1)} %b_join_high.1.refs_4_), channel_id=1, source_target_pairs={{0,8},{1,9},{2,10},{3,11},{4,12},{5,13},{6,14},{7,15},{8,0},{9,1},... | collective-permute-start | bytes 1327112 | tf_op jit(solution)/shard_map/ppermute | solution.py:41
  175.2 5.0 %collective-permute-start.28 = (bf16[1152,1152]{1,0:T(8,128)(2,1)S(1)}, bf16[1152,1152]{1,0:T(8,128)(2,1)S(1)}, u32[]{:S(2)}, u32[]{:S(2)}) collective-permute-start(bf16[1152,1152]{1,0:T(8,128)(2,1)S(1)} %join_all.1.weight), channel_id=1, source_target_pairs={{0,1},{1,0},{2,3},{3,2},{4,5},{5,4},{6,7},{7,6},{8,9},{9,8},{10,11... | collective-permute-start | bytes 7962632 | tf_op jit(solution)/shard_map/ppermute | solution.py:41

commit v5 on v4

--- a/solution.py
+++ b/solution.py
@@ -402,7 +402,7 @@
 
 
 def middle_four_kernel(place, *refs):
-    (low, got_low, high, got_high), (mine, got) = refs[:4], refs[4:6]
+    (high, got_high, low, got_low), (mine, got) = refs[:4], refs[4:6]
     out, out_b, total, total_b = refs[6:]
     height = low.shape[0]
     for m, piece in enumerate((low, got_low)):
@@ -534,7 +534,7 @@
         img_proj,
         txt_proj,
         True,
-        58,
+        30,
         "own_met",
     )
     img_emb, txt_emb, img_other, txt_other, _ = lax.optimization_barrier(
@@ -606,11 +606,11 @@
     keep_low, give_low, keep_high, give_high, keep_b, give_b = middle_one(
         place, parts_a, keep_b, got_b, "middle_one"
     )
-    got_high, got_low = swap(give_high, size, far), swap(give_low, size, near)
+    got_low, got_high = swap(give_low, size, near), swap(give_high, size, far)
     got_b = swap(give_b, size, x_bit[1])
     got_low, got_high, got_b = together((got_low, got_high, got_b))
-    low, high, shard_b = middle_two(
-        place, (keep_low, got_low, keep_high, got_high, keep_b, got_b), "middle_two"
+    high, low, shard_b = middle_two(
+        place, (keep_high, got_high, keep_low, got_low, keep_b, got_b), "middle_two"
     )
     got_low, got_high = swap(low, size, far), swap(high, size, near)
     got_b = swap(shard_b, size, y_bit[1])
@@ -629,7 +629,7 @@
     got_high, got_low = swap(high, size, far), swap(low, size, near)
     got_b = swap(shard_b, size, x_bit[1])
     piece_a, shard_b = middle_four(
-        place, (low, got_low, high, got_high), (shard_b, got_b), "middle_four"
+        place, (high, got_high, low, got_low), (shard_b, got_b), "middle_four"
     )
     got_b = swap(shard_b, size, high_bit[1])
     parts_a = [piece_a, *exchange([piece_a] * 3, plane_masks)]

time: 184 us -> 184 us (level)
    ppermute x1, waiting for transfers between devices: 5.86 us -> 7.96 us  [body(): got_two = lax.ppermute(raw_two, 'dp', raw_target(1, 0))]
    pallas_call x2, Pallas kernels: 14.5 us -> 12.4 us  [met_units(): pl.pallas_call(functools.partial(met_kernel, own_chip), out_shape=(out, o...]
    unnamed x18 -> x10, local copies, waits for them, and re-layouts: 4.84 us -> 4.29 us
  transfers between devices with their start and end apart: 29 -> 29, of which waited for: 21 -> 20; matrix products, arithmetic and copies ran while one was open for 2% -> 2% of each run, Pallas kernels for 31% -> 30%
where the time goes in v5:
time: 184 us; the launch traced here: 183 us
  waiting for transfers between devices  76.7 us (42%)
  Pallas kernels  66.4 us (36%)
  starting transfers between devices  30.2 us (16%)
  local copies, waits for them, and re-layouts  4.38 us (2%)
  other arithmetic  3.39 us (2%)
  between operations  2.42 us (1%)
    ppermute x25, waiting for transfers between devices, swap(): return lax.ppermute(value, 'dp', [(i, i ^ mask) for i in range(size)])  65.5 us
    ppermute x25, starting transfers between devices, swap(): return lax.ppermute(value, 'dp', [(i, i ^ mask) for i in range(size)])  23.2 us
    pallas_call x3, Pallas kernels, call_tiles(): pl.pallas_call(kernel, grid=(rows // TILE,), out_shape=jax.ShapeDtypeStru...  19.9 us
    pallas_call x2, Pallas kernels, met_units(): pl.pallas_call(functools.partial(met_kernel, own_chip), out_shape=(out, o...  12.4 us
    ppermute x1, waiting for transfers between devices, body(): got_two = lax.ppermute(raw_two, 'dp', raw_target(1, 0))  7.96 us
    pallas_call x1, Pallas kernels, second_units(): pl.pallas_call(second_kernel, out_shape=(jax.ShapeDtypeStruct((2 * rows,...  6.36 us
    pallas_call x2, Pallas kernels, widen(): pl.pallas_call(functools.partial(widen_kernel, own), out_shape=(out, out)...  6.06 us
    pallas_call x1, Pallas kernels, last_phase(): pl.pallas_call(last_phase_kernel, grid=(rows // TILE,), out_shape=(jax.Sh...  6.02 us
  transfers between devices with their start and end apart: 29, of which 20 were waited for; matrix products, arithmetic and copies ran while one was open for 2% of the time, Pallas kernels for 30%

profile of v5, /device:TPU:0, one launch (start us, length us, event | category | flops | bytes accessed | tf_op | source)
XLA Modules:
  0.0 183.4 jit_solution(4205179520287485948)
XLA Ops:
  1.2 3.4 %broadcast_select_fusion = (bf16[512,1152]{1,0:T(8,128)(2,1)}, bf16[512,1152]{1,0:T(8,128)(2,1)}) fusion(bf16[512,1152]{1,0:T(8,128)(2,1)} %refs_1_, bf16[512,1152]{1,0:T(8,128)(2,1)} %refs_4_.3, pred[]{:T(512)S(6)} %eq.13), kind=kLoop, calls=%fused_computation | loop fusion | flops 1179648 | bytes 4718593 | tf_op jit(solution)/shard_map/jit(_where)/select_n | solution.py:524
  4.6 6.0 %collective-permute-start.2 = (bf16[512,1152]{1,0:T(8,128)(2,1)}, bf16[512,1152]{1,0:T(8,128)(2,1)}, u32[]{:S(2)}, u32[]{:S(2)}) collective-permute-start(bf16[512,1152]{1,0:T(8,128)(2,1)} %get-tuple-element.155), channel_id=1, source_target_pairs={{0,28},{1,3},{2,1},{3,6},{4,0},{5,7},{6,5},{7,10},{8,4},{9,11},{10... | collective-permute-start | bytes 3538952 | tf_op jit(solution)/shard_map/ppermute | solution.py:525
  10.6 0.9 collective-permute-start.3
  12.3 1.7 copy-done.1
  14.1 1.3 copy-done.3
  15.4 1.3 copy-done.4
  16.6 6.3 %own_met.1 = (bf16[512,1152]{1,0:T(8,128)(2,1)S(1)}, bf16[512,1152]{1,0:T(8,128)(2,1)S(1)}) custom-call(s32[8]{0:T(128)S(1)} %stack.35.place, bf16[512,1152]{1,0:T(8,128)(2,1)S(1)} %copy-done.4, bf16[512,1152]{1,0:T(8,128)(2,1)} %collective-permute-done.1.refs_1_.refs_5_, bf16[512,1152]{1,0:T(8,128)(2,1)S(1)} %copy-done.3, ...), custom_call_target="tpu_custom_call" | custom-call | tf_op jit(solution)/shard_map/own_met/pallas_call | solution.py:72
  22.9 6.4 %second_units.1 = (f32[1024,1152]{1,0:T(8,128)S(1)}, f32[1024,1]{1,0:T(8,128)S(1)}, bf16[1024,1152]{1,0:T(8,128)(2,1)S(1)}, bf16[1152,1152]{1,0:T(8,128)(2,1)S(1)}, bf16[1152,1024]{1,0:T(8,128)(2,1)S(1)}) custom-call(s32[8]{0:T(128)S(1)} %stack.35.place, bf16[1152,1152]{1,0:T(8,128)(2,1)S(1)} %copy-done, bf16[512,1152]{1,0:T(8,128)(2,1)S(1)} %copy-done.3, ...), custom_call_target="tpu_custom_call" | custom-call | tf_op jit(solution)/shard_map/second_units/pallas_call | solution.py:118
  29.3 8.0 %collective-permute-done.3.refs_0_.refs_3_ = bf16[512,1152]{1,0:T(8,128)(2,1)} collective-permute-done((bf16[512,1152]{1,0:T(8,128)(2,1)}, bf16[512,1152]{1,0:T(8,128)(2,1)}, u32[]{:S(2)}, u32[]{:S(2)}) %collective-permute-start.3) | collective-permute-done | bytes 1179680 | tf_op jit(solution)/shard_map/ppermute | solution.py:526
  37.3 6.1 %raw_met.1 = (bf16[512,1152]{1,0:T(8,128)(2,1)S(1)}, bf16[512,1152]{1,0:T(8,128)(2,1)S(1)}) custom-call(s32[8]{0:T(128)S(1)} %stack.35.place, bf16[512,1152]{1,0:T(8,128)(2,1)} %collective-permute-done.3.refs_0_.refs_3_, bf16[512,1152]{1,0:T(8,128)(2,1)} %collective-permute-done.2.refs_1_.refs_2_, bf16[512,1152]{1,0:T(8,128)(2,1)} %collective-permute-done.2.refs_1_.refs_2_, ...), custom_call_target="tpu_custom_call" | custom-call | tf_op jit(solution)/shard_map/raw_met/pallas_call | solution.py:72
  43.5 4.2 %collective-permute-start.5 = (bf16[512,1152]{1,0:T(8,128)(2,1)S(1)}, bf16[512,1152]{1,0:T(8,128)(2,1)S(1)}, u32[]{:S(2)}, u32[]{:S(2)}) collective-permute-start(bf16[512,1152]{1,0:T(8,128)(2,1)S(1)} %get-tuple-element.94.far_other), channel_id=1, source_target_pairs={{0,2},{1,3},{2,0},{3,1},{4,6},{5,7},{6,4},{7,5},{8,10},{9,11},{10,... | collective-permute-start | bytes 3538952 | tf_op jit(solution)/shard_map/ppermute | solution.py:41
  48.4 6.8 %own_chip.1.grad_in = f32[1024,1152]{1,0:T(8,128)S(1)} custom-call(f32[1]{0:T(128)S(6)} %exp.3.scale, f32[1]{0:T(128)S(6)} %copy.15.bias, bf16[1024,1152]{1,0:T(8,128)(2,1)S(1)} %get-tuple-element.95.z, bf16[512,1152]{1,0:T(8,128)(2,1)S(1)} %get-tuple-element.96.met, bf16[512,1152]{1,0:T(8,128)(2,1)S(1)} %get-tuple-element.97.met_other), custom_call_target="tpu_custom_call" | custom-call | tf_op jit(solution)/shard_map/own_chip/pallas_call | solution.py:220
  55.2 11.0 %collective-permute-done.6.one = bf16[512,1152]{1,0:T(8,128)(2,1)S(1)} collective-permute-done((bf16[512,1152]{1,0:T(8,128)(2,1)S(1)}, bf16[512,1152]{1,0:T(8,128)(2,1)S(1)}, u32[]{:S(2)}, u32[]{:S(2)}) %collective-permute-start.6) | collective-permute-done | bytes 1179680 | tf_op jit(solution)/shard_map/ppermute | solution.py:41
  66.2 2.5 %collective-permute-done.7.far_own = bf16[512,1152]{1,0:T(8,128)(2,1)S(1)} collective-permute-done((bf16[512,1152]{1,0:T(8,128)(2,1)S(1)}, bf16[512,1152]{1,0:T(8,128)(2,1)S(1)}, u32[]{:S(2)}, u32[]{:S(2)}) %collective-permute-start.7) | collective-permute-done | bytes 1179680 | tf_op jit(solution)/shard_map/ppermute | solution.py:37
  68.7 9.9 %first_phase.1.grad_in = f32[1024,1152]{1,0:T(8,128)S(1)} custom-call(f32[1]{0:T(128)S(6)} %exp.3.scale, f32[1]{0:T(128)S(6)} %copy.15.bias, bf16[1024,1152]{1,0:T(8,128)(2,1)S(1)} %get-tuple-element.95.z, bf16[512,1152]{1,0:T(8,128)(2,1)S(1)} %collective-permute-done.6.one, bf16[512,1152]{1,0:T(8,128)(2,1)S(1)} %get-tuple-element.93.two, ...), custom_call_target="tpu_custom_call" | custom-call | tf_op jit(solution)/shard_map/first_phase/pallas_call | solution.py:220
  78.6 11.4 %collective-permute-done.5.block = bf16[512,1152]{1,0:T(8,128)(2,1)S(1)} collective-permute-done((bf16[512,1152]{1,0:T(8,128)(2,1)S(1)}, bf16[512,1152]{1,0:T(8,128)(2,1)S(1)}, u32[]{:S(2)}, u32[]{:S(2)}) %collective-permute-start.5) | collective-permute-done | bytes 1179680 | tf_op jit(solution)/shard_map/ppermute | solution.py:41
  90.1 3.2 %relayed.1.grad_in = f32[1024,1152]{1,0:T(8,128)S(1)} custom-call(f32[1]{0:T(128)S(6)} %exp.3.scale, f32[1]{0:T(128)S(6)} %copy.15.bias, bf16[1024,1152]{1,0:T(8,128)(2,1)S(1)} %get-tuple-element.95.z, bf16[512,1152]{1,0:T(8,128)(2,1)S(1)} %collective-permute-done.5.block, f32[1024,1152]{1,0:T(8,128)S(1)} %first_phase.1.grad_in), custom_call_target="tpu_custom_call" | custom-call | tf_op jit(solution)/shard_map/relayed/pallas_call | solution.py:220
  94.0 6.0 %last_phase.1 = (bf16[1024,1152]{1,0:T(8,128)(2,1)S(1)}, bf16[192,1152]{1,0:T(8,128)(2,1)S(1)}) custom-call(s32[8]{0:T(128)S(1)} %stack.35.place, f32[1]{0:T(128)S(6)} %exp.3.scale, f32[1]{0:T(128)S(6)} %copy.15.bias, bf16[1024,1152]{1,0:T(8,128)(2,1)S(1)} %get-tuple-element.95.z, bf16[512,1152]{1,0:T(8,128)(2,1)S(1)} %collective-permute-done.4.block, ...), custom_call_target="tpu_custom_call" | custom-call | tf_op jit(solution)/shard_map/last_phase/pallas_call | solution.py:264
  100.1 2.3 %sent_parts.1 = (bf16[192,1152]{1,0:T(8,128)(2,1)S(1)}, bf16[192,1152]{1,0:T(8,128)(2,1)S(1)}, bf16[192,1152]{1,0:T(8,128)(2,1)S(1)}) custom-call(s32[8]{0:T(128)S(1)} %stack.35.place, bf16[1152,1024]{1,0:T(8,128)(2,1)S(1)} %get-tuple-element.87.emb_t, bf16[1024,1152]{1,0:T(8,128)(2,1)S(1)} %get-tuple-element.110.du), custom_call_target="tpu_custom_call" | custom-call | tf_op jit(solution)/shard_map/sent_parts/pallas_call | solution.py:308
  102.4 1.2 collective-permute-start.10
  103.6 1.6 collective-permute-start.8
  105.9 1.7 kept_parts.1
  107.7 4.6 %collective-permute-done.11.got = bf16[192,1152]{1,0:T(8,128)(2,1)S(1)} collective-permute-done((bf16[192,1152]{1,0:T(8,128)(2,1)S(1)}, bf16[192,1152]{1,0:T(8,128)(2,1)S(1)}, u32[]{:S(2)}, u32[]{:S(2)}) %collective-permute-start.11) | collective-permute-done | bytes 442400 | tf_op jit(solution)/shard_map/ppermute | solution.py:41
  113.1 4.6 %rows_back.1 = (bf16[512,1152]{1,0:T(8,128)(2,1)S(1)}, bf16[512,1152]{1,0:T(8,128)(2,1)S(1)}) custom-call(s32[8]{0:T(128)S(1)} %stack.35.place, bf16[1024,1152]{1,0:T(8,128)(2,1)S(1)} %get-tuple-element.110.du, bf16[1152,1152]{1,0:T(8,128)(2,1)S(1)} %get-tuple-element.111.weight), custom_call_target="tpu_custom_call" | custom-call | tf_op jit(solution)/shard_map/rows_back/pallas_call | solution.py:334
  117.6 7.0 %collective-permute-done.8.refs_1_ = bf16[192,1152]{1,0:T(8,128)(2,1)S(1)} collective-permute-done((bf16[192,1152]{1,0:T(8,128)(2,1)S(1)}, bf16[192,1152]{1,0:T(8,128)(2,1)S(1)}, u32[]{:S(2)}, u32[]{:S(2)}) %collective-permute-start.8) | collective-permute-done | bytes 442400 | tf_op jit(solution)/shard_map/ppermute | solution.py:41
  125.3 1.0 middle_one.1
  126.3 1.5 collective-permute-start.13
  127.8 1.0 collective-permute-start.14
  128.8 1.0 collective-permute-start.15
  129.8 2.9 %collective-permute-done.13.refs_3_ = bf16[48,1152]{1,0:T(8,128)(2,1)S(1)} collective-permute-done((bf16[48,1152]{1,0:T(8,128)(2,1)S(1)}, bf16[48,1152]{1,0:T(8,128)(2,1)S(1)}, u32[]{:S(2)}, u32[]{:S(2)}) %collective-permute-start.13) | collective-permute-done | bytes 110624 | tf_op jit(solution)/shard_map/ppermute | solution.py:41
  132.7 3.6 %collective-permute-done.14.refs_1_ = bf16[48,1152]{1,0:T(8,128)(2,1)S(1)} collective-permute-done((bf16[48,1152]{1,0:T(8,128)(2,1)S(1)}, bf16[48,1152]{1,0:T(8,128)(2,1)S(1)}, u32[]{:S(2)}, u32[]{:S(2)}) %collective-permute-start.14) | collective-permute-done | bytes 110624 | tf_op jit(solution)/shard_map/ppermute | solution.py:41
  137.4 1.6 collective-permute-start.17
  139.0 1.5 collective-permute-start.18
  140.5 2.0 %rows_pick.1 = (bf16[512,1152]{1,0:T(8,128)(2,1)}, bf16[512,1152]{1,0:T(8,128)(2,1)}) custom-call(s32[8]{0:T(128)S(1)} %stack.35.place, bf16[512,1152]{1,0:T(8,128)(2,1)S(1)} %get-tuple-element.131.refs_0_.refs_3_, bf16[512,1152]{1,0:T(8,128)(2,1)S(1)} %collective-permute-done.19.refs_1_.refs_2_, ...), custom_call_target="tpu_custom_call" | custom-call | tf_op jit(solution)/shard_map/rows_pick/pallas_call | solution.py:159
  142.4 1.2 collective-permute-done.16.refs_1_
  145.3 2.0 %collective-permute-start.21 = (bf16[48,1152]{1,0:T(8,128)(2,1)S(1)}, bf16[48,1152]{1,0:T(8,128)(2,1)S(1)}, u32[]{:S(2)}, u32[]{:S(2)}) collective-permute-start(bf16[48,1152]{1,0:T(8,128)(2,1)S(1)} %get-tuple-element.141.refs_2_), channel_id=1, source_target_pairs={{0,8},{1,9},{2,10},{3,11},{4,12},{5,13},{6,14},{7,15},{8,0},{9,1},... | collective-permute-start | bytes 331784 | tf_op jit(solution)/shard_map/ppermute | solution.py:41
  147.4 0.7 collective-permute-start.22
  148.1 3.4 %collective-permute-done.20.refs_1_ = bf16[48,1152]{1,0:T(8,128)(2,1)S(1)} collective-permute-done((bf16[48,1152]{1,0:T(8,128)(2,1)S(1)}, bf16[48,1152]{1,0:T(8,128)(2,1)S(1)}, u32[]{:S(2)}, u32[]{:S(2)}) %collective-permute-start.20) | collective-permute-done | bytes 110624 | tf_op jit(solution)/shard_map/ppermute | solution.py:41
  154.2 1.6 collective-permute-start.24
  155.8 1.2 collective-permute-start.25
  157.0 5.8 %collective-permute-done.26.got = bf16[96,1152]{1,0:T(8,128)(2,1)S(1)} collective-permute-done((bf16[96,1152]{1,0:T(8,128)(2,1)S(1)}, bf16[96,1152]{1,0:T(8,128)(2,1)S(1)}, u32[]{:S(2)}, u32[]{:S(2)}) %collective-permute-start.26) | collective-permute-done | bytes 221216 | tf_op jit(solution)/shard_map/ppermute | solution.py:41
  163.5 3.1 %collective-permute-done.23.refs_1_ = bf16[192,1152]{1,0:T(8,128)(2,1)S(1)} collective-permute-done((bf16[192,1152]{1,0:T(8,128)(2,1)S(1)}, bf16[192,1152]{1,0:T(8,128)(2,1)S(1)}, u32[]{:S(2)}, u32[]{:S(2)}) %collective-permute-start.23) | collective-permute-done | bytes 442400 | tf_op jit(solution)/shard_map/ppermute | solution.py:41
  166.6 6.8 %collective-permute-done.24.refs_2_ = bf16[192,1152]{1,0:T(8,128)(2,1)S(1)} collective-permute-done((bf16[192,1152]{1,0:T(8,128)(2,1)S(1)}, bf16[192,1152]{1,0:T(8,128)(2,1)S(1)}, u32[]{:S(2)}, u32[]{:S(2)}) %collective-permute-start.24) | collective-permute-done | bytes 442400 | tf_op jit(solution)/shard_map/ppermute | solution.py:41
  173.4 1.0 collective-permute-done.27.refs_5_
  174.5 0.7 join_all.1.weight
  175.3 3.0 %widen_own.1 = (f32[1152,1152]{1,0:T(8,128)}, f32[1152,1152]{1,0:T(8,128)}) custom-call(s32[8]{0:T(128)S(1)} %stack.35.place, bf16[1152,1152]{1,0:T(8,128)(2,1)S(1)} %join_all.1.weight), custom_call_target="tpu_custom_call" | custom-call | tf_op jit(solution)/shard_map/widen_own/pallas_call | solution.py:487
  178.3 1.9 %collective-permute-done.28.weight = bf16[1152,1152]{1,0:T(8,128)(2,1)S(1)} collective-permute-done((bf16[1152,1152]{1,0:T(8,128)(2,1)S(1)}, bf16[1152,1152]{1,0:T(8,128)(2,1)S(1)}, u32[]{:S(2)}, u32[]{:S(2)}) %collective-permute-start.28) | collective-permute-done | bytes 2654240 | tf_op jit(solution)/shard_map/ppermute | solution.py:41
  180.2 3.0 %widen_other.1 = (f32[1152,1152]{1,0:T(8,128)}, f32[1152,1152]{1,0:T(8,128)}) custom-call(s32[8]{0:T(128)S(1)} %stack.35.place, bf16[1152,1152]{1,0:T(8,128)(2,1)S(1)} %collective-permute-done.28.weight, f32[1152,1152]{1,0:T(8,128)} %get-tuple-element.150.refs_0_, f32[1152,1152]{1,0:T(8,128)} %get-tuple-element.151.refs_1_), custom_call_target="tpu_custom_call", output_to_operand_aliasing={{0}: (2, {}), {1}: (3, {})} | custom-call | tf_op jit(solution)/shard_map/widen_other/pallas_call | solution.py:487
  (42 shorter events, 9.9 us)
Async XLA Ops:
  0.6 11.7 %collective-permute-start = (bf16[512,1152]{1,0:T(8,128)(2,1)}, bf16[512,1152]{1,0:T(8,128)(2,1)}, u32[]{:S(2)}, u32[]{:S(2)}) collective-permute-start(bf16[512,1152]{1,0:T(8,128)(2,1)} %refs_1_), channel_id=1, source_target_pairs={{0,1},{1,0},{2,3},{3,2},{4,5},{5,4},{6,7},{7,6},{8,9},{9,8},{10,11... | collective-permute-start | bytes 3538952 | tf_op jit(solution)/shard_map/ppermute | solution.py:41
  1.1 11.2 %collective-permute-start.1 = (bf16[512,1152]{1,0:T(8,128)(2,1)}, bf16[512,1152]{1,0:T(8,128)(2,1)}, u32[]{:S(2)}, u32[]{:S(2)}) collective-permute-start(bf16[512,1152]{1,0:T(8,128)(2,1)} %refs_4_.3), channel_id=1, source_target_pairs={{0,1},{1,0},{2,3},{3,2},{4,5},{5,4},{6,7},{7,6},{8,9},{9,8},{10,11... | collective-permute-start | bytes 3538952 | tf_op jit(solution)/shard_map/ppermute | solution.py:41
  1.2 11.1 %copy-start = (bf16[1152,1152]{1,0:T(8,128)(2,1)S(1)}, bf16[1152,1152]{1,0:T(8,128)(2,1)}, u32[]{:S(2)}) copy-start(bf16[1152,1152]{1,0:T(8,128)(2,1)} %refs_5_.3) | copy-start | bytes 7962628
  4.6 24.7 %collective-permute-start.2 = (bf16[512,1152]{1,0:T(8,128)(2,1)}, bf16[512,1152]{1,0:T(8,128)(2,1)}, u32[]{:S(2)}, u32[]{:S(2)}) collective-permute-start(bf16[512,1152]{1,0:T(8,128)(2,1)} %get-tuple-element.155), channel_id=1, source_target_pairs={{0,28},{1,3},{2,1},{3,6},{4,0},{5,7},{6,5},{7,10},{8,4},{9,11},{10... | collective-permute-start | bytes 3538952 | tf_op jit(solution)/shard_map/ppermute | solution.py:525
  10.6 26.7 %collective-permute-start.3 = (bf16[512,1152]{1,0:T(8,128)(2,1)}, bf16[512,1152]{1,0:T(8,128)(2,1)}, u32[]{:S(2)}, u32[]{:S(2)}) collective-permute-start(bf16[512,1152]{1,0:T(8,128)(2,1)} %get-tuple-element.154), channel_id=1, source_target_pairs={{0,29},{1,2},{2,0},{3,7},{4,1},{5,6},{6,4},{7,11},{8,5},{9,10},{10... | collective-permute-start | bytes 3538952 | tf_op jit(solution)/shard_map/ppermute | solution.py:526
  12.3 1.8 copy-start.1
  14.1 1.3 copy-start.3
  15.4 1.3 copy-start.4
  16.6 6.3 %copy-start.2 = (bf16[1152,1152]{1,0:T(8,128)(2,1)S(1)}, bf16[1152,1152]{1,0:T(8,128)(2,1)}, u32[]{:S(2)}) copy-start(bf16[1152,1152]{1,0:T(8,128)(2,1)} %refs_4_.4) | copy-start | bytes 7962628
  37.3 28.9 %collective-permute-start.6 = (bf16[512,1152]{1,0:T(8,128)(2,1)S(1)}, bf16[512,1152]{1,0:T(8,128)(2,1)S(1)}, u32[]{:S(2)}, u32[]{:S(2)}) collective-permute-start(bf16[512,1152]{1,0:T(8,128)(2,1)S(1)} %get-tuple-element.96.met), channel_id=1, source_target_pairs={{0,2},{1,3},{2,0},{3,1},{4,6},{5,7},{6,4},{7,5},{8,10},{9,11},{10,... | collective-permute-start | bytes 3538952 | tf_op jit(solution)/shard_map/ppermute | solution.py:41
  37.3 31.4 %collective-permute-start.7 = (bf16[512,1152]{1,0:T(8,128)(2,1)S(1)}, bf16[512,1152]{1,0:T(8,128)(2,1)S(1)}, u32[]{:S(2)}, u32[]{:S(2)}) collective-permute-start(bf16[512,1152]{1,0:T(8,128)(2,1)S(1)} %get-tuple-element.97.met_other), channel_id=1, source_target_pairs={{0,4},{1,5},{2,30},{3,31},{4,8},{5,9},{6,2},{7,3},{8,12},{9,13},{1... | collective-permute-start | bytes 3538952 | tf_op jit(solution)/shard_map/ppermute | solution.py:37
  43.5 46.6 %collective-permute-start.5 = (bf16[512,1152]{1,0:T(8,128)(2,1)S(1)}, bf16[512,1152]{1,0:T(8,128)(2,1)S(1)}, u32[]{:S(2)}, u32[]{:S(2)}) collective-permute-start(bf16[512,1152]{1,0:T(8,128)(2,1)S(1)} %get-tuple-element.94.far_other), channel_id=1, source_target_pairs={{0,2},{1,3},{2,0},{3,1},{4,6},{5,7},{6,4},{7,5},{8,10},{9,11},{10,... | collective-permute-start | bytes 3538952 | tf_op jit(solution)/shard_map/ppermute | solution.py:41
  47.7 46.3 %collective-permute-start.4 = (bf16[512,1152]{1,0:T(8,128)(2,1)S(1)}, bf16[512,1152]{1,0:T(8,128)(2,1)S(1)}, u32[]{:S(2)}, u32[]{:S(2)}) collective-permute-start(bf16[512,1152]{1,0:T(8,128)(2,1)S(1)} %get-tuple-element.93.two), channel_id=1, source_target_pairs={{0,4},{1,5},{2,30},{3,31},{4,8},{5,9},{6,2},{7,3},{8,12},{9,13},{1... | collective-permute-start | bytes 3538952 | tf_op jit(solution)/shard_map/ppermute | solution.py:37
  100.0 12.3 %collective-permute-start.11 = (bf16[192,1152]{1,0:T(8,128)(2,1)S(1)}, bf16[192,1152]{1,0:T(8,128)(2,1)S(1)}, u32[]{:S(2)}, u32[]{:S(2)}) collective-permute-start(bf16[192,1152]{1,0:T(8,128)(2,1)S(1)} %get-tuple-element.108), channel_id=1, source_target_pairs={{0,8},{1,9},{2,10},{3,11},{4,12},{5,13},{6,14},{7,15},{8,0},{9,1},... | collective-permute-start | bytes 1327112 | tf_op jit(solution)/shard_map/ppermute | solution.py:41
  102.4 15.3 %collective-permute-start.10 = (bf16[192,1152]{1,0:T(8,128)(2,1)S(1)}, bf16[192,1152]{1,0:T(8,128)(2,1)S(1)}, u32[]{:S(2)}, u32[]{:S(2)}) collective-permute-start(bf16[192,1152]{1,0:T(8,128)(2,1)S(1)} %get-tuple-element.106), channel_id=1, source_target_pairs={{0,6},{1,7},{2,4},{3,5},{4,2},{5,3},{6,0},{7,1},{8,14},{9,15},{10,... | collective-permute-start | bytes 1327112 | tf_op jit(solution)/shard_map/ppermute | solution.py:41
  103.6 21.1 %collective-permute-start.8 = (bf16[192,1152]{1,0:T(8,128)(2,1)S(1)}, bf16[192,1152]{1,0:T(8,128)(2,1)S(1)}, u32[]{:S(2)}, u32[]{:S(2)}) collective-permute-start(bf16[192,1152]{1,0:T(8,128)(2,1)S(1)} %get-tuple-element.104), channel_id=1, source_target_pairs={{0,2},{1,3},{2,0},{3,1},{4,6},{5,7},{6,4},{7,5},{8,10},{9,11},{10,... | collective-permute-start | bytes 1327112 | tf_op jit(solution)/shard_map/ppermute | solution.py:41
  105.2 19.8 %collective-permute-start.9 = (bf16[192,1152]{1,0:T(8,128)(2,1)S(1)}, bf16[192,1152]{1,0:T(8,128)(2,1)S(1)}, u32[]{:S(2)}, u32[]{:S(2)}) collective-permute-start(bf16[192,1152]{1,0:T(8,128)(2,1)S(1)} %get-tuple-element.105), channel_id=1, source_target_pairs={{0,4},{1,5},{2,6},{3,7},{4,0},{5,1},{6,2},{7,3},{8,12},{9,13},{10,... | collective-permute-start | bytes 1327112 | tf_op jit(solution)/shard_map/ppermute | solution.py:41
  113.0 12.3 %collective-permute-start.12 = (bf16[96,1152]{1,0:T(8,128)(2,1)S(1)}, bf16[96,1152]{1,0:T(8,128)(2,1)S(1)}, u32[]{:S(2)}, u32[]{:S(2)}) collective-permute-start(bf16[96,1152]{1,0:T(8,128)(2,1)S(1)} %get-tuple-element.109), channel_id=1, source_target_pairs={{0,16},{1,17},{2,18},{3,19},{4,20},{5,21},{6,22},{7,23},{8,24},{9,... | collective-permute-start | bytes 663560 | tf_op jit(solution)/shard_map/ppermute | solution.py:41
  125.3 15.2 %collective-permute-start.19 = (bf16[512,1152]{1,0:T(8,128)(2,1)S(1)}, bf16[512,1152]{1,0:T(8,128)(2,1)S(1)}, u32[]{:S(2)}, u32[]{:S(2)}) collective-permute-start(bf16[512,1152]{1,0:T(8,128)(2,1)S(1)} %get-tuple-element.132), channel_id=1, source_target_pairs={{0,1},{1,0},{2,3},{3,2},{4,5},{5,4},{6,7},{7,6},{8,9},{9,8},{10,11... | collective-permute-start | bytes 3538952 | tf_op jit(solution)/shard_map/ppermute | solution.py:41
  126.3 6.4 %collective-permute-start.13 = (bf16[48,1152]{1,0:T(8,128)(2,1)S(1)}, bf16[48,1152]{1,0:T(8,128)(2,1)S(1)}, u32[]{:S(2)}, u32[]{:S(2)}) collective-permute-start(bf16[48,1152]{1,0:T(8,128)(2,1)S(1)} %get-tuple-element.120), channel_id=1, source_target_pairs={{0,8},{1,9},{2,10},{3,11},{4,12},{5,13},{6,14},{7,15},{8,0},{9,1},... | collective-permute-start | bytes 331784 | tf_op jit(solution)/shard_map/ppermute | solution.py:41
  127.8 8.4 %collective-permute-start.14 = (bf16[48,1152]{1,0:T(8,128)(2,1)S(1)}, bf16[48,1152]{1,0:T(8,128)(2,1)S(1)}, u32[]{:S(2)}, u32[]{:S(2)}) collective-permute-start(bf16[48,1152]{1,0:T(8,128)(2,1)S(1)} %get-tuple-element.121), channel_id=1, source_target_pairs={{0,16},{1,17},{2,18},{3,19},{4,20},{5,21},{6,22},{7,23},{8,24},{9,... | collective-permute-start | bytes 331784 | tf_op jit(solution)/shard_map/ppermute | solution.py:41
  128.8 7.5 %collective-permute-start.15 = (bf16[48,1152]{1,0:T(8,128)(2,1)S(1)}, bf16[48,1152]{1,0:T(8,128)(2,1)S(1)}, u32[]{:S(2)}, u32[]{:S(2)}) collective-permute-start(bf16[48,1152]{1,0:T(8,128)(2,1)S(1)} %get-tuple-element.122), channel_id=1, source_target_pairs={{0,2},{1,3},{2,0},{3,1},{4,6},{5,7},{6,4},{7,5},{8,10},{9,11},{10,... | collective-permute-start | bytes 331784 | tf_op jit(solution)/shard_map/ppermute | solution.py:41
  136.9 6.7 %collective-permute-start.16 = (bf16[48,1152]{1,0:T(8,128)(2,1)S(1)}, bf16[48,1152]{1,0:T(8,128)(2,1)S(1)}, u32[]{:S(2)}, u32[]{:S(2)}) collective-permute-start(bf16[48,1152]{1,0:T(8,128)(2,1)S(1)} %get-tuple-element.128.refs_0_), channel_id=1, source_target_pairs={{0,16},{1,17},{2,18},{3,19},{4,20},{5,21},{6,22},{7,23},{8,24},{9,... | collective-permute-start | bytes 331784 | tf_op jit(solution)/shard_map/ppermute | solution.py:41
  137.4 6.7 %collective-permute-start.17 = (bf16[48,1152]{1,0:T(8,128)(2,1)S(1)}, bf16[48,1152]{1,0:T(8,128)(2,1)S(1)}, u32[]{:S(2)}, u32[]{:S(2)}) collective-permute-start(bf16[48,1152]{1,0:T(8,128)(2,1)S(1)} %get-tuple-element.129.refs_2_), channel_id=1, source_target_pairs={{0,8},{1,9},{2,10},{3,11},{4,12},{5,13},{6,14},{7,15},{8,0},{9,1},... | collective-permute-start | bytes 331784 | tf_op jit(solution)/shard_map/ppermute | solution.py:41
  139.0 5.1 %collective-permute-start.18 = (bf16[48,1152]{1,0:T(8,128)(2,1)S(1)}, bf16[48,1152]{1,0:T(8,128)(2,1)S(1)}, u32[]{:S(2)}, u32[]{:S(2)}) collective-permute-start(bf16[48,1152]{1,0:T(8,128)(2,1)S(1)} %get-tuple-element.130.refs_4_), channel_id=1, source_target_pairs={{0,4},{1,5},{2,6},{3,7},{4,0},{5,1},{6,2},{7,3},{8,12},{9,13},{10,... | collective-permute-start | bytes 331784 | tf_op jit(solution)/shard_map/ppermute | solution.py:41
  144.7 6.7 %collective-permute-start.20 = (bf16[48,1152]{1,0:T(8,128)(2,1)S(1)}, bf16[48,1152]{1,0:T(8,128)(2,1)S(1)}, u32[]{:S(2)}, u32[]{:S(2)}) collective-permute-start(bf16[48,1152]{1,0:T(8,128)(2,1)S(1)} %get-tuple-element.140.refs_0_), channel_id=1, source_target_pairs={{0,16},{1,17},{2,18},{3,19},{4,20},{5,21},{6,22},{7,23},{8,24},{9,... | collective-permute-start | bytes 331784 | tf_op jit(solution)/shard_map/ppermute | solution.py:41
  145.3 6.1 %collective-permute-start.21 = (bf16[48,1152]{1,0:T(8,128)(2,1)S(1)}, bf16[48,1152]{1,0:T(8,128)(2,1)S(1)}, u32[]{:S(2)}, u32[]{:S(2)}) collective-permute-start(bf16[48,1152]{1,0:T(8,128)(2,1)S(1)} %get-tuple-element.141.refs_2_), channel_id=1, source_target_pairs={{0,8},{1,9},{2,10},{3,11},{4,12},{5,13},{6,14},{7,15},{8,0},{9,1},... | collective-permute-start | bytes 331784 | tf_op jit(solution)/shard_map/ppermute | solution.py:41
  147.4 4.7 %collective-permute-start.22 = (bf16[48,1152]{1,0:T(8,128)(2,1)S(1)}, bf16[48,1152]{1,0:T(8,128)(2,1)S(1)}, u32[]{:S(2)}, u32[]{:S(2)}) collective-permute-start(bf16[48,1152]{1,0:T(8,128)(2,1)S(1)} %get-tuple-element.142.refs_4_), channel_id=1, source_target_pairs={{0,2},{1,3},{2,0},{3,1},{4,6},{5,7},{6,4},{7,5},{8,10},{9,11},{10,... | collective-permute-start | bytes 331784 | tf_op jit(solution)/shard_map/ppermute | solution.py:41
  152.8 10.0 %collective-permute-start.26 = (bf16[96,1152]{1,0:T(8,128)(2,1)S(1)}, bf16[96,1152]{1,0:T(8,128)(2,1)S(1)}, u32[]{:S(2)}, u32[]{:S(2)}) collective-permute-start(bf16[96,1152]{1,0:T(8,128)(2,1)S(1)} %get-tuple-element.144.mine), channel_id=1, source_target_pairs={{0,16},{1,17},{2,18},{3,19},{4,20},{5,21},{6,22},{7,23},{8,24},{9,... | collective-permute-start | bytes 663560 | tf_op jit(solution)/shard_map/ppermute | solution.py:41
  153.5 13.1 %collective-permute-start.23 = (bf16[192,1152]{1,0:T(8,128)(2,1)S(1)}, bf16[192,1152]{1,0:T(8,128)(2,1)S(1)}, u32[]{:S(2)}, u32[]{:S(2)}) collective-permute-start(bf16[192,1152]{1,0:T(8,128)(2,1)S(1)} %get-tuple-element.145.refs_0_), channel_id=1, source_target_pairs={{0,2},{1,3},{2,0},{3,1},{4,6},{5,7},{6,4},{7,5},{8,10},{9,11},{10,... | collective-permute-start | bytes 1327112 | tf_op jit(solution)/shard_map/ppermute | solution.py:41
  154.2 19.2 %collective-permute-start.24 = (bf16[192,1152]{1,0:T(8,128)(2,1)S(1)}, bf16[192,1152]{1,0:T(8,128)(2,1)S(1)}, u32[]{:S(2)}, u32[]{:S(2)}) collective-permute-start(bf16[192,1152]{1,0:T(8,128)(2,1)S(1)} %get-tuple-element.145.refs_0_), channel_id=1, source_target_pairs={{0,4},{1,5},{2,6},{3,7},{4,0},{5,1},{6,2},{7,3},{8,12},{9,13},{10,... | collective-permute-start | bytes 1327112 | tf_op jit(solution)/shard_map/ppermute | solution.py:41
  155.8 17.6 %collective-permute-start.25 = (bf16[192,1152]{1,0:T(8,128)(2,1)S(1)}, bf16[192,1152]{1,0:T(8,128)(2,1)S(1)}, u32[]{:S(2)}, u32[]{:S(2)}) collective-permute-start(bf16[192,1152]{1,0:T(8,128)(2,1)S(1)} %get-tuple-element.145.refs_0_), channel_id=1, source_target_pairs={{0,6},{1,7},{2,4},{3,5},{4,2},{5,3},{6,0},{7,1},{8,14},{9,15},{10,... | collective-permute-start | bytes 1327112 | tf_op jit(solution)/shard_map/ppermute | solution.py:41
  163.5 11.0 %collective-permute-start.27 = (bf16[192,1152]{1,0:T(8,128)(2,1)S(1)}, bf16[192,1152]{1,0:T(8,128)(2,1)S(1)}, u32[]{:S(2)}, u32[]{:S(2)}) collective-permute-start(bf16[192,1152]{1,0:T(8,128)(2,1)S(1)} %b_join_high.1.refs_4_), channel_id=1, source_target_pairs={{0,8},{1,9},{2,10},{3,11},{4,12},{5,13},{6,14},{7,15},{8,0},{9,1},... | collective-permute-start | bytes 1327112 | tf_op jit(solution)/shard_map/ppermute | solution.py:41
  175.2 5.0 %collective-permute-start.28 = (bf16[1152,1152]{1,0:T(8,128)(2,1)S(1)}, bf16[1152,1152]{1,0:T(8,128)(2,1)S(1)}, u32[]{:S(2)}, u32[]{:S(2)}) collective-permute-start(bf16[1152,1152]{1,0:T(8,128)(2,1)S(1)} %join_all.1.weight), channel_id=1, source_target_pairs={{0,1},{1,0},{2,3},{3,2},{4,5},{5,4},{6,7},{7,6},{8,9},{9,8},{10,11... | collective-permute-start | bytes 7962632 | tf_op jit(solution)/shard_map/ppermute | solution.py:41
